TPU v7x, 32 devices: a whole 2x2x4 slice. The times are simulated.
32 devices in a mesh: row: 4 (over z), head: 8 (over y, x, core).
Axes of the slice: x: 2, y: 2, z: 4, core: 2. Of those that a mesh axis runs over, the one named last changes fastest.
Arguments:
- hidden: bfloat16 [8, 8192], P(None, 'row'), may hold values from -12 to 12
- norm_gain: bfloat16 [8192], P('row'), may hold values from 0.5 to 1.5
- input_weight: bfloat16 [8192, 2, 16384], P('row', None, 'head'), may hold values from -0.0625 to 0.0625
- group_weight: bfloat16 [8192, 4096], P('row', 'head'), may hold values from -0.0625 to 0.0625
- step_weight: bfloat16 [8192, 256], P('row', 'head'), may hold values from -0.0625 to 0.0625
- conv_inner_weight: bfloat16 [4, 16384], P(None, 'head'), may hold values from -3 to 3
- conv_group_weight: bfloat16 [4, 4096], P(None, 'head'), may hold values from -3 to 3
- conv_inner_state: bfloat16 [8, 3, 16384], P('row', None, 'head'), may hold values from -6 to 6
- conv_group_state: bfloat16 [8, 3, 4096], P('row', None, 'head'), may hold values from -6 to 6
- timestep_bias: float32 [256], P('head'), may hold values from -3 to 0.5
- decay_log: float32 [256], P('head'), may hold values from -1 to 2
- skip_gain: float32 [256], P('head'), may hold values from 0.5 to 1.5
- recurrent_state: bfloat16 [8, 256, 64, 256], P('row', 'head'), may hold values from -6 to 6
- mixer_gain: bfloat16 [16384], P('head'), may hold values from 0.5 to 1.5
- output_weight: bfloat16 [16384, 8192], P('head', 'row'), may hold values from -0.046875 to 0.046875
- final_gain: bfloat16 [8192], P('row'), may hold values from 0.5 to 1.5
- lexicon_matrix: bfloat16 [8192, 65536], P('row', 'head'), may hold values from -0.4375 to 0.4375
- token_mask: int32 [8, 65536], P('row', 'head'), may hold values 0 or 1
- min_share: int32 [8], P('row'), may hold values from 1311 to 13107
Outputs:
- next_state: bfloat16 [8, 256, 64, 256], P('row', 'head')
- next_conv_inner: bfloat16 [8, 3, 16384], P('row', None, 'head')
- next_conv_group: bfloat16 [8, 3, 4096], P('row', None, 'head')
- layer_out: bfloat16 [8, 8192], P(None, 'row')
- next_probs: bfloat16 [8, 65536], P('row', 'head')
Inputs may be any that keep to these rules, and one draw needn't show every extreme that they name: `min_share`: the smallest share of the row's top probability that a token keeps in full at twice that share, times 65536.
All inputs are finite; a program needn't handle non-finite values. No bound on the sum of `token_mask` on one device may be relied on, other than what follows from the above.
Results may differ from a plain program's by a relative error of at most 0.04.
Values may be sent and summed in bfloat16 or wider, within the bound.
No kernel may reach another device: no remote copies, remote signals or barrier semaphores. Data moves between devices by JAX's collectives and lax.ppermute only.
A program may use at most 128 MiB of HBM per device.

v0:
```python
import jax
import jax.numpy as jnp
from jax import lax
from jax.sharding import PartitionSpec as P

D = 8192
HEADS = 256
HEAD_DIM = 64
GROUPS = 8


EPSILON = 1e-05
INVERSE_HEAT = 1.25
FIXED_POINT = 65536.0
NEG_LARGE = -1e30


def conv_step(history, newest, filter_coefficient):
    window = jnp.concatenate([history, newest[:, None, :]], axis=1)
    mixed_taps = jnp.sum(
        window.astype(jnp.float32) * filter_coefficient.astype(jnp.float32)[None, :, :], axis=1
    )
    return (window[:, 1:, :], jax.nn.silu(mixed_taps))


def local(
    hidden,
    norm_gain,
    input_weight,
    group_weight,
    step_weight,
    conv_inner_weight,
    conv_group_weight,
    conv_inner_state,
    conv_group_state,
    timestep_bias,
    decay_log,
    skip_gain,
    recurrent_state,
    mixer_gain,
    output_weight,
    final_gain,
    lexicon_matrix,
    token_mask,
    min_share,
):
    rows_mine, heads_mine, head_width, state_width = recurrent_state.shape
    inner_mine = heads_mine * head_width
    head_devices = lax.axis_size("head")
    group_devices = head_devices // GROUPS
    head_index = lax.axis_index("head")
    hidden_wide = hidden.astype(jnp.float32)
    quadratic_accumulated = lax.psum(jnp.sum(hidden_wide * hidden_wide, axis=1), "row")
    hidden_scale = lax.rsqrt(quadratic_accumulated / D + EPSILON)
    normed = (hidden_wide * hidden_scale[:, None] * norm_gain.astype(jnp.float32)[None, :]).astype(
        jnp.bfloat16
    )
    flat_input = input_weight.reshape(input_weight.shape[0], 2 * inner_mine)
    pair_mine = group_weight.shape[1]
    row_block = normed
    projected = lax.psum_scatter(
        jnp.concatenate(
            [
                jnp.dot(row_block, flat_input, preferred_element_type=jnp.float32),
                jnp.dot(row_block, group_weight, preferred_element_type=jnp.float32),
                jnp.dot(row_block, step_weight, preferred_element_type=jnp.float32),
            ],
            axis=1,
        ),
        "row",
        scatter_dimension=0,
        tiled=True,
    )
    gate_raw = projected[:, :inner_mine]
    inner_raw = projected[:, inner_mine : 2 * inner_mine]
    group_raw = projected[:, 2 * inner_mine : 2 * inner_mine + pair_mine]
    step_raw = projected[:, 2 * inner_mine + pair_mine :]
    next_conv_inner, conv_inner = conv_step(
        conv_inner_state, inner_raw.astype(jnp.bfloat16), conv_inner_weight
    )
    next_conv_group, conv_group = conv_step(
        conv_group_state, group_raw.astype(jnp.bfloat16), conv_group_weight
    )
    group_round = conv_group.astype(jnp.bfloat16)
    every_group = lax.all_gather(group_round, "head", axis=1, tiled=True)
    group_index = head_index // group_devices
    group_layout = every_group.reshape(rows_mine, 2 * state_width, GROUPS)
    group_pair = lax.dynamic_slice_in_dim(group_layout, group_index, 1, 2)[:, :, 0]
    pair_wide = group_pair.astype(jnp.float32)
    state_input = pair_wide[:, :state_width]
    state_readout = pair_wide[:, state_width:]
    step_size = jax.nn.softplus(step_raw + timestep_bias[None, :])
    decay_rate = jnp.exp(-step_size * jnp.exp(decay_log)[None, :])
    inner_heads = conv_inner.reshape(rows_mine, heads_mine, head_width)
    state_new = (
        decay_rate[:, :, None, None] * recurrent_state.astype(jnp.float32)
        + (step_size[:, :, None] * inner_heads)[:, :, :, None] * state_input[:, None, None, :]
    )
    readout = jnp.sum(state_new * state_readout[:, None, None, :], axis=3)
    readout = readout + skip_gain[None, :, None] * inner_heads
    gated_out = readout.reshape(rows_mine, inner_mine) * jax.nn.silu(gate_raw)
    local_squares = jnp.sum(gated_out * gated_out, axis=1)
    selector = (jnp.arange(GROUPS) == group_index).astype(jnp.float32)
    group_table = lax.psum(local_squares[:, None] * selector[None, :], "head")
    group_total = jnp.sum(group_table * selector[None, :], axis=1)
    group_scale = lax.rsqrt(group_total / (HEADS * HEAD_DIM // GROUPS) + EPSILON)
    mixer_in = (gated_out * group_scale[:, None] * mixer_gain.astype(jnp.float32)[None, :]).astype(
        jnp.bfloat16
    )
    mixer_part = jnp.dot(
        lax.all_gather(mixer_in, "row", axis=0, tiled=True),
        output_weight,
        preferred_element_type=jnp.float32,
    )
    final_scale = final_gain.astype(jnp.float32)[None, :]
    mixed_complete = lax.psum(mixer_part, "head")
    layer_out = (hidden_wide + mixed_complete).astype(jnp.bfloat16)
    out_wide = layer_out.astype(jnp.float32)
    out_squares = lax.psum(jnp.sum(out_wide * out_wide, axis=1), "row")
    last_rescaled_vector = (
        out_wide * lax.rsqrt(out_squares / D + EPSILON)[:, None] * final_scale
    ).astype(jnp.bfloat16)
    row_block = last_rescaled_vector
    candidate_scores = (
        lax.psum_scatter(
            jnp.dot(row_block, lexicon_matrix, preferred_element_type=jnp.float32),
            "row",
            scatter_dimension=0,
            tiled=True,
        )
        * INVERSE_HEAT
    )
    allowed = token_mask > 0
    peak_logit = lax.pmax(jnp.max(jnp.where(allowed, candidate_scores, NEG_LARGE), axis=1), "head")
    ratio_to_peak = jnp.where(allowed, jnp.exp(candidate_scores - peak_logit[:, None]), 0.0)
    floor_share = min_share.astype(jnp.float32)[:, None] / FIXED_POINT
    weights = ratio_to_peak * jnp.clip(ratio_to_peak / floor_share - 1.0, 0.0, 1.0)
    kept_total = lax.psum(jnp.sum(weights, axis=1), "head")
    next_probs = (weights / kept_total[:, None]).astype(jnp.bfloat16)
    return (state_new.astype(jnp.bfloat16), next_conv_inner, next_conv_group, layer_out, next_probs)


def solution(mesh):
    in_specs = (
        P(None, "row"),
        P("row"),
        P("row", None, "head"),
        P("row", "head"),
        P("row", "head"),
        P(None, "head"),
        P(None, "head"),
        P("row", None, "head"),
        P("row", None, "head"),
        P("head"),
        P("head"),
        P("head"),
        P("row", "head", None, None),
        P("head"),
        P("head", "row"),
        P("row"),
        P("row", "head"),
        P("row", "head"),
        P("row"),
    )
    out_specs = (
        P("row", "head", None, None),
        P("row", None, "head"),
        P("row", None, "head"),
        P(None, "row"),
        P("row", "head"),
    )
    return jax.shard_map(local, mesh=mesh, in_specs=in_specs, out_specs=out_specs, check_vma=False)
```

profile of v0, /device:TPU:0, one launch (start us, length us, event | category | flops | bytes accessed | tf_op | source)
XLA Modules:
  0.0 263.9 jit_solution(4994922377044472257)
XLA Ops:
  7.2 0.0 copy-start
  7.2 0.0 all-reduce.8.cloned.1.call-start
  7.2 1.0 fusion.4
  8.3 0.7 convert_element_type.70
  8.9 13.4 %psum.35 = f32[8]{0:T(128)S(1)} all-reduce(f32[8]{0:T(128)S(1)} %fusion.4), channel_id=1, replica_groups=mesh['row'=4,'head'=8] {'row'}, use_global_device_ids=true, to_apply=%region_1.0 | all-reduce | flops 8 | bytes 64 | tf_op jit(solution)/shard_map/psum | solution.py:53
  22.4 12.2 %copy.24 = bf16[256,8,2,2048]{3,1,2,0:T(8,128)(2,1)S(1)} copy(bf16[256,8,2,2048]{3,2,1,0:T(2,128)(2,1)} %bitcast.16) | data formatting | bytes 33554432
  34.7 2.3 fusion.21
  37.0 0.4 fusion.19
  37.5 0.2 fusion.17
  37.7 0.7 pad_maximum_fusion
  38.3 0.0 all-reduce.8.cloned.1.call-update
  38.4 0.0 all-reduce.6.cloned.1.call-start
  38.5 0.1 mul.207
  38.6 0.1 mul.208
  38.7 0.6 dynamic-slice
  39.9 31.2 %all-reduce.8.cloned.1.call-done = f32[8,4640]{1,0:T(8,128)} async-done(((f32[8,4640]{1,0:T(8,128)}), f32[8,4640]{1,0:T(8,128)}) %all-reduce.8.cloned.1.call-update) | async-done | bytes 148496
  71.1 0.9 dynamic-slice_convert_fusion
  72.1 0.1 multiply_reduce_fusion.1
  72.1 0.1 reduce_sum.78
  72.3 8.9 %all_gather.6 = bf16[2,4096]{1,0:T(2,128)(2,1)S(1)} all-gather(bf16[2,512]{1,0:T(2,128)(2,1)S(1)} %fusion.16), channel_id=1, replica_groups=mesh['row'=4,'head'=8] {'head'}, dimensions={1}, use_global_device_ids=true | all-gather | bytes 18432 | tf_op jit(solution)/shard_map/all_gather | solution.py:85
  81.1 0.3 reshape.66
  81.5 0.3 convert_reduce_fusion
  81.8 0.8 multiply_exponential_fusion
  82.6 0.1 multiply_multiply_fusion
  82.6 3.9 %multiply_reduce_fusion = (f32[2,32,64]{2,1,0:T(8,128)S(1)}, bf16[2,32,64,256]{3,2,1,0:T(8,128)(2,1)}) fusion(bf16[2,32,64,256]{3,2,1,0:T(8,128)(2,1)} %param.31, f32[2,256]{1,0:T(2,128)S(1)} %get-tuple-element.15, f32[2,256]{1,0:T(2,128)S(1)} %get-tuple-element.16, f32[2,32,64]{2,1,0:T(8,128)S(1)} %multiply_multiply_fusion, f32[2,32]{1,0:T(2,128)S(1)} %get-tuple-element.11), kind=kLoop, calls=%fused_computation | loop fusion | flops 7335936 | bytes 4231424 | tf_op jit(solution)/shard_map/reduce_sum | solution.py:99
  86.5 0.1 reduce_sum.81
  86.6 1.0 multiply_reduce_fusion.2
  87.6 0.1 broadcast_multiply_fusion
  87.7 13.2 %psum.36 = f32[2,8]{1,0:T(2,128)S(1)} all-reduce(f32[2,8]{1,0:T(2,128)S(1)} %broadcast_multiply_fusion), channel_id=1, replica_groups=mesh['row'=4,'head'=8] {'head'}, use_global_device_ids=true, to_apply=%region_7.8 | all-reduce | flops 16 | bytes 128 | tf_op jit(solution)/shard_map/psum | solution.py:104
  100.9 0.1 multiply_reduce_fusion.4
  101.0 0.1 fusion.14
  101.1 13.2 %all-gather = bf16[4,2,2048]{2,1,0:T(2,128)(2,1)S(1)} all-gather(bf16[1,2,2048]{2,1,0:T(2,128)(2,1)S(1)} %fusion.14), channel_id=1, replica_groups=mesh['row'=4,'head'=8] {'row'}, dimensions={0}, use_global_device_ids=true | all-gather | bytes 40960 | tf_op jit(solution)/shard_map/all_gather | solution.py:111
  114.3 5.2 %fusion.27 = f32[8,2048]{1,0:T(8,128)} fusion(bf16[8,2048]{1,0:T(8,128)(2,1)S(1)} %reshape.69, bf16[2048,2048]{1,0:T(8,128)(2,1)} %param.33), kind=kOutput, calls=%fused_computation.58 | convolution fusion | flops 67108864 | bytes 8486912 | tf_op jit(solution)/shard_map/dot_general | solution.py:110
  119.5 0.0 all-reduce.6.cloned.1.call-update
  119.5 0.0 all-reduce.10.cloned.1.call-start
  119.6 51.6 %all-reduce.6.cloned.1.call-done = f32[8,2048]{1,0:T(8,128)} async-done(((f32[8,2048]{1,0:T(8,128)}), f32[8,2048]{1,0:T(8,128)}) %all-reduce.6.cloned.1.call-update) | async-done | bytes 65552 | tf_op jit(solution)/shard_map/psum | solution.py:116
  171.2 1.0 fusion.1
  172.1 11.7 %psum.38 = f32[8]{0:T(128)S(1)} all-reduce(f32[8]{0:T(128)S(1)} %get-tuple-element.7), channel_id=1, replica_groups=mesh['row'=4,'head'=8] {'row'}, use_global_device_ids=true, to_apply=%region_11.12 | all-reduce | flops 8 | bytes 64 | tf_op jit(solution)/shard_map/psum | solution.py:119
  183.9 13.7 %fusion.8 = f32[8,8192]{1,0:T(8,128)} fusion(bf16[2048,8192]{1,0:T(8,128)(2,1)} %param.35, bf16[8,2048]{1,0:T(8,128)(2,1)S(1)} %get-tuple-element.8, f32[2048]{0:T(1024)S(1)} %convert_element_type.86, f32[8]{0:T(128)S(1)} %add_rsqrt_fusion), kind=kOutput, calls=%fused_computation.23 | convolution fusion | flops 268500992 | bytes 33857568 | tf_op jit(solution)/shard_map/dot_general | solution.py:126
  197.6 0.0 all-reduce.10.cloned.1.call-update
  197.6 0.6 fusion.12
  198.3 31.5 %all-reduce.10.cloned.1.call-done = f32[8,8192]{1,0:T(8,128)} async-done(((f32[8,8192]{1,0:T(8,128)}), f32[8,8192]{1,0:T(8,128)}) %all-reduce.10.cloned.1.call-update) | async-done | bytes 262160
  229.7 1.1 select_reduce_fusion
  230.9 0.6 fusion.15
  231.5 12.2 %pmax.7 = f32[2]{0:T(128)S(1)} all-reduce(f32[2]{0:T(128)S(1)} %select_reduce_fusion), channel_id=1, replica_groups=mesh['row'=4,'head'=8] {'head'}, use_global_device_ids=true, to_apply=%region_14.15 | all-reduce | flops 2 | bytes 16 | tf_op jit(solution)/shard_map/pmax | solution.py:134
  243.7 1.2 fusion.23
  244.9 11.8 %psum.39 = f32[2]{0:T(128)S(1)} all-reduce(f32[2]{0:T(128)S(1)} %get-tuple-element.5), channel_id=1, replica_groups=mesh['row'=4,'head'=8] {'head'}, use_global_device_ids=true, to_apply=%region_16.17 | all-reduce | flops 2 | bytes 16 | tf_op jit(solution)/shard_map/psum | solution.py:138
  256.7 0.7 divide_convert_fusion
  (49 shorter events, 0.2 us)
Async XLA Ops:
  7.2 29.9 %copy-start = (bf16[2048,512]{1,0:T(8,128)(2,1)S(1)}, bf16[2048,512]{1,0:T(8,128)(2,1)}, u32[]{:S(2)}) copy-start(bf16[2048,512]{1,0:T(8,128)(2,1)} %param.22) | copy-start | bytes 6291460
  7.2 63.9 %all-reduce.8.cloned.1.call-start = ((), (), s32[]{:S(2)}) async-start(), calls=%async_computation.1 | async-start | bytes 303104
  22.4 12.2 %copy-start.2 = (bf16[8,2048]{1,0:T(8,128)(2,1)S(1)}, bf16[8,2048]{1,0:T(8,128)(2,1)}, u32[]{:S(2)}) copy-start(bf16[8,2048]{1,0:T(8,128)(2,1)} %param.19) | copy-start | bytes 98308
  34.6 2.8 %copy-start.13 = (bf16[2048,32]{0,1:T(8,128)(2,1)S(1)}, bf16[2048,32]{0,1:T(8,128)(2,1)}, u32[]{:S(2)}) copy-start(bf16[2048,32]{0,1:T(8,128)(2,1)} %param.23) | copy-start | bytes 393220
  34.6 3.8 %copy-start.7 = (bf16[4,2048]{1,0:T(4,128)(2,1)S(1)}, bf16[4,2048]{1,0:T(4,128)(2,1)}, u32[]{:S(2)}) copy-start(bf16[4,2048]{1,0:T(4,128)(2,1)} %param.24) | copy-start | bytes 49156
  34.6 3.8 %copy-start.14 = (f32[32]{0:T(128)S(1)}, f32[32]{0:T(128)}, u32[]{:S(2)}) copy-start(f32[32]{0:T(128)} %param.29) | copy-start | bytes 388
  34.6 3.8 %copy-start.8 = (bf16[4,512]{1,0:T(4,128)(2,1)S(1)}, bf16[4,512]{1,0:T(4,128)(2,1)}, u32[]{:S(2)}) copy-start(bf16[4,512]{1,0:T(4,128)(2,1)} %param.25) | copy-start | bytes 12292
  34.7 3.8 %copy-start.11 = (f32[32]{0:T(128)S(1)}, f32[32]{0:T(128)}, u32[]{:S(2)}) copy-start(f32[32]{0:T(128)} %param.30) | copy-start | bytes 388
  34.7 4.0 %copy-start.16 = (u32[32]{0:T(128)S(1)}, u32[32]{0:T(128)}, u32[]{:S(2)}) copy-start(u32[32]{0:T(128)} %constant.60) | copy-start | bytes 388
  34.7 37.4 %copy-start.5 = (bf16[2,3,2048]{2,0,1:T(2,128)(2,1)S(1)}, bf16[2,3,2048]{2,0,1:T(2,128)(2,1)}, u32[]{:S(2)}) copy-start(bf16[2,3,2048]{2,0,1:T(2,128)(2,1)} %param.26) | copy-start | bytes 73732
  34.7 37.5 %copy-start.6 = (bf16[2,3,512]{2,0,1:T(2,128)(2,1)S(1)}, bf16[2,3,512]{2,0,1:T(2,128)(2,1)}, u32[]{:S(2)}) copy-start(bf16[2,3,512]{2,0,1:T(2,128)(2,1)} %param.27) | copy-start | bytes 18436
  34.7 47.1 %copy-start.12 = (f32[32]{0:T(128)S(1)}, f32[32]{0:T(128)}, u32[]{:S(2)}) copy-start(f32[32]{0:T(128)} %param.28) | copy-start | bytes 388
  37.0 50.6 %copy-start.9 = (bf16[2048]{0:T(1024)(128)(2,1)S(1)}, bf16[2048]{0:T(1024)(128)(2,1)}, u32[]{:S(2)}) copy-start(bf16[2048]{0:T(1024)(128)(2,1)} %param.32) | copy-start | bytes 12292
  38.4 132.8 %all-reduce.6.cloned.1.call-start = ((), (), s32[]{:S(2)}) async-start(), calls=%async_computation | async-start | bytes 131072 | tf_op jit(solution)/shard_map/psum | solution.py:116
  114.3 5.3 %copy-start.10 = (bf16[2048]{0:T(1024)(128)(2,1)S(1)}, bf16[2048]{0:T(1024)(128)(2,1)}, u32[]{:S(2)}) copy-start(bf16[2048]{0:T(1024)(128)(2,1)} %param.34) | copy-start | bytes 12292
  119.5 110.2 %all-reduce.10.cloned.1.call-start = ((), (), s32[]{:S(2)}) async-start(), calls=%async_computation.2 | async-start | bytes 524288
  172.1 25.4 %copy-start.4 = (bf16[8,2048]{1,0:T(8,128)(2,1)}, bf16[8,2048]{1,0:T(8,128)(2,1)S(1)}, u32[]{:S(2)}) copy-start(bf16[8,2048]{1,0:T(8,128)(2,1)S(1)} %get-tuple-element.8) | copy-start | bytes 98308
  183.8 13.8 %copy-start.15 = (s32[2]{0:T(128)S(1)}, s32[2]{0:T(128)}, u32[]{:S(2)}) copy-start(s32[2]{0:T(128)} %param.37) | copy-start | bytes 28
  183.8 45.9 %copy-start.3 = (s32[2,8192]{1,0:T(2,128)S(1)}, s32[2,8192]{1,0:T(2,128)}, u32[]{:S(2)}) copy-start(s32[2,8192]{1,0:T(2,128)} %param.36) | copy-start | bytes 196612
  183.8 73.6 %copy-start.1 = (bf16[2048,512]{1,0:T(8,128)(2,1)S(1)}, bf16[2048,512]{1,0:T(8,128)(2,1)}, u32[]{:S(2)}) copy-start(bf16[2048,512]{1,0:T(8,128)(2,1)} %param.22) | copy-start | bytes 6291460
Sparse Core Ops, SparseCore 0:
  38.5 32.5 all-reduce.7
  119.6 51.4 all-reduce.5
  197.7 31.9 all-reduce.9
where the time goes:
time: 265 us; the launch traced here: 264 us
  waiting for transfers between devices  114 us (43%)
  blocking collectives  84.3 us (32%)
  matrix products  21.8 us (8%)
  between operations  14.7 us (6%)
  local copies, waits for them, and re-layouts  14.5 us (5%)
  other arithmetic  14.2 us (5%)
    unnamed x5, waiting for transfers between devices  62.7 us
    psum x1, waiting for transfers between devices, local(): mixed_complete = lax.psum(mixer_part, 'head')  51.6 us
    dot_general x1, matrix products, local(): jnp.dot(row_block, lexicon_matrix, preferred_element_type=jnp.float32)  13.7 us
    psum x1, blocking collectives, local(): lax.psum(jnp.sum(hidden_wide * hidden_wide, axis=1), 'row')  13.4 us
    all_gather x1, blocking collectives, local(): lax.all_gather(mixer_in, 'row', axis=0, tiled=True)  13.2 us
    psum x1, blocking collectives, local(): group_table = lax.psum(local_squares[:, None] * selector[None, :], 'head')  13.2 us
    unnamed x37, local copies, waits for them, and re-layouts  12.9 us
    pmax x1, blocking collectives, local(): lax.pmax(jnp.max(jnp.where(allowed, candidate_scores, NEG_LARGE), axis=1)...  12.2 us
  transfers between devices with their start and end apart: 3, of which 3 were waited for; matrix products, arithmetic and copies ran while one was open for 1% of the time, Pallas kernels for 0%

commit v1 on v0

v1 whole, which is shorter than its diff:
```python
import functools

import jax
import jax.numpy as jnp
from jax import lax
from jax.experimental import pallas as pl
from jax.experimental.pallas import tpu as pltpu
from jax.sharding import PartitionSpec as P

D = 8192
HEADS = 256
HEAD_DIM = 64
GROUPS = 8

EPSILON = 1e-05
INVERSE_HEAT = 1.25
FIXED_POINT = 65536.0
NEG_LARGE = -1e30

MIB = 2**20
LANES = 128
TILE = 256
SHARES = (3, 12, 18, 24)
VMEM = pl.BlockSpec(memory_space=pltpu.VMEM)
ANY = pl.BlockSpec(memory_space=pl.ANY)
f32 = jnp.float32
bf16 = jnp.bfloat16


def xor_permute(values, axis, distance):
    size = lax.axis_size(axis)
    return lax.ppermute(values, axis, [(at, at ^ distance) for at in range(size)])


def tree_sum(values):
    values = list(values)
    while len(values) > 1:
        values = [a + b for a, b in zip(values[0::2], values[1::2])]
    return values[0]


def split(values):
    high = values.astype(bf16)
    return high, (values - high.astype(f32)).astype(bf16)


def split_three(values):
    high, rest = split(values)
    middle = values - high.astype(f32)
    return high, rest, (middle - rest.astype(f32)).astype(bf16)


def silu(values):
    return values / (1.0 + jnp.exp(-values))


def dot(left, right):
    return jnp.dot(left, right, preferred_element_type=f32)


def dot_transposed(left, right):
    return lax.dot_general(left, right, (((1,), (1,)), ((), ())), preferred_element_type=f32)


def in_hbm(values):
    return pltpu.with_memory_space_constraint(values, pltpu.HBM)


def call(kernel, outs, operands, specs, scratch=(), limit=4, cost=0, out_specs=None, name=None):
    return pl.pallas_call(
        kernel,
        out_shape=outs,
        in_specs=specs,
        out_specs=out_specs if out_specs is not None else jax.tree.map(lambda _: VMEM, outs),
        scratch_shapes=list(scratch),
        compiler_params=pltpu.CompilerParams(vmem_limit_bytes=limit * MIB),
        cost_estimate=pl.CostEstimate(flops=1000, bytes_accessed=cost, transcendentals=0),
        name=name,
    )(*operands)


def shape(dims, dtype=f32):
    return jax.ShapeDtypeStruct(tuple(dims), dtype)


def squares_kernel(count, *refs):
    sources, targets = refs[:count], refs[count : 2 * count]
    squares_ref, sems = refs[2 * count :]
    copies = [pltpu.make_async_copy(sources[at], targets[at], sems.at[at]) for at in range(count)]
    for copy in copies:
        copy.start()
    for copy in copies:
        copy.wait()
    wide = targets[0][...].astype(f32)
    squares_ref[...] = jnp.broadcast_to(jnp.sum(wide * wide, axis=1, keepdims=True), squares_ref.shape)


def prepare_kernel(pieces, *refs):
    hidden_ref, gain_ref, step_ref, state_ref, taps_ref, weight_ref = refs[pieces : pieces + 6]
    normed_ref, sent_ref, small_ref, stack = refs[pieces + 6 :]
    rows = hidden_ref.shape[0]
    columns = weight_ref.shape[1]
    entries = columns // GROUPS
    devices = sent_ref.shape[0]
    squares = tree_sum([ref[...] for ref in refs[:pieces]])[:, 0:1]
    scaled = hidden_ref[...].astype(f32) * lax.rsqrt(squares / D + EPSILON)
    normed = (scaled * gain_ref[...].astype(f32)).astype(bf16)
    normed_ref[...] = normed
    part = dot(normed, weight_ref[...])
    step = dot_transposed(normed, step_ref[...])
    small_ref[:, :columns] = part
    small_ref[:, columns:] = jnp.zeros((rows, LANES), f32)
    small_ref[:, columns : columns + step.shape[1]] = step

    part_high, part_low = split(part)
    stack[...] = jnp.zeros_like(stack)
    stack[:rows] = part_high.astype(f32)
    stack[rows : 2 * rows] = part_low.astype(f32)
    for at in range(3):
        here = 2 * rows + at * state_ref.shape[1]
        stack[here : here + state_ref.shape[1]] = state_ref[at].astype(f32)
    tail = sent_ref.shape[1] - rows
    stack[2 * rows + tail : 2 * rows + tail + taps_ref.shape[0]] = taps_ref[...].astype(f32)
    source = lax.broadcasted_iota(jnp.int32, (columns, columns), 0)
    target = lax.broadcasted_iota(jnp.int32, (columns, columns), 1)
    order = (source % GROUPS) * entries + source // GROUPS == target
    grouped = dot(stack[...].astype(bf16), order.astype(f32).astype(bf16))
    for device in range(devices):
        group = device // (devices // GROUPS)
        here = grouped[:, group * entries : (group + 1) * entries].astype(bf16)
        sent_ref[device, :rows, :entries] = here[:rows]
        sent_ref[device, :rows, entries:] = here[rows : 2 * rows]
        sent_ref[device, rows:, :entries] = here[2 * rows : 2 * rows + tail]
        sent_ref[device, rows:, entries:] = here[2 * rows + tail :]


def input_kernel(normed_ref, weight_ref, _, out_ref, left, held, sems):
    depth, _, width = weight_ref.shape
    rows = normed_ref.shape[0]
    chunks = sems.shape[0]
    part = depth // chunks

    def copy(at):
        here = pl.ds(at * part, part)
        return pltpu.make_async_copy(weight_ref.at[here], held.at[here], sems.at[at])

    for at in range(chunks):
        copy(at).start()
    source = lax.broadcasted_iota(jnp.int32, (LANES, 2 * LANES), 0)
    target = lax.broadcasted_iota(jnp.int32, (LANES, 2 * LANES), 1)
    spread = [(2 * source + at == target).astype(f32).astype(bf16) for at in range(2)]
    for block in range(depth // LANES):
        here = normed_ref[:, block * LANES : (block + 1) * LANES]
        left[:, 2 * block * LANES : 2 * (block + 1) * LANES] = jnp.concatenate(
            [dot(here, spread[at]) for at in range(2)], axis=0
        ).astype(bf16)
    for at in range(chunks):
        copy(at).wait()
        piece = left[:, at * 2 * part : (at + 1) * 2 * part]
        for column in range(0, width, TILE):
            tile = jnp.concatenate(
                [
                    held[at * part : (at + 1) * part, :, start : start + LANES].reshape(2 * part, LANES)
                    for start in range(column, column + TILE, LANES)
                ],
                axis=1,
            )
            term = dot(piece, tile)
            if at == 0:
                out_ref[:, column : column + TILE] = term
            else:
                out_ref[:, column : column + TILE] += term


def pack_kernel(both_ref, small_ref, arrived_ref, out_ref, held_ref):
    rows, width = small_ref.shape[0], both_ref.shape[1]
    blocks, mine, _ = out_ref.shape
    devices, _, double = arrived_ref.shape
    entries = double // 2
    columns = small_ref.shape[1] - LANES
    index = lax.axis_index("row")
    arrived = arrived_ref[...].astype(f32)
    pair = arrived[:, :rows, :entries] + arrived[:, :rows, entries:]
    for device in range(devices):
        here = slice(device * entries, (device + 1) * entries)
        held_ref[0, :, here] = arrived[device, rows:, :entries]
        held_ref[1, :, here] = arrived[device, rows:, entries:]
    for block in range(blocks):
        place = block ^ index
        here = slice(block * mine, (block + 1) * mine)
        out_ref[place, :, :width] = both_ref[here]
        out_ref[place, :, width : 2 * width] = both_ref[rows + block * mine : rows + (block + 1) * mine]
        out_ref[place, :, 2 * width : 2 * width + columns + LANES] = small_ref[here]
        start = 2 * width + columns + LANES
        for device in range(devices):
            out_ref[place, :, start + device * entries : start + (device + 1) * entries] = pair[device, here]


def state_kernel(finish, pieces, *refs):
    parts = [ref[...] for ref in refs[:pieces]]
    (heads_ref, held_ref, inner_state_ref, group_state_ref, inner_taps_ref, group_taps_ref) = refs[
        pieces : pieces + 6
    ]
    del group_taps_ref
    state_ref, gain_ref = refs[pieces + 6 : pieces + 8]
    mixer_ref, next_inner_ref, next_group_ref, driven_ref, decay_ref, input_ref = refs[pieces + 8 :]
    total = tree_sum(parts)
    mine, width, state_width = state_ref.shape
    columns = group_state_ref.shape[2]
    start = 2 * width + columns
    gate = total[:, :width]
    inner_raw = total[:, width : 2 * width].astype(bf16)
    next_inner_ref[0] = inner_state_ref[1]
    next_inner_ref[1] = inner_state_ref[2]
    next_inner_ref[2] = inner_raw
    next_group_ref[0] = group_state_ref[1]
    next_group_ref[1] = group_state_ref[2]
    next_group_ref[2] = total[:, 2 * width : start].astype(bf16)
    taps = inner_taps_ref[...].astype(f32)
    mixed = inner_raw.astype(f32) * taps[3:4]
    for at in range(3):
        mixed = mixed + inner_state_ref[at].astype(f32) * taps[at : at + 1]
    conv_inner = silu(mixed)
    taps = held_ref[1]
    mixed = total[:, start + LANES :].astype(bf16).astype(f32) * taps[3:4]
    for at in range(3):
        mixed = mixed + held_ref[0, at * mine : (at + 1) * mine] * taps[at : at + 1]
    pair = silu(mixed).astype(bf16)
    state_input = pair[:, :state_width].astype(f32)
    state_output = pair[:, state_width:]

    step_raw = total[:, start : start + LANES] + heads_ref[0:1]
    step_size = jnp.maximum(step_raw, 0.0) + jnp.log1p(jnp.exp(-jnp.abs(step_raw)))
    decay_rate = jnp.exp(-step_size * jnp.exp(heads_ref[1:2]))
    stacked = jnp.concatenate([step_size, decay_rate, heads_ref[2:3]], axis=0)
    head = lax.broadcasted_iota(jnp.int32, (LANES, width), 0)
    channel = lax.broadcasted_iota(jnp.int32, (LANES, width), 1)
    spread = (channel // HEAD_DIM == head).astype(f32).astype(bf16)
    wide = tree_sum([dot(part, spread) for part in split_three(stacked)[:2]]) + dot(
        split_three(stacked)[2], spread
    )
    step_wide, decay_wide, skip_wide = wide[:mine], wide[mine : 2 * mine], wide[2 * mine :]
    driven = step_wide * conv_inner
    overlap = jnp.sum(state_input * state_output.astype(f32), axis=1, keepdims=True)
    old = jnp.concatenate(
        [dot_transposed(state_output, state_ref[row])[row : row + 1] for row in range(mine)], axis=0
    )
    readout = decay_wide * old + driven * overlap + skip_wide * conv_inner
    gated = readout * silu(gate)
    driven_ref[...] = driven
    decay_ref[...] = decay_wide
    input_ref[...] = state_input
    if finish:
        group_total = jnp.sum(gated * gated, axis=1, keepdims=True)
        group_scale = lax.rsqrt(group_total / (HEADS * HEAD_DIM // GROUPS) + EPSILON)
        gated = gated * group_scale * gain_ref[...].astype(f32)
    mixer_ref[...] = gated.astype(mixer_ref.dtype)


def update_kernel(driven_ref, decay_ref, input_ref, state_ref, _, out_ref, new, sems):
    mine, width, _ = state_ref.shape
    block = min(512, width)
    blocks = width // block

    def copy(row, at):
        here = pl.ds(at * block, block)
        return pltpu.make_async_copy(new.at[row, here], out_ref.at[row, here], sems.at[row, at])

    for row in range(mine):
        both = jnp.concatenate(
            [driven_ref[row : row + 1], decay_ref[row : row + 1], jnp.zeros((6, width), f32)], axis=0
        )
        turned = jnp.transpose(both)
        for at in range(blocks):
            here = slice(at * block, (at + 1) * block)
            new[row, here] = (
                turned[here, 1:2] * state_ref[row, here].astype(f32)
                + turned[here, 0:1] * input_ref[row : row + 1]
            ).astype(bf16)
            copy(row, at).start()
    for row in range(mine):
        for at in range(blocks):
            copy(row, at).wait()


def output_kernel(pieces, *refs):
    weight_ref, _, out_ref, rows_held = refs[pieces:]
    index = lax.axis_index("row")
    for at in range(pieces):
        rows_held[index ^ at] = refs[at][...].astype(f32)
    left = jnp.concatenate([rows_held[at] for at in range(pieces)], axis=0).astype(bf16)
    width = weight_ref.shape[1]
    for column in range(0, width, TILE):
        out_ref[:, column : column + TILE] = dot(left, weight_ref[:, column : column + TILE])


def add_kernel(left_ref, right_ref, _, out_ref):
    out_ref[...] = left_ref[...] + right_ref[...]


def lexicon_kernel(pieces, *refs):
    hidden_ref, gain_ref, mixed_ref = refs[:3]
    held_refs = refs[3 : 3 + pieces]
    weight_ref, layer_ref, out_ref, rest, left, sems = refs[3 + pieces :]
    rows = hidden_ref.shape[0]
    blocks, mine, _ = out_ref.shape
    vocab = weight_ref.shape[1]
    done = vocab - rest.shape[1]
    copy = pltpu.make_async_copy(weight_ref.at[:, pl.ds(done, vocab - done)], rest, sems.at[0])
    copy.start()
    index = lax.axis_index("row")
    layer = (hidden_ref[...].astype(f32) + mixed_ref[...]).astype(bf16)
    layer_ref[...] = layer
    wide = layer.astype(f32)
    squares = jnp.sum(wide * wide, axis=1, keepdims=True)
    high, low = split(wide * gain_ref[...].astype(f32))
    left[:rows] = high
    left[rows:] = low

    def put(value, column, width):
        for block in range(blocks):
            out_ref[block ^ index, :, column : column + width] = value[block * mine : (block + 1) * mine]

    put(jnp.broadcast_to(squares, (rows, LANES)), vocab, LANES)
    base = 0
    for number, held in enumerate(list(held_refs) + [rest]):
        if number == pieces:
            copy.wait()
        for column in range(0, held.shape[1], TILE):
            term = dot(left[...], held[:, column : column + TILE])
            put(term[:rows] + term[rows:], base + column, TILE)
        base += held.shape[1]


def share_kernel(pieces, *refs):
    mask_ref, sent_ref, share_ref, top_ref, spread = refs[pieces:]
    mine, vocab = mask_ref.shape
    lines = sent_ref.shape[0] // mine
    part = vocab // lines
    total = tree_sum([ref[...] for ref in refs[:pieces]])
    scale = lax.rsqrt(total[:, vocab : vocab + 1] / D + EPSILON) * INVERSE_HEAT
    allowed = mask_ref[...] > 0
    logits = jnp.where(allowed, total[:, :vocab] * scale, NEG_LARGE)
    top = jnp.max(logits, axis=1, keepdims=True)
    share = jnp.where(allowed, jnp.exp(logits - top), 0.0)
    share_ref[...] = share
    top_ref[...] = jnp.broadcast_to(top, top_ref.shape)
    spread[...] = jnp.zeros_like(spread)
    parts = [value.astype(f32) for value in split_three(top)]
    for row in range(mine):
        for line in range(lines):
            here = slice(row * lines + line, row * lines + line + 1)
            spread[here, :part] = share[row : row + 1, line * part : (line + 1) * part]
        here = slice(row * lines, (row + 1) * lines)
        for at in range(3):
            spread[here, part + at : part + at + 1] = jnp.broadcast_to(parts[at][row : row + 1], (lines, 1))
    sent_ref[...] = spread[...].astype(bf16)


def weigh(relative, inverse_floor):
    return relative * jnp.clip(relative * inverse_floor - 1.0, 0.0, 1.0)


def probability_kernel(every_ref, share_ref, top_ref, floor_ref, out_ref):
    mine, vocab = share_ref.shape
    devices, lines, _ = every_ref.shape
    part = vocab * mine // lines
    inverse = FIXED_POINT / floor_ref[:, 0:1].astype(f32)
    tops = [
        jnp.sum(every_ref[device, :, part:].astype(f32), axis=1, keepdims=True)
        for device in range(devices)
    ]
    peak = functools.reduce(jnp.maximum, tops)
    per_row = lines // mine
    spread = jnp.concatenate(
        [jnp.broadcast_to(inverse[row : row + 1], (per_row, 1)) for row in range(mine)], axis=0
    )
    kept = jnp.zeros((lines, part), f32)
    for device in range(devices):
        relative = every_ref[device, :, :part].astype(f32) * jnp.exp(tops[device] - peak)
        kept = kept + weigh(relative, spread)
    kept = jnp.sum(kept, axis=1, keepdims=True)
    total = jnp.concatenate(
        [jnp.sum(kept[row * per_row : (row + 1) * per_row], axis=0, keepdims=True) for row in range(mine)],
        axis=0,
    )
    highest = jnp.concatenate([peak[row * per_row : row * per_row + 1] for row in range(mine)], axis=0)
    own = weigh(share_ref[...] * jnp.exp(top_ref[:, 0:1] - highest), inverse)
    out_ref[...] = (own / total).astype(bf16)


def fetch_kernel(count, starts, *refs):
    sources = refs[:count]
    targets = refs[-count - 1 : -1]
    sems = refs[-1]
    copies = []
    for at in range(count):
        source = sources[at]
        if starts[at] is not None:
            source = source.at[:, pl.ds(starts[at], targets[at].shape[1])]
        copies.append(pltpu.make_async_copy(source, targets[at], sems.at[at]))
    for copy in copies:
        copy.start()
    for copy in copies:
        copy.wait()


def fetch(sources, columns, after, name):
    outs = []
    size = 0
    for source, part in zip(sources, columns):
        dims = source.shape if part is None else (source.shape[0], part[1])
        outs.append(pltpu.VMEM(dims, source.dtype))
        size += 2 * functools.reduce(lambda a, b: a * b, dims)
    starts = [None if part is None else part[0] for part in columns]
    return call(
        functools.partial(fetch_kernel, len(sources), starts),
        outs,
        [in_hbm(source) for source in sources] + [after],
        [ANY] * (len(sources) + 1),
        scratch=[pltpu.SemaphoreType.DMA((len(sources),))],
        limit=1,
        cost=size,
        out_specs=[VMEM] * len(outs),
        name=name,
    )


def local(
    hidden,
    norm_gain,
    input_weight,
    group_weight,
    step_weight,
    conv_inner_weight,
    conv_group_weight,
    conv_inner_state,
    conv_group_state,
    timestep_bias,
    decay_log,
    skip_gain,
    recurrent_state,
    mixer_gain,
    output_weight,
    final_gain,
    lexicon_matrix,
    token_mask,
    min_share,
):
    mine, heads_mine, head_width, state_width = recurrent_state.shape
    width = heads_mine * head_width
    rows, depth = hidden.shape
    vocab = lexicon_matrix.shape[1]
    row_devices = lax.axis_size("row")
    head_devices = lax.axis_size("head")
    group_devices = head_devices // GROUPS
    columns = group_weight.shape[1]
    entries = columns // GROUPS
    held_rows = -(-3 * mine // 8) * 8

    heads = jnp.pad(
        jnp.stack([timestep_bias, decay_log, skip_gain]), ((0, 0), (0, LANES - heads_mine))
    )
    inner_state = jnp.moveaxis(conv_inner_state, 1, 0)
    group_state = jnp.moveaxis(conv_group_state, 1, 0)
    state = recurrent_state.reshape(mine, width, state_width)
    floors = jnp.broadcast_to(min_share[:, None], (mine, LANES))

    small_arrays = [hidden, norm_gain[None], step_weight.T, group_state, conv_group_weight]
    *small_held, squares = call(
        functools.partial(squares_kernel, len(small_arrays)),
        [pltpu.VMEM(array.shape, array.dtype) for array in small_arrays] + [shape((rows, LANES))],
        [in_hbm(array) for array in small_arrays],
        [ANY] * len(small_arrays),
        scratch=[pltpu.SemaphoreType.DMA((len(small_arrays),))],
        limit=1,
        out_specs=[VMEM] * (len(small_arrays) + 1),
        name="squares",
    )
    all_squares = [squares] + [xor_permute(squares, "row", at) for at in range(1, row_devices)]
    (group_held,) = fetch([group_weight], [None], squares, "fetch_group")
    normed, sent, small = call(
        functools.partial(prepare_kernel, row_devices),
        [
            shape((rows, depth), bf16),
            shape((head_devices, rows + held_rows, 2 * entries), bf16),
            shape((rows, columns + LANES)),
        ],
        all_squares + small_held + [group_held],
        [VMEM] * (row_devices + 6),
        scratch=[pltpu.VMEM((2 * rows + 2 * held_rows, columns), f32)],
        limit=4,
        cost=2 * MIB,
        name="group_projection",
    )
    arrived = lax.all_to_all(sent, "head", 0, 0, tiled=True)

    chunks = 8
    both = call(
        input_kernel,
        shape((2 * rows, width)),
        [normed, in_hbm(input_weight), sent],
        [VMEM, ANY, ANY],
        scratch=[
            pltpu.VMEM((2 * rows, 2 * depth), bf16),
            pltpu.VMEM((depth, 2, width), bf16),
            pltpu.SemaphoreType.DMA((chunks,)),
        ],
        limit=24,
        cost=2 * input_weight.size,
        name="input_projection",
    )
    packed_width = 2 * width + columns + LANES + 2 * state_width
    packed, held = call(
        pack_kernel,
        [shape((row_devices, mine, packed_width)), shape((2, held_rows, 2 * state_width))],
        [both, small, arrived],
        [VMEM] * 3,
        name="pack_rows",
    )
    pieces = [packed[0]] + [xor_permute(packed[at], "row", at) for at in range(1, row_devices)]

    tiles = vocab // TILE
    cuts = [tiles * share // 32 * TILE for share in SHARES]
    spans = [(start, end - start) for start, end in zip([0] + cuts[:-1], cuts)]
    fetched = []

    def fetch_lexicon(stage, after, name):
        if spans[stage][1]:
            fetched.extend(fetch([lexicon_matrix], [spans[stage]], after, name))
            return fetched[-1]
        return after

    output_held, state_held, *fetched = fetch(
        [output_weight, state] + [lexicon_matrix] * (spans[0][1] > 0),
        [None, None] + [spans[0]] * (spans[0][1] > 0),
        packed,
        "fetch_output",
    )

    finish = group_devices == 1
    mixer_in, next_inner, next_group, driven, decay, state_input = call(
        functools.partial(state_kernel, finish, row_devices),
        [
            shape((mine, width), bf16 if finish else f32),
            shape((3, mine, width), bf16),
            shape((3, mine, columns), bf16),
            shape((mine, width)),
            shape((mine, width)),
            shape((mine, state_width)),
        ],
        pieces
        + [heads, held, inner_state, group_state, conv_inner_weight, conv_group_weight, state_held]
        + [mixer_gain[None]],
        [VMEM] * (row_devices + 8),
        limit=8,
        cost=2 * MIB,
        name="state_readout",
    )
    if not finish:
        members = [
            [group * group_devices + at for at in range(group_devices)] for group in range(GROUPS)
        ]
        group_total = lax.psum(jnp.sum(mixer_in * mixer_in, axis=1), "head", axis_index_groups=members)
        group_scale = lax.rsqrt(group_total / (HEADS * HEAD_DIM // GROUPS) + EPSILON)
        mixer_in = (mixer_in * group_scale[:, None] * mixer_gain.astype(f32)[None]).astype(bf16)

    mixer_rows = [mixer_in] + [xor_permute(mixer_in, "row", at) for at in range(1, row_devices)]
    ahead = fetch_lexicon(1, mixer_in, "fetch_lexicon_1")
    mixed = call(
        functools.partial(output_kernel, row_devices),
        shape((rows, depth)),
        mixer_rows + [output_held, ahead],
        [VMEM] * (row_devices + 1) + [ANY],
        scratch=[pltpu.VMEM((row_devices, mine, width), f32)],
        cost=4 * MIB,
        name="output_projection",
    )
    distance = 1
    while distance < head_devices:
        other = xor_permute(mixed, "head", distance)
        ahead = mixed
        for stage, place in ((2, head_devices // 4), (3, head_devices // 2)):
            if distance == place:
                ahead = fetch_lexicon(stage, mixed, f"fetch_lexicon_{stage}")
        mixed = call(
            add_kernel, shape((rows, depth)), [mixed, other, ahead], [VMEM, VMEM, ANY], name="add"
        )
        distance *= 2
    layer_out, scores = call(
        functools.partial(lexicon_kernel, len(fetched)),
        [shape((rows, depth), bf16), shape((row_devices, mine, vocab + LANES))],
        [hidden, final_gain[None], mixed] + fetched + [in_hbm(lexicon_matrix)],
        [VMEM] * (3 + len(fetched)) + [ANY],
        scratch=[
            pltpu.VMEM((depth, vocab - cuts[-1]), bf16),
            pltpu.VMEM((2 * rows, depth), bf16),
            pltpu.SemaphoreType.DMA((1,)),
        ],
        limit=12,
        cost=16 * MIB,
        name="lexicon_projection",
    )
    score_rows = [scores[0]] + [xor_permute(scores[at], "row", at) for at in range(1, row_devices)]
    next_state = call(
        update_kernel,
        shape((mine, width, state_width), bf16),
        [driven, decay, state_input, state_held, scores],
        [VMEM] * 4 + [ANY],
        scratch=[
            pltpu.VMEM((mine, width, state_width), bf16),
            pltpu.SemaphoreType.DMA((mine, width // min(512, width))),
        ],
        limit=8,
        cost=4 * MIB,
        out_specs=ANY,
        name="state_update",
    )
    lines = 8 * mine
    shares, share, top = call(
        functools.partial(share_kernel, row_devices),
        [
            shape((lines, vocab * mine // lines + LANES), bf16),
            shape((mine, vocab)),
            shape((mine, LANES)),
        ],
        score_rows + [token_mask],
        [VMEM] * (row_devices + 1),
        scratch=[pltpu.VMEM((lines, vocab * mine // lines + LANES), f32)],
        name="share_of_peak",
    )
    every = lax.all_gather(shares, "head", axis=0)
    next_probs = call(
        probability_kernel,
        shape((mine, vocab), bf16),
        [every, share, top, floors],
        [VMEM] * 4,
        name="probabilities",
    )
    return (
        next_state.reshape(recurrent_state.shape),
        jnp.moveaxis(next_inner, 0, 1),
        jnp.moveaxis(next_group, 0, 1),
        layer_out,
        next_probs,
    )


def solution(mesh):
    in_specs = (
        P(None, "row"),
        P("row"),
        P("row", None, "head"),
        P("row", "head"),
        P("row", "head"),
        P(None, "head"),
        P(None, "head"),
        P("row", None, "head"),
        P("row", None, "head"),
        P("head"),
        P("head"),
        P("head"),
        P("row", "head", None, None),
        P("head"),
        P("head", "row"),
        P("row"),
        P("row", "head"),
        P("row", "head"),
        P("row"),
    )
    out_specs = (
        P("row", "head", None, None),
        P("row", None, "head"),
        P("row", None, "head"),
        P(None, "row"),
        P("row", "head"),
    )
    return jax.shard_map(local, mesh=mesh, in_specs=in_specs, out_specs=out_specs, check_vma=False)
```

time: 265 us -> 84 us (0.32)
  waiting for transfers between devices: 114 us -> 6.23 us
  blocking collectives: 84.3 us -> 9.31 us
  Pallas kernels: 0 us -> 38.5 us
  starting transfers between devices: 0.12 us -> 26.3 us
  matrix products: 21.8 us -> 0 us
  other arithmetic: 14.2 us -> 0.01 us
  between operations: 14.7 us -> 0.99 us
  local copies, waits for them, and re-layouts: 14.5 us -> 2.2 us
    unnamed x5 -> x0, waiting for transfers between devices: 62.7 us -> none
    psum x1 -> x0, waiting for transfers between devices: 51.6 us -> none  [local(): mixed_complete = lax.psum(mixer_part, 'head')]
    psum x4 -> x0, blocking collectives: 50.1 us -> none  [the longest x1 13.4 us: local(): lax.psum(jnp.sum(hidden_wide * hidden_wide, axis=1), 'row')]
    pallas_call x0 -> x18, Pallas kernels: none -> 38.5 us  [call(): pl.pallas_call(kernel, out_shape=outs, in_specs=specs, out_specs=out_spec...]
    ppermute x0 -> x15, starting transfers between devices: none -> 22.6 us  [xor_permute(): lax.ppermute(values, axis, [(at, at ^ distance) for at in range(size)])]
    dot_general x5 -> x0, matrix products: 21.8 us -> none  [the longest x1 13.7 us: local(): jnp.dot(row_block, lexicon_matrix, preferred_element_type=jnp.float32)]
    all_gather x2 -> x1, blocking collectives: 22.1 us -> 9.31 us  [local(): every = lax.all_gather(shares, 'head', axis=0)]
    pmax x1 -> x0, blocking collectives: 12.2 us -> none  [local(): lax.pmax(jnp.max(jnp.where(allowed, candidate_scores, NEG_LARGE), axis=1)...]
  transfers between devices with their start and end apart: 3 -> 16, of which waited for: 3 -> 5; matrix products, arithmetic and copies ran while one was open for 1% -> 0% of each run, Pallas kernels for 0% -> 31%
where the time goes in v1:
time: 84 us; the launch traced here: 83.5 us
  Pallas kernels  38.5 us (46%)
  starting transfers between devices  26.3 us (31%)
  blocking collectives  9.31 us (11%)
  waiting for transfers between devices  6.23 us (7%)
  local copies, waits for them, and re-layouts  2.2 us (3%)
  between operations  0.99 us (1%)
    pallas_call x18, Pallas kernels, call(): pl.pallas_call(kernel, out_shape=outs, in_specs=specs, out_specs=out_spec...  38.5 us
    ppermute x15, starting transfers between devices, xor_permute(): lax.ppermute(values, axis, [(at, at ^ distance) for at in range(size)])  22.6 us
    all_gather x1, blocking collectives, local(): every = lax.all_gather(shares, 'head', axis=0)  9.31 us
    ppermute x15, waiting for transfers between devices, xor_permute(): lax.ppermute(values, axis, [(at, at ^ distance) for at in range(size)])  6.22 us
    all_to_all x1, starting transfers between devices, local(): arrived = lax.all_to_all(sent, 'head', 0, 0, tiled=True)  3.72 us
  transfers between devices with their start and end apart: 16, of which 5 were waited for; matrix products, arithmetic and copies ran while one was open for 0% of the time, Pallas kernels for 31%

profile of v1, /device:TPU:0, one launch (start us, length us, event | category | flops | bytes accessed | tf_op | source)
XLA Modules:
  0.0 83.5 jit_solution(1193541802414173259)
XLA Ops:
  0.6 1.3 %broadcast_in_dim.15.refs_1_ = bf16[1,2048]{1,0:T(2,128)(2,1)} reshape(bf16[2048]{0:T(1024)(128)(2,1)} %param.20) | data formatting | bytes 8192 | tf_op jit(solution)/shard_map/broadcast_in_dim | solution.py:469
  1.9 1.1 %squares.1 = (bf16[8,2048]{1,0:T(8,128)(2,1)S(1)}, bf16[1,2048]{1,0:T(2,128)(2,1)S(1)}, bf16[32,2048]{1,0:T(8,128)(2,1)S(1)}, bf16[3,2,512]{2,1,0:T(2,128)(2,1)S...) custom-call(bf16[8,2048]{1,0:T(8,128)(2,1)} %refs_0_.13, bf16[1,2048]{1,0:T(2,128)(2,1)} %broadcast_in_dim.15.refs_1_, ...), custom_call_target="tpu_custom_call" | custom-call | flops 1000 | tf_op jit(solution)/shard_map/squares/pallas_call | solution.py:70
  3.0 3.1 %collective-permute-start = (f32[8,128]{1,0:T(8,128)S(1)}, f32[8,128]{1,0:T(8,128)S(1)}, u32[]{:S(2)}, u32[]{:S(2)}) collective-permute-start(f32[8,128]{1,0:T(8,128)S(1)} %get-tuple-element.30.refs_1_.refs_0_), channel_id=1, source_target_pairs={{0,8},{8,0},{16,24},{24,16},{1,9},{9,1},{17,25},{25,17},{2,10},{10... | collective-permute-start | bytes 12296 | tf_op jit(solution)/shard_map/ppermute | solution.py:32
  6.1 2.6 %collective-permute-start.1 = (f32[8,128]{1,0:T(8,128)S(1)}, f32[8,128]{1,0:T(8,128)S(1)}, u32[]{:S(2)}, u32[]{:S(2)}) collective-permute-start(f32[8,128]{1,0:T(8,128)S(1)} %get-tuple-element.30.refs_1_.refs_0_), channel_id=1, source_target_pairs={{0,16},{8,24},{16,0},{24,8},{1,17},{9,25},{17,1},{25,9},{2,18},{10... | collective-permute-start | bytes 12296 | tf_op jit(solution)/shard_map/ppermute | solution.py:32
  8.7 0.0 collective-permute-start.2
  8.7 1.6 %fetch_group.1.refs_9_ = bf16[2048,512]{1,0:T(8,128)(2,1)S(1)} custom-call(bf16[2048,512]{1,0:T(8,128)(2,1)} %refs_0_.8, f32[8,128]{1,0:T(8,128)S(1)} %get-tuple-element.30.refs_1_.refs_0_), custom_call_target="tpu_custom_call" | custom-call | flops 1000 | bytes 2097152 | tf_op jit(solution)/shard_map/fetch_group/pallas_call | solution.py:70
  10.3 0.0 collective-permute-done.refs_1_
  10.3 0.3 collective-permute-done.1.refs_2_
  10.6 3.5 %collective-permute-done.2.refs_3_ = f32[8,128]{1,0:T(8,128)S(1)} collective-permute-done((f32[8,128]{1,0:T(8,128)S(1)}, f32[8,128]{1,0:T(8,128)S(1)}, u32[]{:S(2)}, u32[]{:S(2)}) %collective-permute-start.2) | collective-permute-done | bytes 4128 | tf_op jit(solution)/shard_map/ppermute | solution.py:32
  14.1 1.3 %group_projection.1 = (bf16[8,2048]{1,0:T(8,128)(2,1)S(1)}, bf16[8,16,128]{2,1,0:T(8,128)(2,1)}, f32[8,640]{1,0:T(8,128)S(1)}) custom-call(f32[8,128]{1,0:T(8,128)S(1)} %get-tuple-element.30.refs_1_.refs_0_, f32[8,128]{1,0:T(8,128)S(1)} %collective-permute-done.refs_1_, f32[8,128]{1,0:T(8,128)S(1)} %collective-permute-done.1.refs_2_, ...), custom_call_target="tpu_custom_call" | custom-call | flops 1000 | bytes 2097152 | tf_op jit(solution)/shard_map/group_projection/pallas_call | solution.py:70
  15.4 3.7 %all-to-all-start = ((bf16[8,16,128]{2,1,0:T(8,128)(2,1)}), bf16[8,16,128]{2,1,0:T(8,128)(2,1)S(1)}, u32[]{:S(2)}, u32[]{:S(2)}) async-start(bf16[8,16,128]{2,1,0:T(8,128)(2,1)} %get-tuple-element.37._), calls=%async_computation | async-start | bytes 65536 | tf_op jit(solution)/shard_map/all_to_all | solution.py:496
  19.1 0.0 copy-start.9
  19.1 0.0 copy-start.10
  19.1 0.0 copy-start.6
  19.1 7.1 %input_projection.1.both_ref = f32[16,2048]{1,0:T(8,128)S(1)} custom-call(bf16[8,2048]{1,0:T(8,128)(2,1)S(1)} %get-tuple-element.36.normed_ref, bf16[2048,2,2048]{2,1,0:T(2,128)(2,1)} %weight_ref.1, bf16[8,16,128]{2,1,0:T(8,128)(2,1)} %get-tuple-element.37._), custom_call_target="tpu_custom_call" | custom-call | flops 1000 | bytes 16777216 | tf_op jit(solution)/shard_map/input_projection/pallas_call | solution.py:70
  26.3 0.2 pack_rows.1
  26.5 0.1 collective-permute-start.3
  26.6 0.8 collective-permute-start.4
  27.3 3.6 %collective-permute-start.5 = (f32[2,5248]{1,0:T(2,128)S(1)}, f32[2,5248]{1,0:T(2,128)S(1)}, u32[]{:S(2)}, u32[]{:S(2)}) collective-permute-start(f32[2,5248]{1,0:T(2,128)S(1)} %get-tuple-element.59), channel_id=1, source_target_pairs={{0,24},{8,16},{16,8},{24,0},{1,25},{9,17},{17,9},{25,1},{2,26},{10... | collective-permute-start | bytes 125960 | tf_op jit(solution)/shard_map/ppermute | solution.py:32
  31.0 0.0 copy-start.2
  31.0 0.0 copy-start.3
  31.0 0.0 copy-start.4
  31.0 0.0 copy-start.5
  31.0 4.9 %fetch_output.1 = (bf16[2048,2048]{1,0:T(8,128)(2,1)S(1)}, bf16[2,2048,256]{2,1,0:T(8,128)(2,1)S(1)}, bf16[2048,768]{1,0:T(8,128)(2,1)S(1)}) custom-call(bf16[2048,2048]{1,0:T(8,128)(2,1)} %refs_0_.9, bf16[2,2048,256]{2,1,0:T(8,128)(2,1)} %bitcast.31, bf16[2048,8192]{1,0:T(8,128)(2,1)} %refs_7_.1, f32[4,2,5248]{2,1,0:T(2,128)S(1)} %get-tuple-element.39.refs_3_), custom_call_target="tpu_custom_call" | custom-call | flops 1000 | bytes 13631488 | tf_op jit(solution)/shard_map/fetch_output/pallas_call | solution.py:70
  36.0 1.4 %state_readout.1 = (bf16[2,2048]{1,0:T(2,128)(2,1)S(1)}, bf16[3,2,2048]{2,1,0:T(2,128)(2,1)}, bf16[3,2,512]{2,1,0:T(2,128)(2,1)}, f32[2,2048]{1,0:T(2,128)S(1)},...) custom-call(f32[2,5248]{1,0:T(2,128)S(1)} %get-tuple-element.62.refs_0_, f32[2,5248]{1,0:T(2,128)S(1)} %collective-permute-done.3.refs_1_, ...), custom_call_target="tpu_custom_call" | custom-call | flops 1000 | bytes 2097152 | tf_op jit(solution)/shard_map/state_readout/pallas_call | solution.py:70
  37.5 1.3 %collective-permute-start.7 = (bf16[2,2048]{1,0:T(2,128)(2,1)S(1)}, bf16[2,2048]{1,0:T(2,128)(2,1)S(1)}, u32[]{:S(2)}, u32[]{:S(2)}) collective-permute-start(bf16[2,2048]{1,0:T(2,128)(2,1)S(1)} %get-tuple-element.45.refs_1_.refs_0_), channel_id=1, source_target_pairs={{0,16},{8,24},{16,0},{24,8},{1,17},{9,25},{17,1},{25,9},{2,18},{10... | collective-permute-start | bytes 24584 | tf_op jit(solution)/shard_map/ppermute | solution.py:32
  38.8 3.1 %collective-permute-start.8 = (bf16[2,2048]{1,0:T(2,128)(2,1)S(1)}, bf16[2,2048]{1,0:T(2,128)(2,1)S(1)}, u32[]{:S(2)}, u32[]{:S(2)}) collective-permute-start(bf16[2,2048]{1,0:T(2,128)(2,1)S(1)} %get-tuple-element.45.refs_1_.refs_0_), channel_id=1, source_target_pairs={{0,24},{8,16},{16,8},{24,0},{1,25},{9,17},{17,9},{25,1},{2,26},{10... | collective-permute-start | bytes 24584 | tf_op jit(solution)/shard_map/ppermute | solution.py:32
  41.8 3.7 %fetch_lexicon_1.1.refs_5_.refs_4_ = bf16[2048,2304]{1,0:T(8,128)(2,1)S(1)} custom-call(bf16[2048,8192]{1,0:T(8,128)(2,1)} %refs_7_.1, bf16[2,2048]{1,0:T(2,128)(2,1)S(1)} %get-tuple-element.45.refs_1_.refs_0_), custom_call_target="tpu_custom_call" | custom-call | flops 1000 | bytes 9437184 | tf_op jit(solution)/shard_map/fetch_lexicon_1/pallas_call | solution.py:70
  45.6 1.2 %output_projection.1.left_ref._ = f32[8,2048]{1,0:T(8,128)S(1)} custom-call(bf16[2,2048]{1,0:T(2,128)(2,1)S(1)} %get-tuple-element.45.refs_1_.refs_0_, bf16[2,2048]{1,0:T(2,128)(2,1)S(1)} %collective-permute-done.6.refs_1_, bf16[2,2048]{1,0:T(2,128)(2,1)S(1)} %collective-permute-done.7.refs_2_, bf16[2,2048]{1,0:T(2,128)(2,1)S(1)} %collective-permute-done.8.refs_3_, ...), custom_call_target="tpu_custom_call" | custom-call | flops 1000 | bytes 4194304 | tf_op jit(solution)/shard_map/output_projection/pallas_call | solution.py:70
  46.8 1.3 %collective-permute-done.9.right_ref = f32[8,2048]{1,0:T(8,128)S(1)} collective-permute-done((f32[8,2048]{1,0:T(8,128)S(1)}, f32[8,2048]{1,0:T(8,128)S(1)}, u32[]{:S(2)}, u32[]{:S(2)}) %collective-permute-start.9) | collective-permute-done | bytes 65568 | tf_op jit(solution)/shard_map/ppermute | solution.py:32
  48.0 2.1 %collective-permute-start.10 = (f32[8,2048]{1,0:T(8,128)S(1)}, f32[8,2048]{1,0:T(8,128)S(1)}, u32[]{:S(2)}, u32[]{:S(2)}) collective-permute-start(f32[8,2048]{1,0:T(8,128)S(1)} %add.5.refs_1_.left_ref), channel_id=1, source_target_pairs={{0,2},{1,3},{2,0},{3,1},{4,6},{5,7},{6,4},{7,5},{8,10},{9,11},{10,... | collective-permute-start | bytes 196616 | tf_op jit(solution)/shard_map/ppermute | solution.py:32
  50.1 2.8 %fetch_lexicon_2.1._.refs_5_ = bf16[2048,1536]{1,0:T(8,128)(2,1)S(1)} custom-call(bf16[2048,8192]{1,0:T(8,128)(2,1)} %refs_7_.1, f32[8,2048]{1,0:T(8,128)S(1)} %add.5.refs_1_.left_ref), custom_call_target="tpu_custom_call" | custom-call | flops 1000 | bytes 6291456 | tf_op jit(solution)/shard_map/fetch_lexicon_2/pallas_call | solution.py:70
  52.9 0.0 copy-start.7
  52.9 1.5 %collective-permute-start.11 = (f32[8,2048]{1,0:T(8,128)S(1)}, f32[8,2048]{1,0:T(8,128)S(1)}, u32[]{:S(2)}, u32[]{:S(2)}) collective-permute-start(f32[8,2048]{1,0:T(8,128)S(1)} %add.6.refs_1_.left_ref), channel_id=1, source_target_pairs={{0,4},{1,5},{2,6},{3,7},{4,0},{5,1},{6,2},{7,3},{8,12},{9,13},{10,... | collective-permute-start | bytes 196616 | tf_op jit(solution)/shard_map/ppermute | solution.py:32
  54.5 2.8 %fetch_lexicon_3.1._.refs_6_ = bf16[2048,1536]{1,0:T(8,128)(2,1)S(1)} custom-call(bf16[2048,8192]{1,0:T(8,128)(2,1)} %refs_7_.1, f32[8,2048]{1,0:T(8,128)S(1)} %add.6.refs_1_.left_ref), custom_call_target="tpu_custom_call" | custom-call | flops 1000 | bytes 6291456 | tf_op jit(solution)/shard_map/fetch_lexicon_3/pallas_call | solution.py:70
  57.3 0.0 copy-start
  57.3 0.7 copy-done
  58.1 6.3 %lexicon_projection.1 = (bf16[8,2048]{1,0:T(8,128)(2,1)}, f32[4,2,8320]{2,1,0:T(2,128)S(1)}) custom-call(bf16[8,2048]{1,0:T(8,128)(2,1)S(1)} %copy-done, bf16[1,2048]{1,0:T(2,128)(2,1)S(1)} %broadcast_in_dim.17.refs_1_, f32[8,2048]{1,0:T(8,128)S(1)} %add.7.refs_2_, bf16[2048,768]{1,0:T(8,128)(2,1)S(1)} %get-tuple-element.47.refs_3_, ...), custom_call_target="tpu_custom_call" | custom-call | flops 1000 | bytes 16777216 | tf_op jit(solution)/shard_map/lexicon_projection/pallas_call | solution.py:70
  64.4 0.1 collective-permute-start.12
  64.5 2.3 %collective-permute-start.13 = (f32[2,8320]{1,0:T(2,128)S(1)}, f32[2,8320]{1,0:T(2,128)S(1)}, u32[]{:S(2)}, u32[]{:S(2)}) collective-permute-start(f32[2,8320]{1,0:T(2,128)S(1)} %get-tuple-element.56), channel_id=1, source_target_pairs={{0,16},{8,24},{16,0},{24,8},{1,17},{9,25},{17,1},{25,9},{2,18},{10... | collective-permute-start | bytes 199688 | tf_op jit(solution)/shard_map/ppermute | solution.py:32
  66.7 2.1 %collective-permute-start.14 = (f32[2,8320]{1,0:T(2,128)S(1)}, f32[2,8320]{1,0:T(2,128)S(1)}, u32[]{:S(2)}, u32[]{:S(2)}) collective-permute-start(f32[2,8320]{1,0:T(2,128)S(1)} %get-tuple-element.55), channel_id=1, source_target_pairs={{0,24},{8,16},{16,8},{24,0},{1,25},{9,17},{17,9},{25,1},{2,26},{10... | collective-permute-start | bytes 199688 | tf_op jit(solution)/shard_map/ppermute | solution.py:32
  68.8 2.9 %state_update.1 = bf16[2,2048,256]{2,1,0:T(8,128)(2,1)} custom-call(f32[2,2048]{1,0:T(2,128)S(1)} %get-tuple-element.42.driven_ref, f32[2,2048]{1,0:T(2,128)S(1)} %get-tuple-element.43.decay_ref, f32[2,256]{1,0:T(2,128)S(1)} %get-tuple-element.44.input_ref, bf16[2,2048,256]{2,1,0:T(8,128)(2,1)S(1)} %get-tuple-element.41.refs_10_.state_ref, ...), custom_call_target="tpu_custom_call" | custom-call | flops 1000 | bytes 4194304 | tf_op jit(solution)/shard_map/state_update/pallas_call | solution.py:70
  71.7 0.2 collective-permute-done.13.refs_2_
  71.9 1.0 %collective-permute-done.14.refs_3_ = f32[2,8320]{1,0:T(2,128)S(1)} collective-permute-done((f32[2,8320]{1,0:T(2,128)S(1)}, f32[2,8320]{1,0:T(2,128)S(1)}, u32[]{:S(2)}, u32[]{:S(2)}) %collective-permute-start.14) | collective-permute-done | bytes 66592 | tf_op jit(solution)/shard_map/ppermute | solution.py:32
  72.9 0.2 share_of_peak.1
  73.1 9.3 %all-gather = bf16[128,1152]{1,0:T(8,128)(2,1)S(1)} all-gather(bf16[16,1152]{1,0:T(8,128)(2,1)S(1)} %get-tuple-element.52), channel_id=2, replica_groups=mesh['row'=4,'head'=8] {'head'}, dimensions={0}, use_global_device_ids=true | all-gather | bytes 331776 | tf_op jit(solution)/shard_map/all_gather | solution.py:632
  82.4 0.1 broadcast_in_dim.18.floor_ref
  82.5 1.1 %probabilities.1 = bf16[2,8192]{1,0:T(2,128)(2,1)} custom-call(bf16[8,16,1152]{2,1,0:T(8,128)(2,1)S(1)} %bitcast.27, f32[2,8192]{1,0:T(2,128)S(1)} %get-tuple-element.53.share_ref, f32[2,128]{1,0:T(2,128)S(1)} %get-tuple-element.54.top_ref, s32[2,128]{1,0:T(2,128)S(1)} %broadcast_in_dim.18.floor_ref), custom_call_target="tpu_custom_call" | custom-call | flops 1000 | tf_op jit(solution)/shard_map/probabilities/pallas_call | solution.py:70
  (34 shorter events, 0.1 us)
Async XLA Ops:
  3.0 7.3 %collective-permute-start = (f32[8,128]{1,0:T(8,128)S(1)}, f32[8,128]{1,0:T(8,128)S(1)}, u32[]{:S(2)}, u32[]{:S(2)}) collective-permute-start(f32[8,128]{1,0:T(8,128)S(1)} %get-tuple-element.30.refs_1_.refs_0_), channel_id=1, source_target_pairs={{0,8},{8,0},{16,24},{24,16},{1,9},{9,1},{17,25},{25,17},{2,10},{10... | collective-permute-start | bytes 12296 | tf_op jit(solution)/shard_map/ppermute | solution.py:32
  6.1 4.5 %collective-permute-start.1 = (f32[8,128]{1,0:T(8,128)S(1)}, f32[8,128]{1,0:T(8,128)S(1)}, u32[]{:S(2)}, u32[]{:S(2)}) collective-permute-start(f32[8,128]{1,0:T(8,128)S(1)} %get-tuple-element.30.refs_1_.refs_0_), channel_id=1, source_target_pairs={{0,16},{8,24},{16,0},{24,8},{1,17},{9,25},{17,1},{25,9},{2,18},{10... | collective-permute-start | bytes 12296 | tf_op jit(solution)/shard_map/ppermute | solution.py:32
  8.7 5.4 %collective-permute-start.2 = (f32[8,128]{1,0:T(8,128)S(1)}, f32[8,128]{1,0:T(8,128)S(1)}, u32[]{:S(2)}, u32[]{:S(2)}) collective-permute-start(f32[8,128]{1,0:T(8,128)S(1)} %get-tuple-element.30.refs_1_.refs_0_), channel_id=1, source_target_pairs={{0,24},{8,16},{16,8},{24,0},{1,25},{9,17},{17,9},{25,1},{2,26},{10... | collective-permute-start | bytes 12296 | tf_op jit(solution)/shard_map/ppermute | solution.py:32
  15.4 10.9 %all-to-all-start = ((bf16[8,16,128]{2,1,0:T(8,128)(2,1)}), bf16[8,16,128]{2,1,0:T(8,128)(2,1)S(1)}, u32[]{:S(2)}, u32[]{:S(2)}) async-start(bf16[8,16,128]{2,1,0:T(8,128)(2,1)} %get-tuple-element.37._), calls=%async_computation | async-start | bytes 65536 | tf_op jit(solution)/shard_map/all_to_all | solution.py:496
  19.1 11.8 %copy-start.8 = (f32[32]{0:T(128)S(1)}, f32[32]{0:T(128)}, u32[]{:S(2)}) copy-start(f32[32]{0:T(128)} %param.30) | copy-start | bytes 388
  19.1 11.8 %copy-start.9 = (f32[32]{0:T(128)S(1)}, f32[32]{0:T(128)}, u32[]{:S(2)}) copy-start(f32[32]{0:T(128)} %param.29) | copy-start | bytes 388
  19.1 11.8 %copy-start.10 = (f32[32]{0:T(128)S(1)}, f32[32]{0:T(128)}, u32[]{:S(2)}) copy-start(f32[32]{0:T(128)} %param.28) | copy-start | bytes 388
  19.1 11.8 %copy-start.6 = (bf16[2048]{0:T(1024)(128)(2,1)S(1)}, bf16[2048]{0:T(1024)(128)(2,1)}, u32[]{:S(2)}) copy-start(bf16[2048]{0:T(1024)(128)(2,1)} %param.32) | copy-start | bytes 12292
  26.5 9.5 %collective-permute-start.3 = (f32[2,5248]{1,0:T(2,128)S(1)}, f32[2,5248]{1,0:T(2,128)S(1)}, u32[]{:S(2)}, u32[]{:S(2)}) collective-permute-start(f32[2,5248]{1,0:T(2,128)S(1)} %get-tuple-element.61), channel_id=1, source_target_pairs={{0,8},{8,0},{16,24},{24,16},{1,9},{9,1},{17,25},{25,17},{2,10},{10... | collective-permute-start | bytes 125960 | tf_op jit(solution)/shard_map/ppermute | solution.py:32
  26.6 9.4 %collective-permute-start.4 = (f32[2,5248]{1,0:T(2,128)S(1)}, f32[2,5248]{1,0:T(2,128)S(1)}, u32[]{:S(2)}, u32[]{:S(2)}) collective-permute-start(f32[2,5248]{1,0:T(2,128)S(1)} %get-tuple-element.60), channel_id=1, source_target_pairs={{0,16},{8,24},{16,0},{24,8},{1,17},{9,25},{17,1},{25,9},{2,18},{10... | collective-permute-start | bytes 125960 | tf_op jit(solution)/shard_map/ppermute | solution.py:32
  27.3 8.6 %collective-permute-start.5 = (f32[2,5248]{1,0:T(2,128)S(1)}, f32[2,5248]{1,0:T(2,128)S(1)}, u32[]{:S(2)}, u32[]{:S(2)}) collective-permute-start(f32[2,5248]{1,0:T(2,128)S(1)} %get-tuple-element.59), channel_id=1, source_target_pairs={{0,24},{8,16},{16,8},{24,0},{1,25},{9,17},{17,9},{25,1},{2,26},{10... | collective-permute-start | bytes 125960 | tf_op jit(solution)/shard_map/ppermute | solution.py:32
  31.0 5.0 %copy-start.2 = (bf16[2,3,2048]{2,0,1:T(2,128)(2,1)S(1)}, bf16[2,3,2048]{2,0,1:T(2,128)(2,1)}, u32[]{:S(2)}) copy-start(bf16[2,3,2048]{2,0,1:T(2,128)(2,1)} %param.26) | copy-start | bytes 73732
  31.0 5.0 %copy-start.3 = (bf16[2,3,512]{2,0,1:T(2,128)(2,1)S(1)}, bf16[2,3,512]{2,0,1:T(2,128)(2,1)}, u32[]{:S(2)}) copy-start(bf16[2,3,512]{2,0,1:T(2,128)(2,1)} %param.27) | copy-start | bytes 18436
  31.0 5.0 %copy-start.4 = (bf16[4,2048]{1,0:T(4,128)(2,1)S(1)}, bf16[4,2048]{1,0:T(4,128)(2,1)}, u32[]{:S(2)}) copy-start(bf16[4,2048]{1,0:T(4,128)(2,1)} %refs_8_.1) | copy-start | bytes 49156
  31.0 5.0 %copy-start.5 = (bf16[4,512]{1,0:T(4,128)(2,1)S(1)}, bf16[4,512]{1,0:T(4,128)(2,1)}, u32[]{:S(2)}) copy-start(bf16[4,512]{1,0:T(4,128)(2,1)} %refs_9_.1) | copy-start | bytes 12292
  37.4 8.1 %collective-permute-start.6 = (bf16[2,2048]{1,0:T(2,128)(2,1)S(1)}, bf16[2,2048]{1,0:T(2,128)(2,1)S(1)}, u32[]{:S(2)}, u32[]{:S(2)}) collective-permute-start(bf16[2,2048]{1,0:T(2,128)(2,1)S(1)} %get-tuple-element.45.refs_1_.refs_0_), channel_id=1, source_target_pairs={{0,8},{8,0},{16,24},{24,16},{1,9},{9,1},{17,25},{25,17},{2,10},{10... | collective-permute-start | bytes 24584 | tf_op jit(solution)/shard_map/ppermute | solution.py:32
  37.5 8.1 %collective-permute-start.7 = (bf16[2,2048]{1,0:T(2,128)(2,1)S(1)}, bf16[2,2048]{1,0:T(2,128)(2,1)S(1)}, u32[]{:S(2)}, u32[]{:S(2)}) collective-permute-start(bf16[2,2048]{1,0:T(2,128)(2,1)S(1)} %get-tuple-element.45.refs_1_.refs_0_), channel_id=1, source_target_pairs={{0,16},{8,24},{16,0},{24,8},{1,17},{9,25},{17,1},{25,9},{2,18},{10... | collective-permute-start | bytes 24584 | tf_op jit(solution)/shard_map/ppermute | solution.py:32
  38.8 6.8 %collective-permute-start.8 = (bf16[2,2048]{1,0:T(2,128)(2,1)S(1)}, bf16[2,2048]{1,0:T(2,128)(2,1)S(1)}, u32[]{:S(2)}, u32[]{:S(2)}) collective-permute-start(bf16[2,2048]{1,0:T(2,128)(2,1)S(1)} %get-tuple-element.45.refs_1_.refs_0_), channel_id=1, source_target_pairs={{0,24},{8,16},{16,8},{24,0},{1,25},{9,17},{17,9},{25,1},{2,26},{10... | collective-permute-start | bytes 24584 | tf_op jit(solution)/shard_map/ppermute | solution.py:32
  46.8 1.3 %collective-permute-start.9 = (f32[8,2048]{1,0:T(8,128)S(1)}, f32[8,2048]{1,0:T(8,128)S(1)}, u32[]{:S(2)}, u32[]{:S(2)}) collective-permute-start(f32[8,2048]{1,0:T(8,128)S(1)} %output_projection.1.left_ref._), channel_id=1, source_target_pairs={{0,1},{1,0},{2,3},{3,2},{4,5},{5,4},{6,7},{7,6},{8,9},{9,8},{10,11... | collective-permute-start | bytes 196616 | tf_op jit(solution)/shard_map/ppermute | solution.py:32
  48.0 4.9 %collective-permute-start.10 = (f32[8,2048]{1,0:T(8,128)S(1)}, f32[8,2048]{1,0:T(8,128)S(1)}, u32[]{:S(2)}, u32[]{:S(2)}) collective-permute-start(f32[8,2048]{1,0:T(8,128)S(1)} %add.5.refs_1_.left_ref), channel_id=1, source_target_pairs={{0,2},{1,3},{2,0},{3,1},{4,6},{5,7},{6,4},{7,5},{8,10},{9,11},{10,... | collective-permute-start | bytes 196616 | tf_op jit(solution)/shard_map/ppermute | solution.py:32
  52.9 1.6 %copy-start.7 = (bf16[2048]{0:T(1024)(128)(2,1)S(1)}, bf16[2048]{0:T(1024)(128)(2,1)}, u32[]{:S(2)}) copy-start(bf16[2048]{0:T(1024)(128)(2,1)} %param.34) | copy-start | bytes 12292
  52.9 4.4 %collective-permute-start.11 = (f32[8,2048]{1,0:T(8,128)S(1)}, f32[8,2048]{1,0:T(8,128)S(1)}, u32[]{:S(2)}, u32[]{:S(2)}) collective-permute-start(f32[8,2048]{1,0:T(8,128)S(1)} %add.6.refs_1_.left_ref), channel_id=1, source_target_pairs={{0,4},{1,5},{2,6},{3,7},{4,0},{5,1},{6,2},{7,3},{8,12},{9,13},{10,... | collective-permute-start | bytes 196616 | tf_op jit(solution)/shard_map/ppermute | solution.py:32
  57.3 0.8 copy-start
  58.1 14.8 %copy-start.1 = (s32[2,8192]{1,0:T(2,128)S(1)}, s32[2,8192]{1,0:T(2,128)}, u32[]{:S(2)}) copy-start(s32[2,8192]{1,0:T(2,128)} %refs_4_.3) | copy-start | bytes 196612
  58.1 24.3 %copy-start.11 = (s32[2]{0:T(128)S(1)}, s32[2]{0:T(128)}, u32[]{:S(2)}) copy-start(s32[2]{0:T(128)} %param.37) | copy-start | bytes 28
  64.4 7.3 %collective-permute-start.12 = (f32[2,8320]{1,0:T(2,128)S(1)}, f32[2,8320]{1,0:T(2,128)S(1)}, u32[]{:S(2)}, u32[]{:S(2)}) collective-permute-start(f32[2,8320]{1,0:T(2,128)S(1)} %get-tuple-element.57), channel_id=1, source_target_pairs={{0,8},{8,0},{16,24},{24,16},{1,9},{9,1},{17,25},{25,17},{2,10},{10... | collective-permute-start | bytes 199688 | tf_op jit(solution)/shard_map/ppermute | solution.py:32
  64.5 7.4 %collective-permute-start.13 = (f32[2,8320]{1,0:T(2,128)S(1)}, f32[2,8320]{1,0:T(2,128)S(1)}, u32[]{:S(2)}, u32[]{:S(2)}) collective-permute-start(f32[2,8320]{1,0:T(2,128)S(1)} %get-tuple-element.56), channel_id=1, source_target_pairs={{0,16},{8,24},{16,0},{24,8},{1,17},{9,25},{17,1},{25,9},{2,18},{10... | collective-permute-start | bytes 199688 | tf_op jit(solution)/shard_map/ppermute | solution.py:32
  66.7 6.1 %collective-permute-start.14 = (f32[2,8320]{1,0:T(2,128)S(1)}, f32[2,8320]{1,0:T(2,128)S(1)}, u32[]{:S(2)}, u32[]{:S(2)}) collective-permute-start(f32[2,8320]{1,0:T(2,128)S(1)} %get-tuple-element.55), channel_id=1, source_target_pairs={{0,24},{8,16},{16,8},{24,0},{1,25},{9,17},{17,9},{25,1},{2,26},{10... | collective-permute-start | bytes 199688 | tf_op jit(solution)/shard_map/ppermute | solution.py:32

commit v2 on v1

v2 whole, which is shorter than its diff:
```python
import functools

import jax
import jax.numpy as jnp
from jax import lax
from jax.experimental import pallas as pl
from jax.experimental.pallas import tpu as pltpu
from jax.sharding import PartitionSpec as P

D = 8192
HEADS = 256
HEAD_DIM = 64
GROUPS = 8
FIXED_BITS = 15.0

EPSILON = 1e-05
INVERSE_HEAT = 1.25
FIXED_POINT = 65536.0
NEG_LARGE = -1e30

MIB = 2**20
LANES = 128
TILE = 256
SHARES = (3, 12, 18, 24)
EARLY_INPUT = 6
VMEM = pl.BlockSpec(memory_space=pltpu.VMEM)
ANY = pl.BlockSpec(memory_space=pl.ANY)
f32 = jnp.float32
bf16 = jnp.bfloat16


def xor_permute(values, axis, distance):
    size = lax.axis_size(axis)
    return lax.ppermute(values, axis, [(at, at ^ distance) for at in range(size)])


def tree_sum(values):
    values = list(values)
    while len(values) > 1:
        values = [a + b for a, b in zip(values[0::2], values[1::2])]
    return values[0]


def split(values):
    high = values.astype(bf16)
    return high, (values - high.astype(f32)).astype(bf16)


def split_three(values):
    high, rest = split(values)
    middle = values - high.astype(f32)
    return high, rest, (middle - rest.astype(f32)).astype(bf16)


def silu(values):
    return values / (1.0 + jnp.exp(-values))


def dot(left, right):
    return jnp.dot(left, right, preferred_element_type=f32)


def dot_transposed(left, right):
    return lax.dot_general(left, right, (((1,), (1,)), ((), ())), preferred_element_type=f32)


def times_gain(values, gain_ref):
    return jnp.concatenate(
        [
            values[:, at * LANES : (at + 1) * LANES] * gain_ref[at : at + 1].astype(f32)
            for at in range(gain_ref.shape[0])
        ],
        axis=1,
    )


def beside_copies(body):
    pl.when(lax.axis_index("row") >= 0)(body)


def in_hbm(values):
    return pltpu.with_memory_space_constraint(values, pltpu.HBM)


def call(kernel, outs, operands, specs, scratch=(), limit=4, cost=0, out_specs=None, name=None):
    return pl.pallas_call(
        kernel,
        out_shape=outs,
        in_specs=specs,
        out_specs=out_specs if out_specs is not None else jax.tree.map(lambda _: VMEM, outs),
        scratch_shapes=list(scratch),
        compiler_params=pltpu.CompilerParams(vmem_limit_bytes=limit * MIB),
        cost_estimate=pl.CostEstimate(flops=1000, bytes_accessed=cost, transcendentals=0),
        name=name,
    )(*operands)


def shape(dims, dtype=f32):
    return jax.ShapeDtypeStruct(tuple(dims), dtype)


def group_kernel(keep, *refs):
    sources = refs[: keep + 3]
    weight_hbm, state_hbm, taps_hbm = sources[keep:]
    kept = refs[keep + 3 : 2 * keep + 3]
    part_ref, squares_ref, sent_ref, order, weight_ref, state_ref, taps_ref, stack, sems = refs[2 * keep + 3 :]
    places = list(kept) + [weight_ref, state_ref, taps_ref]
    copies = [
        pltpu.make_async_copy(source, place, sems.at[at])
        for at, (source, place) in enumerate(zip(sources, places))
    ]
    for copy in copies:
        copy.start()

    @beside_copies
    def _():
        regroup_matrix(order)
        stack[...] = jnp.zeros_like(stack)

    hidden_ref, gain_ref = kept[:2]
    rows = hidden_ref.shape[0]
    columns = weight_ref.shape[1]
    entries = columns // GROUPS
    devices = sent_ref.shape[0]
    for copy in copies:
        copy.wait()
    wide = hidden_ref[...].astype(f32)
    squares_ref[...] = jnp.broadcast_to(jnp.sum(wide * wide, axis=1, keepdims=True), squares_ref.shape)
    high, low = split(times_gain(wide, gain_ref))
    part = dot(jnp.concatenate([high, low], axis=0), weight_ref[...])
    part = part[:rows] + part[rows:]
    part_ref[...] = part
    part_high, part_low = split(part)
    stack[:rows] = part_high.astype(f32)
    stack[rows : 2 * rows] = part_low.astype(f32)
    for at in range(3):
        here = 2 * rows + at * state_ref.shape[1]
        stack[here : here + state_ref.shape[1]] = state_ref[at].astype(f32)
    tail = sent_ref.shape[1] - rows
    stack[2 * rows + tail : 2 * rows + tail + taps_ref.shape[0]] = taps_ref[...].astype(f32)
    grouped = dot(stack[...].astype(bf16), order[...])
    for device in range(devices):
        group = device // (devices // GROUPS)
        here = grouped[:, group * entries : (group + 1) * entries].astype(bf16)
        sent_ref[device, :rows, :entries] = here[:rows]
        sent_ref[device, :rows, entries:] = here[rows : 2 * rows]
        sent_ref[device, rows:, :entries] = here[2 * rows : 2 * rows + tail]
        sent_ref[device, rows:, entries:] = here[2 * rows + tail :]


def input_tile(weight_ref, at):
    depth, _, width = weight_ref.shape
    return weight_ref.reshape(2 * depth, width).at[:, pl.ds(at * LANES, LANES)]


def tile_moves(weight_ref, start, target, parts):
    size = target.shape[1] // parts
    return [
        (input_tile(weight_ref, start + tile).at[pl.ds(at * size, size)], target.at[tile, pl.ds(at * size, size)])
        for tile in range(target.shape[0])
        for at in range(parts)
    ]


def input_kernel(pieces, count, *refs):
    square_refs = refs[:pieces]
    hidden_ref, gain_ref, step_ref = refs[pieces : pieces + 3]
    tiles = list(refs[pieces + 3 : pieces + 3 + count])
    weight_ref, out_ref, small_ref, left, rest, sems = refs[pieces + 3 + count :]
    depth, _, width = weight_ref.shape
    rows = hidden_ref.shape[0]
    held = 2 * count
    parts = sems.shape[0] // rest.shape[0]
    copies = [
        pltpu.make_async_copy(source, place, sems.at[at])
        for at, (source, place) in enumerate(tile_moves(weight_ref, held, rest, parts))
    ]
    for copy in copies:
        copy.start()
    def project(first, pair):
        out_ref[:, first * LANES : (first + 2) * LANES] = dot(left[...], jnp.concatenate(pair, axis=1))

    @beside_copies
    def _():
        squares = tree_sum([ref[...] for ref in square_refs])[:, 0:1]
        scale = lax.rsqrt(squares / D + EPSILON)
        normed = times_gain(hidden_ref[...].astype(f32) * scale, gain_ref).astype(bf16).astype(f32)
        step = dot_transposed(normed.astype(bf16), step_ref[...])
        small_ref[...] = jnp.zeros_like(small_ref)
        small_ref[:, : step.shape[1]] = step
        small_ref[:, LANES:] = jnp.broadcast_to(scale, (rows, LANES))
        source = lax.broadcasted_iota(jnp.int32, (LANES, 4 * LANES), 0)
        target = lax.broadcasted_iota(jnp.int32, (LANES, 4 * LANES), 1)
        spread = 2 * source + target // (2 * LANES) == target % (2 * LANES)
        blocks = jnp.concatenate(
            [normed[:, block * LANES : (block + 1) * LANES] for block in range(depth // LANES)], axis=0
        )
        wide = dot(blocks.astype(bf16), spread.astype(f32).astype(bf16))
        for block in range(depth // LANES):
            here = wide[block * rows : (block + 1) * rows]
            left[:, 2 * block * LANES : 2 * (block + 1) * LANES] = jnp.concatenate(
                [here[:, : 2 * LANES], here[:, 2 * LANES :]], axis=0
            ).astype(bf16)
        for first in range(0, held, 2):
            project(first, [tiles[first // 2][0], tiles[first // 2][1]])

    for first in range(held, width // LANES, 2):
        for copy in copies[(first - held) * parts : (first - held + 2) * parts]:
            copy.wait()
        project(first, [rest[first - held], rest[first - held + 1]])


def pack_kernel(both_ref, part_ref, small_ref, arrived_ref, out_ref, held_ref):
    rows, width = small_ref.shape[0], both_ref.shape[1]
    blocks, mine, _ = out_ref.shape
    devices, _, double = arrived_ref.shape
    entries = double // 2
    columns = part_ref.shape[1]
    index = lax.axis_index("row")
    scale = small_ref[:, LANES : LANES + 1]
    arrived = arrived_ref[...].astype(f32)
    pair = (arrived[:, :rows, :entries] + arrived[:, :rows, entries:]) * scale[None]
    part = part_ref[...] * scale
    for device in range(devices):
        here = slice(device * entries, (device + 1) * entries)
        held_ref[0, :, here] = arrived[device, rows:, :entries]
        held_ref[1, :, here] = arrived[device, rows:, entries:]
    for block in range(blocks):
        place = block ^ index
        here = slice(block * mine, (block + 1) * mine)
        out_ref[place, :, :width] = both_ref[here]
        out_ref[place, :, width : 2 * width] = both_ref[rows + block * mine : rows + (block + 1) * mine]
        out_ref[place, :, 2 * width : 2 * width + columns] = part[here]
        out_ref[place, :, 2 * width + columns : 2 * width + columns + LANES] = small_ref[here, :LANES]
        start = 2 * width + columns + LANES
        for device in range(devices):
            out_ref[place, :, start + device * entries : start + (device + 1) * entries] = pair[device, here]


def state_kernel(finish, pieces, *refs):
    parts = [ref[...] for ref in refs[:pieces]]
    heads_ref, held_ref, inner_state_ref, inner_taps_ref = refs[pieces : pieces + 4]
    state_ref, gain_ref, spread_ref = refs[pieces + 4 : pieces + 7]
    mixer_ref, raw_ref, driven_ref, decay_ref, input_ref = refs[pieces + 7 :]
    total = tree_sum(parts)
    mine, width, state_width = state_ref.shape
    columns = raw_ref.shape[1] - width
    start = 2 * width + columns
    gate = total[:, :width]
    inner_raw = total[:, width : 2 * width].astype(bf16)
    raw_ref[...] = total[:, width:start]
    taps = inner_taps_ref[...].astype(f32)
    mixed = inner_raw.astype(f32) * taps[3:4]
    for at in range(3):
        mixed = mixed + inner_state_ref[at].astype(f32) * taps[at : at + 1]
    conv_inner = silu(mixed)
    taps = held_ref[1]
    mixed = total[:, start + LANES :].astype(bf16).astype(f32) * taps[3:4]
    for at in range(3):
        mixed = mixed + held_ref[0, at * mine : (at + 1) * mine] * taps[at : at + 1]
    pair = silu(mixed).astype(bf16)
    state_input = pair[:, :state_width].astype(f32)
    state_output = pair[:, state_width:]

    step_raw = total[:, start : start + LANES] + heads_ref[0:1]
    step_size = jnp.maximum(step_raw, 0.0) + jnp.log1p(jnp.exp(-jnp.abs(step_raw)))
    decay_rate = jnp.exp(-step_size * jnp.exp(heads_ref[1:2]))
    stacked = jnp.concatenate([step_size, decay_rate, heads_ref[2:3]], axis=0)
    parts = split_three(stacked)
    wide = (dot(parts[0], spread_ref[...]) + dot(parts[1], spread_ref[...])) + dot(parts[2], spread_ref[...])
    step_wide, decay_wide, skip_wide = wide[:mine], wide[mine : 2 * mine], wide[2 * mine :]
    driven = step_wide * conv_inner
    overlap = jnp.sum(state_input * state_output.astype(f32), axis=1, keepdims=True)
    old = jnp.concatenate(
        [dot_transposed(state_output, state_ref[row])[row : row + 1] for row in range(mine)], axis=0
    )
    readout = decay_wide * old + driven * overlap + skip_wide * conv_inner
    gated = readout * silu(gate)
    driven_ref[...] = driven
    decay_ref[...] = decay_wide
    input_ref[...] = state_input
    if finish:
        group_total = jnp.sum(gated * gated, axis=1, keepdims=True)
        group_scale = lax.rsqrt(group_total / (HEADS * HEAD_DIM // GROUPS) + EPSILON)
        gated = gated * group_scale * gain_ref[...].astype(f32)
    mixer_ref[...] = gated.astype(mixer_ref.dtype)


def update_kernel(
    driven_ref, decay_ref, input_ref, state_ref, raw_ref, inner_state_ref, group_state_ref, layer_ref, _, *refs
):
    out_ref, next_inner_ref, next_group_ref, layer_out_ref, new, sems = refs
    mine, width, _ = state_ref.shape
    block = min(512, width)
    blocks = width // block

    def copy(row, at):
        here = pl.ds(at * block, block)
        return pltpu.make_async_copy(new.at[row, here], out_ref.at[row, here], sems.at[row, at])

    for row in range(mine):
        both = jnp.concatenate(
            [driven_ref[row : row + 1], decay_ref[row : row + 1], jnp.zeros((6, width), f32)], axis=0
        )
        turned = jnp.transpose(both)
        for at in range(blocks):
            here = slice(at * block, (at + 1) * block)
            new[row, here] = (
                turned[here, 1:2] * state_ref[row, here].astype(f32)
                + turned[here, 0:1] * input_ref[row : row + 1]
            ).astype(bf16)
            copy(row, at).start()
    layer_out_ref[...] = layer_ref[...]
    next_inner_ref[0] = inner_state_ref[1]
    next_inner_ref[1] = inner_state_ref[2]
    next_inner_ref[2] = raw_ref[:, :width].astype(bf16)
    next_group_ref[0] = group_state_ref[1]
    next_group_ref[1] = group_state_ref[2]
    next_group_ref[2] = raw_ref[:, width:].astype(bf16)
    for row in range(mine):
        for at in range(blocks):
            copy(row, at).wait()


def output_kernel(pieces, *refs):
    weight_ref, _, out_ref, rows_held = refs[pieces:]
    index = lax.axis_index("row")
    for at in range(pieces):
        rows_held[index ^ at] = refs[at][...].astype(f32)
    left = jnp.concatenate([rows_held[at] for at in range(pieces)], axis=0).astype(bf16)
    width = weight_ref.shape[1]
    for column in range(0, width, TILE):
        out_ref[:, column : column + TILE] = dot(left, weight_ref[:, column : column + TILE])


def add_kernel(left_ref, right_ref, _, out_ref):
    out_ref[...] = left_ref[...] + right_ref[...]


def fixed_exponent(values):
    return jnp.floor(jnp.log2(jnp.maximum(values, 1e-30))) + 2.0


def lexicon_kernel(pieces, *refs):
    hidden_ref, gain_ref, mixed_ref = refs[:3]
    held_refs = refs[3 : 3 + pieces]
    weight_ref, layer_ref, out_ref, rest, left, scores, sems = refs[3 + pieces :]
    rows = hidden_ref.shape[0]
    blocks, mine, _ = out_ref.shape
    vocab = weight_ref.shape[1]
    done = vocab - rest.shape[1]
    part = rest.shape[1] // sems.shape[0]
    copies = [
        pltpu.make_async_copy(
            weight_ref.at[:, pl.ds(done + at * part, part)], rest.at[:, pl.ds(at * part, part)], sems.at[at]
        )
        for at in range(sems.shape[0])
    ]
    for copy in copies:
        copy.start()
    index = lax.axis_index("row")

    def put(value, column, width):
        value = value.astype(jnp.int32).astype(jnp.int16)
        for block in range(blocks):
            out_ref[block ^ index, :, column : column + width] = value[block * mine : (block + 1) * mine]

    def project(tile, column):
        term = dot(left[...], tile)
        scores[:, column : column + TILE] = term[:rows] + term[rows:]

    @beside_copies
    def _():
        layer = (hidden_ref[...].astype(f32) + mixed_ref[...]).astype(bf16)
        layer_ref[...] = layer
        wide = layer.astype(f32)
        squares = jnp.sum(wide * wide, axis=1, keepdims=True)
        high, low = split(wide * gain_ref[...].astype(f32))
        left[:rows] = high
        left[rows:] = low
        scores[:, vocab:] = jnp.broadcast_to(squares, (rows, LANES))
        base = 0
        for held in held_refs:
            for column in range(0, held.shape[1], TILE):
                project(held[:, column : column + TILE], base + column)
            base += held.shape[1]

    for column in range(0, rest.shape[1], TILE):
        if column % part == 0:
            copies[column // part].wait()
        project(rest[:, column : column + TILE], done + column)
    squares = scores[:, vocab : vocab + 1]
    peak = jnp.max(jnp.abs(scores[:, :vocab]), axis=1, keepdims=True)
    exponent = fixed_exponent(peak)
    square_exponent = fixed_exponent(squares)
    digits = squares * jnp.exp2(FIXED_BITS - square_exponent)
    digit = jnp.floor(digits)
    rest_digit = jnp.floor((digits - digit) * 2.0**FIXED_BITS)
    lane = lax.broadcasted_iota(jnp.int32, (rows, LANES), 1)
    tail = jnp.where(lane == 0, exponent, jnp.where(lane == 1, square_exponent, 0.0))
    put(jnp.where(lane == 2, digit, jnp.where(lane == 3, rest_digit, tail)), vocab, LANES)
    factor = jnp.exp2(FIXED_BITS - exponent)
    for column in range(0, vocab, 4 * TILE):
        put(jnp.round(scores[:, column : column + 4 * TILE] * factor), column, 4 * TILE)


def share_kernel(pieces, *refs):
    mask_ref, sent_ref, share_ref, top_ref, spread = refs[pieces:]
    mine, vocab = mask_ref.shape
    lines = sent_ref.shape[0] // mine
    part = vocab // lines
    terms, squares = [], []
    for ref in refs[:pieces]:
        tail = ref[:, vocab:].astype(jnp.int32).astype(f32)
        digits = tail[:, 2:3] + tail[:, 3:4] * 2.0**-FIXED_BITS
        squares.append(digits * jnp.exp2(tail[:, 1:2] - FIXED_BITS))
        terms.append(ref[:, :vocab].astype(jnp.int32).astype(f32) * jnp.exp2(tail[:, 0:1] - FIXED_BITS))
    scale = lax.rsqrt(tree_sum(squares) / D + EPSILON) * INVERSE_HEAT
    allowed = mask_ref[...] > 0
    logits = jnp.where(allowed, tree_sum(terms) * scale, NEG_LARGE)
    top = jnp.max(logits, axis=1, keepdims=True)
    share = jnp.where(allowed, jnp.exp(logits - top), 0.0)
    share_ref[...] = share
    top_ref[...] = jnp.broadcast_to(top, top_ref.shape)
    spread[...] = jnp.zeros_like(spread)
    parts = [value.astype(f32) for value in split_three(top)]
    for row in range(mine):
        for line in range(lines):
            here = slice(row * lines + line, row * lines + line + 1)
            spread[here, :part] = share[row : row + 1, line * part : (line + 1) * part]
        here = slice(row * lines, (row + 1) * lines)
        for at in range(3):
            spread[here, part + at : part + at + 1] = jnp.broadcast_to(parts[at][row : row + 1], (lines, 1))
    sent_ref[...] = spread[...].astype(bf16)


def weigh(relative, inverse_floor):
    return relative * jnp.clip(relative * inverse_floor - 1.0, 0.0, 1.0)


def probability_kernel(every_ref, share_ref, top_ref, floor_ref, out_ref):
    mine, vocab = share_ref.shape
    devices, lines, _ = every_ref.shape
    part = vocab * mine // lines
    inverse = FIXED_POINT / floor_ref[:, 0:1].astype(f32)
    tops = [
        jnp.sum(every_ref[device, :, part:].astype(f32), axis=1, keepdims=True)
        for device in range(devices)
    ]
    peak = functools.reduce(jnp.maximum, tops)
    per_row = lines // mine
    spread = jnp.concatenate(
        [jnp.broadcast_to(inverse[row : row + 1], (per_row, 1)) for row in range(mine)], axis=0
    )
    kept = jnp.zeros((lines, part), f32)
    for device in range(devices):
        relative = every_ref[device, :, :part].astype(f32) * jnp.exp(tops[device] - peak)
        kept = kept + weigh(relative, spread)
    kept = jnp.sum(kept, axis=1, keepdims=True)
    total = jnp.concatenate(
        [jnp.sum(kept[row * per_row : (row + 1) * per_row], axis=0, keepdims=True) for row in range(mine)],
        axis=0,
    )
    highest = jnp.concatenate([peak[row * per_row : row * per_row + 1] for row in range(mine)], axis=0)
    own = weigh(share_ref[...] * jnp.exp(top_ref[:, 0:1] - highest), inverse)
    out_ref[...] = (own / total).astype(bf16)


def regroup_matrix(ref):
    columns = ref.shape[0]
    source = lax.broadcasted_iota(jnp.int32, ref.shape, 0)
    target = lax.broadcasted_iota(jnp.int32, ref.shape, 1)
    order = (source % GROUPS) * (columns // GROUPS) + source // GROUPS == target
    ref[...] = order.astype(f32).astype(bf16)


def head_matrix(ref):
    head = lax.broadcasted_iota(jnp.int32, ref.shape, 0)
    channel = lax.broadcasted_iota(jnp.int32, ref.shape, 1)
    ref[...] = (channel // HEAD_DIM == head).astype(f32).astype(bf16)


def fetch_kernel(count, jobs, makes, *refs):
    sources = refs[:count]
    targets = refs[count + 1 : count + 1 + len(jobs)]
    made = refs[count + 1 + len(jobs) : -1]
    sems = refs[-1]
    copies = []
    for (at, kind, start), target in zip(jobs, targets):
        if kind == "whole":
            moves = [(sources[at], target)]
        elif kind == "columns":
            moves = [(sources[at].at[:, pl.ds(start, target.shape[1])], target)]
        else:
            moves = tile_moves(sources[at], start, target, 1)
        for source, place in moves:
            copies.append(pltpu.make_async_copy(source, place, sems.at[len(copies)]))
    for copy in copies:
        copy.start()
    if makes:

        @beside_copies
        def _():
            for make, ref in zip(makes, made):
                make(ref)

    for copy in copies:
        copy.wait()


def fetch(jobs, after, name, makes=()):
    jobs = [job for job in jobs if 0 not in job[3]]
    if not jobs and not makes:
        return []
    sources = []
    for source, *_ in jobs:
        if not any(source is other for other in sources):
            sources.append(source)
    plan = [
        ([source is other for other in sources].index(True), kind, start) for source, kind, start, _ in jobs
    ]
    outs = [pltpu.VMEM(dims, bf16) for *_, dims in jobs] + [pltpu.VMEM(dims, bf16) for _, dims in makes]
    size = sum(2 * functools.reduce(lambda a, b: a * b, dims) for *_, dims in jobs)
    return list(call(
        functools.partial(fetch_kernel, len(sources), plan, [make for make, _ in makes]),
        outs,
        [in_hbm(source) for source in sources] + [after],
        [ANY] * (len(sources) + 1),
        scratch=[pltpu.SemaphoreType.DMA((sum(dims[0] if kind == "tiles" else 1 for _, kind, _, dims in jobs),))],
        limit=2,
        cost=size,
        out_specs=[VMEM] * len(outs),
        name=name,
    ))


def local(
    hidden,
    norm_gain,
    input_weight,
    group_weight,
    step_weight,
    conv_inner_weight,
    conv_group_weight,
    conv_inner_state,
    conv_group_state,
    timestep_bias,
    decay_log,
    skip_gain,
    recurrent_state,
    mixer_gain,
    output_weight,
    final_gain,
    lexicon_matrix,
    token_mask,
    min_share,
):
    mine, heads_mine, head_width, state_width = recurrent_state.shape
    width = heads_mine * head_width
    rows, depth = hidden.shape
    vocab = lexicon_matrix.shape[1]
    row_devices = lax.axis_size("row")
    head_devices = lax.axis_size("head")
    group_devices = head_devices // GROUPS
    columns = group_weight.shape[1]
    entries = columns // GROUPS
    held_rows = -(-3 * mine // 8) * 8

    heads = jnp.pad(
        jnp.stack([timestep_bias, decay_log, skip_gain]), ((0, 0), (0, LANES - heads_mine))
    )
    inner_state = jnp.moveaxis(conv_inner_state, 1, 0)
    group_state = jnp.moveaxis(conv_group_state, 1, 0)
    state = recurrent_state.reshape(mine, width, state_width)
    floors = jnp.broadcast_to(min_share[:, None], (mine, LANES))

    kept_arrays = [hidden, norm_gain.reshape(-1, LANES), step_weight.T]
    used_arrays = [group_weight, group_state, conv_group_weight]
    hidden_held, gain_held, step_held, group_part, squares, sent = call(
        functools.partial(group_kernel, len(kept_arrays)),
        [pltpu.VMEM(array.shape, array.dtype) for array in kept_arrays]
        + [
            shape((rows, columns)),
            shape((rows, LANES)),
            shape((head_devices, rows + held_rows, 2 * entries), bf16),
        ],
        [in_hbm(array) for array in kept_arrays + used_arrays],
        [ANY] * 6,
        scratch=[pltpu.VMEM((columns, columns), bf16)]
        + [pltpu.VMEM(array.shape, array.dtype) for array in used_arrays]
        + [
            pltpu.VMEM((2 * rows + 2 * held_rows, columns), f32),
            pltpu.SemaphoreType.DMA((6,)),
        ],
        limit=6,
        cost=2 * MIB,
        out_specs=[VMEM] * 6,
        name="group_projection",
    )
    arrived = lax.all_to_all(sent, "head", 0, 0, tiled=True)
    all_squares = [squares] + [xor_permute(squares, "row", at) for at in range(1, row_devices)]
    pairs = width // TILE
    early = 2 * (pairs * EARLY_INPUT // 8)
    late = width // LANES - early
    input_held = fetch(
        [(input_weight, "tiles", at, (2, 2 * depth, LANES)) for at in range(0, early, 2)],
        arrived,
        "fetch_input",
    )
    parts = 1
    both, small = call(
        functools.partial(input_kernel, row_devices, len(input_held)),
        [shape((2 * rows, width)), shape((rows, 2 * LANES))],
        all_squares + [hidden_held, gain_held, step_held] + input_held + [in_hbm(input_weight)],
        [VMEM] * (row_devices + 3 + len(input_held)) + [ANY],
        scratch=[
            pltpu.VMEM((2 * rows, 2 * depth), bf16),
            pltpu.VMEM((late, 2 * depth, LANES), bf16),
            pltpu.SemaphoreType.DMA((late * parts,)),
        ],
        limit=late + 6,
        cost=2 * input_weight.size,
        name="input_projection",
    )
    tiles = vocab // TILE
    cuts = [tiles * share // 32 * TILE for share in SHARES]
    spans = [(start, end - start) for start, end in zip([0] + cuts[:-1], cuts)]
    fetched = []

    def lexicon_job(stage):
        start, size = spans[stage]
        return (lexicon_matrix, "columns", start, (depth, size))

    def fetch_lexicon(stage, after, name):
        if not spans[stage][1]:
            return after
        fetched.extend(fetch([lexicon_job(stage)], after, name))
        return fetched[-1]

    packed_width = 2 * width + columns + LANES + 2 * state_width
    packed, held = call(
        pack_kernel,
        [shape((row_devices, mine, packed_width)), shape((2, held_rows, 2 * state_width))],
        [both, group_part, small, arrived],
        [VMEM] * 4,
        name="pack_rows",
    )
    pieces = [packed[0]] + [xor_permute(packed[at], "row", at) for at in range(1, row_devices)]

    output_held, state_held, *fetched, spread = fetch(
        [
            (output_weight, "whole", 0, output_weight.shape),
            (state, "whole", 0, state.shape),
            lexicon_job(0),
        ],
        packed,
        "fetch_output",
        [(head_matrix, (LANES, width))],
    )
    finish = group_devices == 1
    mixer_in, raw, driven, decay, state_input = call(
        functools.partial(state_kernel, finish, row_devices),
        [
            shape((mine, width), bf16 if finish else f32),
            shape((mine, width + columns)),
            shape((mine, width)),
            shape((mine, width)),
            shape((mine, state_width)),
        ],
        pieces + [heads, held, inner_state, conv_inner_weight, state_held, mixer_gain[None], spread],
        [VMEM] * (row_devices + 7),
        limit=8,
        cost=2 * MIB,
        name="state_readout",
    )
    if not finish:
        members = [
            [group * group_devices + at for at in range(group_devices)] for group in range(GROUPS)
        ]
        group_total = lax.psum(jnp.sum(mixer_in * mixer_in, axis=1), "head", axis_index_groups=members)
        group_scale = lax.rsqrt(group_total / (HEADS * HEAD_DIM // GROUPS) + EPSILON)
        mixer_in = (mixer_in * group_scale[:, None] * mixer_gain.astype(f32)[None]).astype(bf16)

    mixer_rows = [mixer_in] + [xor_permute(mixer_in, "row", at) for at in range(1, row_devices)]
    ahead = fetch_lexicon(1, mixer_in, "fetch_lexicon_1")
    mixed = call(
        functools.partial(output_kernel, row_devices),
        shape((rows, depth)),
        mixer_rows + [output_held, ahead],
        [VMEM] * (row_devices + 1) + [ANY],
        scratch=[pltpu.VMEM((row_devices, mine, width), f32)],
        cost=4 * MIB,
        name="output_projection",
    )
    distance = 1
    while distance < head_devices:
        other = xor_permute(mixed, "head", distance)
        ahead = mixed
        for stage, place in ((2, head_devices // 4), (3, head_devices // 2)):
            if distance == place:
                ahead = fetch_lexicon(stage, mixed, f"fetch_lexicon_{stage}")
        mixed = call(
            add_kernel, shape((rows, depth)), [mixed, other, ahead], [VMEM, VMEM, ANY], name="add"
        )
        distance *= 2
    layer, scores = call(
        functools.partial(lexicon_kernel, len(fetched)),
        [pltpu.VMEM((rows, depth), bf16), shape((row_devices, mine, vocab + LANES), jnp.int16)],
        [hidden_held, final_gain[None], mixed] + fetched + [in_hbm(lexicon_matrix)],
        [VMEM] * (3 + len(fetched)) + [ANY],
        scratch=[
            pltpu.VMEM((depth, vocab - cuts[-1]), bf16),
            pltpu.VMEM((2 * rows, depth), bf16),
            pltpu.VMEM((rows, vocab + LANES), f32),
            pltpu.SemaphoreType.DMA((max(1, (vocab - cuts[-1]) // (2 * TILE)),)),
        ],
        limit=16,
        cost=16 * MIB,
        name="lexicon_projection",
    )
    score_rows = [scores[0]] + [xor_permute(scores[at], "row", at) for at in range(1, row_devices)]
    next_state, next_inner, next_group, layer_out = call(
        update_kernel,
        [
            shape((mine, width, state_width), bf16),
            shape((3, mine, width), bf16),
            shape((3, mine, columns), bf16),
            shape((rows, depth), bf16),
        ],
        [driven, decay, state_input, state_held, raw, inner_state, group_state, layer, scores],
        [VMEM] * 8 + [ANY],
        scratch=[
            pltpu.VMEM((mine, width, state_width), bf16),
            pltpu.SemaphoreType.DMA((mine, width // min(512, width))),
        ],
        limit=8,
        cost=4 * MIB,
        out_specs=[ANY, VMEM, VMEM, VMEM],
        name="state_update",
    )
    lines = 8 * mine
    shares, share, top = call(
        functools.partial(share_kernel, row_devices),
        [
            shape((lines, vocab * mine // lines + LANES), bf16),
            shape((mine, vocab)),
            shape((mine, LANES)),
        ],
        score_rows + [token_mask],
        [VMEM] * (row_devices + 1),
        scratch=[pltpu.VMEM((lines, vocab * mine // lines + LANES), f32)],
        name="share_of_peak",
    )
    every = lax.all_gather(shares, "head", axis=0)
    next_probs = call(
        probability_kernel,
        shape((mine, vocab), bf16),
        [every, share, top, floors],
        [VMEM] * 4,
        name="probabilities",
    )
    return (
        next_state.reshape(recurrent_state.shape),
        jnp.moveaxis(next_inner, 0, 1),
        jnp.moveaxis(next_group, 0, 1),
        layer_out,
        next_probs,
    )


def solution(mesh):
    in_specs = (
        P(None, "row"),
        P("row"),
        P("row", None, "head"),
        P("row", "head"),
        P("row", "head"),
        P(None, "head"),
        P(None, "head"),
        P("row", None, "head"),
        P("row", None, "head"),
        P("head"),
        P("head"),
        P("head"),
        P("row", "head", None, None),
        P("head"),
        P("head", "row"),
        P("row"),
        P("row", "head"),
        P("row", "head"),
        P("row"),
    )
    out_specs = (
        P("row", "head", None, None),
        P("row", None, "head"),
        P("row", None, "head"),
        P(None, "row"),
        P("row", "head"),
    )
    return jax.shard_map(local, mesh=mesh, in_specs=in_specs, out_specs=out_specs, check_vma=False)
```

time: 84 us -> 78.6 us (0.936)
  waiting for transfers between devices: 6.23 us -> 3.94 us
  local copies, waits for them, and re-layouts: 2.2 us -> 0.26 us
  Pallas kernels: 38.5 us -> 37.6 us
    ppermute x15, waiting for transfers between devices: 6.22 us -> 3.48 us  [xor_permute(): lax.ppermute(values, axis, [(at, at ^ distance) for at in range(size)])]
    ppermute x15, starting transfers between devices: 22.6 us -> 20.9 us  [xor_permute(): lax.ppermute(values, axis, [(at, at ^ distance) for at in range(size)])]
    all_to_all x1, starting transfers between devices: 3.72 us -> 5.18 us  [local(): arrived = lax.all_to_all(sent, 'head', 0, 0, tiled=True)]
    broadcast_in_dim x1 -> x0, local copies, waits for them, and re-layouts: 1.29 us -> none  [local(): norm_gain[None]]
    pallas_call x18 -> x17, Pallas kernels: 38.5 us -> 37.6 us  [call(): pl.pallas_call(kernel, out_shape=outs, in_specs=specs, out_specs=out_spec...]
  transfers between devices with their start and end apart: 16 -> 16, of which waited for: 5 -> 5; matrix products, arithmetic and copies ran while one was open for 0% -> 0% of each run, Pallas kernels for 31% -> 29%
where the time goes in v2:
time: 78.6 us; the launch traced here: 78.2 us
  Pallas kernels  37.6 us (48%)
  starting transfers between devices  26.1 us (33%)
  blocking collectives  9.37 us (12%)
  waiting for transfers between devices  3.94 us (5%)
  between operations  0.97 us (1%)
    pallas_call x17, Pallas kernels, call(): pl.pallas_call(kernel, out_shape=outs, in_specs=specs, out_specs=out_spec...  37.6 us
    ppermute x15, starting transfers between devices, xor_permute(): lax.ppermute(values, axis, [(at, at ^ distance) for at in range(size)])  20.9 us
    all_gather x1, blocking collectives, local(): every = lax.all_gather(shares, 'head', axis=0)  9.37 us
    all_to_all x1, starting transfers between devices, local(): arrived = lax.all_to_all(sent, 'head', 0, 0, tiled=True)  5.18 us
    ppermute x15, waiting for transfers between devices, xor_permute(): lax.ppermute(values, axis, [(at, at ^ distance) for at in range(size)])  3.48 us
  transfers between devices with their start and end apart: 16, of which 5 were waited for; matrix products, arithmetic and copies ran while one was open for 0% of the time, Pallas kernels for 29%

profile of v2, /device:TPU:0, one launch (start us, length us, event | category | flops | bytes accessed | tf_op | source)
XLA Modules:
  0.0 78.2 jit_solution(18419399135819261483)
XLA Ops:
  0.6 3.0 %group_projection.1 = (bf16[8,2048]{1,0:T(8,128)(2,1)S(1)}, bf16[16,128]{1,0:T(8,128)(2,1)S(1)}, bf16[32,2048]{1,0:T(8,128)(2,1)S(1)}, f32[8,512]{1,0:T(8,128)S(...) custom-call(bf16[8,2048]{1,0:T(8,128)(2,1)} %refs_0_.6, bf16[16,128]{1,0:T(8,128)(2,1)} %bitcast.35, ...), custom_call_target="tpu_custom_call" | custom-call | flops 1000 | bytes 2097152 | tf_op jit(solution)/shard_map/group_projection/pallas_call | solution.py:86
  3.7 5.2 %all-to-all-start = ((bf16[8,16,128]{2,1,0:T(8,128)(2,1)}), bf16[8,16,128]{2,1,0:T(8,128)(2,1)S(1)}, u32[]{:S(2)}, u32[]{:S(2)}) async-start(bf16[8,16,128]{2,1,0:T(8,128)(2,1)} %get-tuple-element.43), calls=%async_computation | async-start | bytes 65536 | tf_op jit(solution)/shard_map/all_to_all | solution.py:600
  8.8 1.6 %collective-permute-start = (f32[8,128]{1,0:T(8,128)S(1)}, f32[8,128]{1,0:T(8,128)S(1)}, u32[]{:S(2)}, u32[]{:S(2)}) collective-permute-start(f32[8,128]{1,0:T(8,128)S(1)} %get-tuple-element.39.refs_0_), channel_id=1, source_target_pairs={{0,8},{8,0},{16,24},{24,16},{1,9},{9,1},{17,25},{25,17},{2,10},{10... | collective-permute-start | bytes 12296 | tf_op jit(solution)/shard_map/ppermute | solution.py:34
  10.4 2.6 %collective-permute-start.1 = (f32[8,128]{1,0:T(8,128)S(1)}, f32[8,128]{1,0:T(8,128)S(1)}, u32[]{:S(2)}, u32[]{:S(2)}) collective-permute-start(f32[8,128]{1,0:T(8,128)S(1)} %get-tuple-element.39.refs_0_), channel_id=1, source_target_pairs={{0,16},{8,24},{16,0},{24,8},{1,17},{9,25},{17,1},{25,9},{2,18},{10... | collective-permute-start | bytes 12296 | tf_op jit(solution)/shard_map/ppermute | solution.py:34
  13.0 0.2 collective-permute-start.2
  13.2 0.5 all-to-all-done.refs_1_.arrived_ref
  13.7 4.9 %fetch_input.1 = (bf16[2,4096,128]{2,1,0:T(8,128)(2,1)S(1)}, bf16[2,4096,128]{2,1,0:T(8,128)(2,1)S(1)}, bf16[2,4096,128]{2,1,0:T(8,128)(2,1)S(1)}, bf16[2,4096,1...) custom-call(bf16[2048,2,2048]{2,1,0:T(2,128)(2,1)} %refs_13_.1, ...), custom_call_target="tpu_custom_call" | custom-call | flops 1000 | bytes 12582912 | tf_op jit(solution)/shard_map/fetch_input/pallas_call | solution.py:86
  18.6 0.0 collective-permute-done.refs_1_
  18.6 0.0 copy-start.6
  18.6 0.0 copy-start.7
  18.6 0.0 copy-start.8
  18.6 0.0 copy-start.4
  18.6 3.3 %input_projection.1 = (f32[16,2048]{1,0:T(8,128)S(1)}, f32[8,256]{1,0:T(8,128)S(1)}) custom-call(f32[8,128]{1,0:T(8,128)S(1)} %get-tuple-element.39.refs_0_, f32[8,128]{1,0:T(8,128)S(1)} %collective-permute-done.refs_1_, f32[8,128]{1,0:T(8,128)S(1)} %collective-permute-done.1.refs_2_, f32[8,128]{1,0:T(8,128)S(1)} %collective-permute-done.2.refs_3_, ...), custom_call_target="tpu_custom_call" | custom-call | flops 1000 | bytes 16777216 | tf_op jit(solution)/shard_map/input_projection/pallas_call | solution.py:86
  22.0 0.2 pack_rows.1
  22.2 1.6 %collective-permute-start.3 = (f32[2,5248]{1,0:T(2,128)S(1)}, f32[2,5248]{1,0:T(2,128)S(1)}, u32[]{:S(2)}, u32[]{:S(2)}) collective-permute-start(f32[2,5248]{1,0:T(2,128)S(1)} %get-tuple-element.75), channel_id=1, source_target_pairs={{0,8},{8,0},{16,24},{24,16},{1,9},{9,1},{17,25},{25,17},{2,10},{10... | collective-permute-start | bytes 125960 | tf_op jit(solution)/shard_map/ppermute | solution.py:34
  23.8 2.6 %collective-permute-start.4 = (f32[2,5248]{1,0:T(2,128)S(1)}, f32[2,5248]{1,0:T(2,128)S(1)}, u32[]{:S(2)}, u32[]{:S(2)}) collective-permute-start(f32[2,5248]{1,0:T(2,128)S(1)} %get-tuple-element.74), channel_id=1, source_target_pairs={{0,16},{8,24},{16,0},{24,8},{1,17},{9,25},{17,1},{25,9},{2,18},{10... | collective-permute-start | bytes 125960 | tf_op jit(solution)/shard_map/ppermute | solution.py:34
  26.4 0.2 collective-permute-start.5
  26.7 0.0 copy-start
  26.7 0.0 copy-start.3
  26.7 4.9 %fetch_output.1 = (bf16[2048,2048]{1,0:T(8,128)(2,1)S(1)}, bf16[2,2048,256]{2,1,0:T(8,128)(2,1)S(1)}, bf16[2048,768]{1,0:T(8,128)(2,1)S(1)}, bf16[128,2048]{1,0:T(8,128)(2,1)S(1)}) custom-call(bf16[2048,2048]{1,0:T(8,128)(2,1)} %refs_0_.8, bf16[2,2048,256]{2,1,0:T(8,128)(2,1)} %bitcast.33, bf16[2048,8192]{1,0:T(8,128)(2,1)} %refs_7_.3, ...), custom_call_target="tpu_custom_call" | custom-call | flops 1000 | bytes 13631488 | tf_op jit(solution)/shard_map/fetch_output/pallas_call | solution.py:86
  31.6 0.6 collective-permute-done.5.refs_3_
  32.2 1.0 %state_readout.1 = (bf16[2,2048]{1,0:T(2,128)(2,1)S(1)}, f32[2,2560]{1,0:T(2,128)S(1)}, f32[2,2048]{1,0:T(2,128)S(1)}, f32[2,2048]{1,0:T(2,128)S(1)}, f32[2,256]{1,0:T(2,128)S(1)}) custom-call(f32[2,5248]{1,0:T(2,128)S(1)} %get-tuple-element.76.refs_0_, f32[2,5248]{1,0:T(2,128)S(1)} %collective-permute-done.3.refs_1_, ...), custom_call_target="tpu_custom_call" | custom-call | flops 1000 | bytes 2097152 | tf_op jit(solution)/shard_map/state_readout/pallas_call | solution.py:86
  33.2 0.2 collective-permute-start.6
  33.4 3.5 %collective-permute-start.7 = (bf16[2,2048]{1,0:T(2,128)(2,1)S(1)}, bf16[2,2048]{1,0:T(2,128)(2,1)S(1)}, u32[]{:S(2)}, u32[]{:S(2)}) collective-permute-start(bf16[2,2048]{1,0:T(2,128)(2,1)S(1)} %get-tuple-element.61.refs_1_.refs_0_), channel_id=1, source_target_pairs={{0,16},{8,24},{16,0},{24,8},{1,17},{9,25},{17,1},{25,9},{2,18},{10... | collective-permute-start | bytes 24584 | tf_op jit(solution)/shard_map/ppermute | solution.py:34
  36.9 0.8 collective-permute-start.8
  37.7 3.7 %fetch_lexicon_1.1.refs_5_.refs_4_ = bf16[2048,2304]{1,0:T(8,128)(2,1)S(1)} custom-call(bf16[2048,8192]{1,0:T(8,128)(2,1)} %refs_7_.3, bf16[2,2048]{1,0:T(2,128)(2,1)S(1)} %get-tuple-element.61.refs_1_.refs_0_), custom_call_target="tpu_custom_call" | custom-call | flops 1000 | bytes 9437184 | tf_op jit(solution)/shard_map/fetch_lexicon_1/pallas_call | solution.py:86
  41.4 1.0 %collective-permute-done.8.refs_3_ = bf16[2,2048]{1,0:T(2,128)(2,1)S(1)} collective-permute-done((bf16[2,2048]{1,0:T(2,128)(2,1)S(1)}, bf16[2,2048]{1,0:T(2,128)(2,1)S(1)}, u32[]{:S(2)}, u32[]{:S(2)}) %collective-permute-start.8) | collective-permute-done | bytes 8224 | tf_op jit(solution)/shard_map/ppermute | solution.py:34
  42.4 1.2 %output_projection.1.left_ref._ = f32[8,2048]{1,0:T(8,128)S(1)} custom-call(bf16[2,2048]{1,0:T(2,128)(2,1)S(1)} %get-tuple-element.61.refs_1_.refs_0_, bf16[2,2048]{1,0:T(2,128)(2,1)S(1)} %collective-permute-done.6.refs_1_, bf16[2,2048]{1,0:T(2,128)(2,1)S(1)} %collective-permute-done.7.refs_2_, bf16[2,2048]{1,0:T(2,128)(2,1)S(1)} %collective-permute-done.8.refs_3_, ...), custom_call_target="tpu_custom_call" | custom-call | flops 1000 | bytes 4194304 | tf_op jit(solution)/shard_map/output_projection/pallas_call | solution.py:86
  43.6 1.3 %collective-permute-done.9.right_ref = f32[8,2048]{1,0:T(8,128)S(1)} collective-permute-done((f32[8,2048]{1,0:T(8,128)S(1)}, f32[8,2048]{1,0:T(8,128)S(1)}, u32[]{:S(2)}, u32[]{:S(2)}) %collective-permute-start.9) | collective-permute-done | bytes 65568 | tf_op jit(solution)/shard_map/ppermute | solution.py:34
  44.8 1.6 %collective-permute-start.10 = (f32[8,2048]{1,0:T(8,128)S(1)}, f32[8,2048]{1,0:T(8,128)S(1)}, u32[]{:S(2)}, u32[]{:S(2)}) collective-permute-start(f32[8,2048]{1,0:T(8,128)S(1)} %add.5.refs_1_.left_ref), channel_id=1, source_target_pairs={{0,2},{1,3},{2,0},{3,1},{4,6},{5,7},{6,4},{7,5},{8,10},{9,11},{10,... | collective-permute-start | bytes 196616 | tf_op jit(solution)/shard_map/ppermute | solution.py:34
  46.5 2.8 %fetch_lexicon_2.1._.refs_5_ = bf16[2048,1536]{1,0:T(8,128)(2,1)S(1)} custom-call(bf16[2048,8192]{1,0:T(8,128)(2,1)} %refs_7_.3, f32[8,2048]{1,0:T(8,128)S(1)} %add.5.refs_1_.left_ref), custom_call_target="tpu_custom_call" | custom-call | flops 1000 | bytes 6291456 | tf_op jit(solution)/shard_map/fetch_lexicon_2/pallas_call | solution.py:86
  49.3 0.0 copy-start.5
  49.3 1.5 %collective-permute-start.11 = (f32[8,2048]{1,0:T(8,128)S(1)}, f32[8,2048]{1,0:T(8,128)S(1)}, u32[]{:S(2)}, u32[]{:S(2)}) collective-permute-start(f32[8,2048]{1,0:T(8,128)S(1)} %add.6.refs_1_.left_ref), channel_id=1, source_target_pairs={{0,4},{1,5},{2,6},{3,7},{4,0},{5,1},{6,2},{7,3},{8,12},{9,13},{10,... | collective-permute-start | bytes 196616 | tf_op jit(solution)/shard_map/ppermute | solution.py:34
  50.9 2.8 %fetch_lexicon_3.1._.refs_6_ = bf16[2048,1536]{1,0:T(8,128)(2,1)S(1)} custom-call(bf16[2048,8192]{1,0:T(8,128)(2,1)} %refs_7_.3, f32[8,2048]{1,0:T(8,128)S(1)} %add.6.refs_1_.left_ref), custom_call_target="tpu_custom_call" | custom-call | flops 1000 | bytes 6291456 | tf_op jit(solution)/shard_map/fetch_lexicon_3/pallas_call | solution.py:86
  53.7 0.0 copy-start.2
  53.7 5.1 %lexicon_projection.1 = (bf16[8,2048]{1,0:T(8,128)(2,1)S(1)}, s16[4,2,8320]{2,1,0:T(2,128)(2,1)S(1)}) custom-call(bf16[8,2048]{1,0:T(8,128)(2,1)S(1)} %get-tuple-element.40.refs_4_.refs_0_, bf16[1,2048]{1,0:T(2,128)(2,1)S(1)} %broadcast_in_dim.13.refs_1_, f32[8,2048]{1,0:T(8,128)S(1)} %add.7.refs_2_, bf16[2048,768]{1,0:T(8,128)(2,1)S(1)} %get-tuple-element.63.refs_3_, ...), custom_call_target="tpu_custom_call" | custom-call | flops 1000 | bytes 16777216 | tf_op jit(solution)/shard_map/lexicon_projection/pallas_call | solution.py:86
  58.8 0.0 copy-start.1
  58.8 0.0 copy-start.9
  58.9 0.1 slice_bitcast_fusion.4
  59.0 0.1 collective-permute-start.12
  59.0 2.7 %collective-permute-start.13 = (s16[2,8320]{1,0:T(2,128)(2,1)S(1)}, s16[2,8320]{1,0:T(2,128)(2,1)S(1)}, u32[]{:S(2)}, u32[]{:S(2)}) collective-permute-start(s16[2,8320]{1,0:T(2,128)(2,1)S(1)} %get-tuple-element.78), channel_id=1, source_target_pairs={{0,16},{8,24},{16,0},{24,8},{1,17},{9,25},{17,1},{25,9},{2,18},{10... | collective-permute-start | bytes 99848 | tf_op jit(solution)/shard_map/ppermute | solution.py:34
  61.7 1.7 %collective-permute-start.14 = (s16[2,8320]{1,0:T(2,128)(2,1)S(1)}, s16[2,8320]{1,0:T(2,128)(2,1)S(1)}, u32[]{:S(2)}, u32[]{:S(2)}) collective-permute-start(s16[2,8320]{1,0:T(2,128)(2,1)S(1)} %get-tuple-element.77), channel_id=1, source_target_pairs={{0,24},{8,16},{16,8},{24,0},{1,25},{9,17},{17,9},{25,1},{2,26},{10... | collective-permute-start | bytes 99848 | tf_op jit(solution)/shard_map/ppermute | solution.py:34
  63.4 3.3 %state_update.1 = (bf16[2,2048,256]{2,1,0:T(8,128)(2,1)}, bf16[3,2,2048]{2,1,0:T(2,128)(2,1)}, bf16[3,2,512]{2,1,0:T(2,128)(2,1)}, bf16[8,2048]{1,0:T(8,128)(2,1)}) custom-call(f32[2,2048]{1,0:T(2,128)S(1)} %get-tuple-element.57.driven_ref, f32[2,2048]{1,0:T(2,128)S(1)} %get-tuple-element.58.decay_ref, f32[2,256]{1,0:T(2,128)S(1)} %get-tuple-element.59.input_ref, ...), custom_call_target="tpu_custom_call" | custom-call | flops 1000 | bytes 4194304 | tf_op jit(solution)/shard_map/state_update/pallas_call | solution.py:86
  66.8 0.6 collective-permute-done.14.refs_3_
  67.4 0.3 share_of_peak.1
  67.7 9.4 %all-gather = bf16[128,1152]{1,0:T(8,128)(2,1)S(1)} all-gather(bf16[16,1152]{1,0:T(8,128)(2,1)S(1)} %get-tuple-element.70), channel_id=2, replica_groups=mesh['row'=4,'head'=8] {'head'}, dimensions={0}, use_global_device_ids=true | all-gather | bytes 331776 | tf_op jit(solution)/shard_map/all_gather | solution.py:754
  77.1 0.1 broadcast_in_dim.14.floor_ref
  77.2 1.1 %probabilities.1 = bf16[2,8192]{1,0:T(2,128)(2,1)} custom-call(bf16[8,16,1152]{2,1,0:T(8,128)(2,1)S(1)} %bitcast.28, f32[2,8192]{1,0:T(2,128)S(1)} %get-tuple-element.71.share_ref, f32[2,128]{1,0:T(2,128)S(1)} %get-tuple-element.72.top_ref, s32[2,128]{1,0:T(2,128)S(1)} %broadcast_in_dim.14.floor_ref), custom_call_target="tpu_custom_call" | custom-call | flops 1000 | tf_op jit(solution)/shard_map/probabilities/pallas_call | solution.py:86
  (28 shorter events, 0.1 us)
Async XLA Ops:
  3.7 10.0 %all-to-all-start = ((bf16[8,16,128]{2,1,0:T(8,128)(2,1)}), bf16[8,16,128]{2,1,0:T(8,128)(2,1)S(1)}, u32[]{:S(2)}, u32[]{:S(2)}) async-start(bf16[8,16,128]{2,1,0:T(8,128)(2,1)} %get-tuple-element.43), calls=%async_computation | async-start | bytes 65536 | tf_op jit(solution)/shard_map/all_to_all | solution.py:600
  8.8 9.7 %collective-permute-start = (f32[8,128]{1,0:T(8,128)S(1)}, f32[8,128]{1,0:T(8,128)S(1)}, u32[]{:S(2)}, u32[]{:S(2)}) collective-permute-start(f32[8,128]{1,0:T(8,128)S(1)} %get-tuple-element.39.refs_0_), channel_id=1, source_target_pairs={{0,8},{8,0},{16,24},{24,16},{1,9},{9,1},{17,25},{25,17},{2,10},{10... | collective-permute-start | bytes 12296 | tf_op jit(solution)/shard_map/ppermute | solution.py:34
  10.4 8.2 %collective-permute-start.1 = (f32[8,128]{1,0:T(8,128)S(1)}, f32[8,128]{1,0:T(8,128)S(1)}, u32[]{:S(2)}, u32[]{:S(2)}) collective-permute-start(f32[8,128]{1,0:T(8,128)S(1)} %get-tuple-element.39.refs_0_), channel_id=1, source_target_pairs={{0,16},{8,24},{16,0},{24,8},{1,17},{9,25},{17,1},{25,9},{2,18},{10... | collective-permute-start | bytes 12296 | tf_op jit(solution)/shard_map/ppermute | solution.py:34
  13.0 5.6 %collective-permute-start.2 = (f32[8,128]{1,0:T(8,128)S(1)}, f32[8,128]{1,0:T(8,128)S(1)}, u32[]{:S(2)}, u32[]{:S(2)}) collective-permute-start(f32[8,128]{1,0:T(8,128)S(1)} %get-tuple-element.39.refs_0_), channel_id=1, source_target_pairs={{0,24},{8,16},{16,8},{24,0},{1,25},{9,17},{17,9},{25,1},{2,26},{10... | collective-permute-start | bytes 12296 | tf_op jit(solution)/shard_map/ppermute | solution.py:34
  18.6 8.0 %copy-start.6 = (f32[32]{0:T(128)S(1)}, f32[32]{0:T(128)}, u32[]{:S(2)}) copy-start(f32[32]{0:T(128)} %param.30) | copy-start | bytes 388
  18.6 8.0 %copy-start.7 = (f32[32]{0:T(128)S(1)}, f32[32]{0:T(128)}, u32[]{:S(2)}) copy-start(f32[32]{0:T(128)} %param.29) | copy-start | bytes 388
  18.6 8.0 %copy-start.8 = (f32[32]{0:T(128)S(1)}, f32[32]{0:T(128)}, u32[]{:S(2)}) copy-start(f32[32]{0:T(128)} %param.28) | copy-start | bytes 388
  18.6 8.0 %copy-start.4 = (bf16[2048]{0:T(1024)(128)(2,1)S(1)}, bf16[2048]{0:T(1024)(128)(2,1)}, u32[]{:S(2)}) copy-start(bf16[2048]{0:T(1024)(128)(2,1)} %param.32) | copy-start | bytes 12292
  22.2 9.4 %collective-permute-start.3 = (f32[2,5248]{1,0:T(2,128)S(1)}, f32[2,5248]{1,0:T(2,128)S(1)}, u32[]{:S(2)}, u32[]{:S(2)}) collective-permute-start(f32[2,5248]{1,0:T(2,128)S(1)} %get-tuple-element.75), channel_id=1, source_target_pairs={{0,8},{8,0},{16,24},{24,16},{1,9},{9,1},{17,25},{25,17},{2,10},{10... | collective-permute-start | bytes 125960 | tf_op jit(solution)/shard_map/ppermute | solution.py:34
  23.8 7.8 %collective-permute-start.4 = (f32[2,5248]{1,0:T(2,128)S(1)}, f32[2,5248]{1,0:T(2,128)S(1)}, u32[]{:S(2)}, u32[]{:S(2)}) collective-permute-start(f32[2,5248]{1,0:T(2,128)S(1)} %get-tuple-element.74), channel_id=1, source_target_pairs={{0,16},{8,24},{16,0},{24,8},{1,17},{9,25},{17,1},{25,9},{2,18},{10... | collective-permute-start | bytes 125960 | tf_op jit(solution)/shard_map/ppermute | solution.py:34
  26.4 5.8 %collective-permute-start.5 = (f32[2,5248]{1,0:T(2,128)S(1)}, f32[2,5248]{1,0:T(2,128)S(1)}, u32[]{:S(2)}, u32[]{:S(2)}) collective-permute-start(f32[2,5248]{1,0:T(2,128)S(1)} %get-tuple-element.73), channel_id=1, source_target_pairs={{0,24},{8,16},{16,8},{24,0},{1,25},{9,17},{17,9},{25,1},{2,26},{10... | collective-permute-start | bytes 125960 | tf_op jit(solution)/shard_map/ppermute | solution.py:34
  26.7 5.5 %copy-start = (bf16[2,3,2048]{2,0,1:T(2,128)(2,1)S(1)}, bf16[2,3,2048]{2,0,1:T(2,128)(2,1)}, u32[]{:S(2)}) copy-start(bf16[2,3,2048]{2,0,1:T(2,128)(2,1)} %param.26) | copy-start | bytes 73732
  26.7 5.5 %copy-start.3 = (bf16[4,2048]{1,0:T(4,128)(2,1)S(1)}, bf16[4,2048]{1,0:T(4,128)(2,1)}, u32[]{:S(2)}) copy-start(bf16[4,2048]{1,0:T(4,128)(2,1)} %refs_7_.2) | copy-start | bytes 49156
  33.2 8.2 %collective-permute-start.6 = (bf16[2,2048]{1,0:T(2,128)(2,1)S(1)}, bf16[2,2048]{1,0:T(2,128)(2,1)S(1)}, u32[]{:S(2)}, u32[]{:S(2)}) collective-permute-start(bf16[2,2048]{1,0:T(2,128)(2,1)S(1)} %get-tuple-element.61.refs_1_.refs_0_), channel_id=1, source_target_pairs={{0,8},{8,0},{16,24},{24,16},{1,9},{9,1},{17,25},{25,17},{2,10},{10... | collective-permute-start | bytes 24584 | tf_op jit(solution)/shard_map/ppermute | solution.py:34
  33.4 8.0 %collective-permute-start.7 = (bf16[2,2048]{1,0:T(2,128)(2,1)S(1)}, bf16[2,2048]{1,0:T(2,128)(2,1)S(1)}, u32[]{:S(2)}, u32[]{:S(2)}) collective-permute-start(bf16[2,2048]{1,0:T(2,128)(2,1)S(1)} %get-tuple-element.61.refs_1_.refs_0_), channel_id=1, source_target_pairs={{0,16},{8,24},{16,0},{24,8},{1,17},{9,25},{17,1},{25,9},{2,18},{10... | collective-permute-start | bytes 24584 | tf_op jit(solution)/shard_map/ppermute | solution.py:34
  36.9 5.4 %collective-permute-start.8 = (bf16[2,2048]{1,0:T(2,128)(2,1)S(1)}, bf16[2,2048]{1,0:T(2,128)(2,1)S(1)}, u32[]{:S(2)}, u32[]{:S(2)}) collective-permute-start(bf16[2,2048]{1,0:T(2,128)(2,1)S(1)} %get-tuple-element.61.refs_1_.refs_0_), channel_id=1, source_target_pairs={{0,24},{8,16},{16,8},{24,0},{1,25},{9,17},{17,9},{25,1},{2,26},{10... | collective-permute-start | bytes 24584 | tf_op jit(solution)/shard_map/ppermute | solution.py:34
  43.5 1.3 %collective-permute-start.9 = (f32[8,2048]{1,0:T(8,128)S(1)}, f32[8,2048]{1,0:T(8,128)S(1)}, u32[]{:S(2)}, u32[]{:S(2)}) collective-permute-start(f32[8,2048]{1,0:T(8,128)S(1)} %output_projection.1.left_ref._), channel_id=1, source_target_pairs={{0,1},{1,0},{2,3},{3,2},{4,5},{5,4},{6,7},{7,6},{8,9},{9,8},{10,11... | collective-permute-start | bytes 196616 | tf_op jit(solution)/shard_map/ppermute | solution.py:34
  44.8 4.5 %collective-permute-start.10 = (f32[8,2048]{1,0:T(8,128)S(1)}, f32[8,2048]{1,0:T(8,128)S(1)}, u32[]{:S(2)}, u32[]{:S(2)}) collective-permute-start(f32[8,2048]{1,0:T(8,128)S(1)} %add.5.refs_1_.left_ref), channel_id=1, source_target_pairs={{0,2},{1,3},{2,0},{3,1},{4,6},{5,7},{6,4},{7,5},{8,10},{9,11},{10,... | collective-permute-start | bytes 196616 | tf_op jit(solution)/shard_map/ppermute | solution.py:34
  49.3 1.6 %copy-start.5 = (bf16[2048]{0:T(1024)(128)(2,1)S(1)}, bf16[2048]{0:T(1024)(128)(2,1)}, u32[]{:S(2)}) copy-start(bf16[2048]{0:T(1024)(128)(2,1)} %param.34) | copy-start | bytes 12292
  49.3 4.4 %collective-permute-start.11 = (f32[8,2048]{1,0:T(8,128)S(1)}, f32[8,2048]{1,0:T(8,128)S(1)}, u32[]{:S(2)}, u32[]{:S(2)}) collective-permute-start(f32[8,2048]{1,0:T(8,128)S(1)} %add.6.refs_1_.left_ref), channel_id=1, source_target_pairs={{0,4},{1,5},{2,6},{3,7},{4,0},{5,1},{6,2},{7,3},{8,12},{9,13},{10,... | collective-permute-start | bytes 196616 | tf_op jit(solution)/shard_map/ppermute | solution.py:34
  53.7 9.7 %copy-start.2 = (bf16[2,3,512]{2,0,1:T(2,128)(2,1)S(1)}, bf16[2,3,512]{2,0,1:T(2,128)(2,1)}, u32[]{:S(2)}) copy-start(bf16[2,3,512]{2,0,1:T(2,128)(2,1)} %param.27) | copy-start | bytes 18436
  58.8 8.6 %copy-start.1 = (s32[2,8192]{1,0:T(2,128)S(1)}, s32[2,8192]{1,0:T(2,128)}, u32[]{:S(2)}) copy-start(s32[2,8192]{1,0:T(2,128)} %refs_4_.1) | copy-start | bytes 196612
  58.8 18.2 %copy-start.9 = (s32[2]{0:T(128)S(1)}, s32[2]{0:T(128)}, u32[]{:S(2)}) copy-start(s32[2]{0:T(128)} %param.37) | copy-start | bytes 28
  59.0 7.8 %collective-permute-start.12 = (s16[2,8320]{1,0:T(2,128)(2,1)S(1)}, s16[2,8320]{1,0:T(2,128)(2,1)S(1)}, u32[]{:S(2)}, u32[]{:S(2)}) collective-permute-start(s16[2,8320]{1,0:T(2,128)(2,1)S(1)} %get-tuple-element.79), channel_id=1, source_target_pairs={{0,8},{8,0},{16,24},{24,16},{1,9},{9,1},{17,25},{25,17},{2,10},{10... | collective-permute-start | bytes 99848 | tf_op jit(solution)/shard_map/ppermute | solution.py:34
  59.0 7.7 %collective-permute-start.13 = (s16[2,8320]{1,0:T(2,128)(2,1)S(1)}, s16[2,8320]{1,0:T(2,128)(2,1)S(1)}, u32[]{:S(2)}, u32[]{:S(2)}) collective-permute-start(s16[2,8320]{1,0:T(2,128)(2,1)S(1)} %get-tuple-element.78), channel_id=1, source_target_pairs={{0,16},{8,24},{16,0},{24,8},{1,17},{9,25},{17,1},{25,9},{2,18},{10... | collective-permute-start | bytes 99848 | tf_op jit(solution)/shard_map/ppermute | solution.py:34
  61.7 5.7 %collective-permute-start.14 = (s16[2,8320]{1,0:T(2,128)(2,1)S(1)}, s16[2,8320]{1,0:T(2,128)(2,1)S(1)}, u32[]{:S(2)}, u32[]{:S(2)}) collective-permute-start(s16[2,8320]{1,0:T(2,128)(2,1)S(1)} %get-tuple-element.77), channel_id=1, source_target_pairs={{0,24},{8,16},{16,8},{24,0},{1,25},{9,17},{17,9},{25,1},{2,26},{10... | collective-permute-start | bytes 99848 | tf_op jit(solution)/shard_map/ppermute | solution.py:34

commit v3 on v2

--- a/solution.py
+++ b/solution.py
@@ -21,7 +21,7 @@
 MIB = 2**20
 LANES = 128
 TILE = 256
-SHARES = (3, 12, 18, 24)
+SHARES = (7, 15, 26)
 EARLY_INPUT = 6
 VMEM = pl.BlockSpec(memory_space=pltpu.VMEM)
 ANY = pl.BlockSpec(memory_space=pl.ANY)
@@ -32,6 +32,19 @@
 def xor_permute(values, axis, distance):
     size = lax.axis_size(axis)
     return lax.ppermute(values, axis, [(at, at ^ distance) for at in range(size)])
+
+
+def row_send(values, distance):
+    size = lax.axis_size("row")
+    return lax.ppermute(values, "row", [(at, (at + distance) % size) for at in range(size)])
+
+
+def row_place(block, index, count):
+    return lax.rem(block - index + count, count)
+
+
+def row_origin(index, distance, count):
+    return lax.rem(index - distance + count, count)
 
 
 def tree_sum(values):
@@ -133,19 +146,22 @@
     part_high, part_low = split(part)
     stack[:rows] = part_high.astype(f32)
     stack[rows : 2 * rows] = part_low.astype(f32)
-    for at in range(3):
-        here = 2 * rows + at * state_ref.shape[1]
-        stack[here : here + state_ref.shape[1]] = state_ref[at].astype(f32)
-    tail = sent_ref.shape[1] - rows
-    stack[2 * rows + tail : 2 * rows + tail + taps_ref.shape[0]] = taps_ref[...].astype(f32)
+    taps = taps_ref[...].astype(f32)
+    for side in range(2):
+        here = 2 * rows + 8 * side
+        for at in range(3):
+            stack[here + at : here + at + 1] = state_ref[at, side : side + 1].astype(f32)
+        for at in range(2):
+            stack[here + 3 + at : here + 4 + at] = taps[2 * at + side : 2 * at + side + 1]
     grouped = dot(stack[...].astype(bf16), order[...])
-    for device in range(devices):
-        group = device // (devices // GROUPS)
-        here = grouped[:, group * entries : (group + 1) * entries].astype(bf16)
-        sent_ref[device, :rows, :entries] = here[:rows]
-        sent_ref[device, :rows, entries:] = here[rows : 2 * rows]
-        sent_ref[device, rows:, :entries] = here[2 * rows : 2 * rows + tail]
-        sent_ref[device, rows:, entries:] = here[2 * rows + tail :]
+    each = devices // GROUPS
+    for group in range(GROUPS):
+        here = grouped[:, group * entries : (group + 1) * entries]
+        first = jnp.concatenate([here[:rows], here[2 * rows : 2 * rows + 8]], axis=0)
+        second = jnp.concatenate([here[rows : 2 * rows], here[2 * rows + 8 :]], axis=0)
+        value = jnp.concatenate([first, second], axis=1).astype(bf16)
+        for at in range(each):
+            sent_ref[group * each + at] = value
 
 
 def input_tile(weight_ref, at):
@@ -221,12 +237,17 @@
     arrived = arrived_ref[...].astype(f32)
     pair = (arrived[:, :rows, :entries] + arrived[:, :rows, entries:]) * scale[None]
     part = part_ref[...] * scale
+    held_ref[...] = jnp.zeros_like(held_ref)
     for device in range(devices):
         here = slice(device * entries, (device + 1) * entries)
-        held_ref[0, :, here] = arrived[device, rows:, :entries]
-        held_ref[1, :, here] = arrived[device, rows:, entries:]
+        for side in range(2):
+            lines = arrived[device, rows:, side * entries : (side + 1) * entries]
+            for at in range(3):
+                held_ref[0, at * mine + side : at * mine + side + 1, here] = lines[at : at + 1]
+            for at in range(2):
+                held_ref[1, 2 * at + side : 2 * at + side + 1, here] = lines[3 + at : 4 + at]
     for block in range(blocks):
-        place = block ^ index
+        place = row_place(block, index, blocks)
         here = slice(block * mine, (block + 1) * mine)
         out_ref[place, :, :width] = both_ref[here]
         out_ref[place, :, width : 2 * width] = both_ref[rows + block * mine : rows + (block + 1) * mine]
@@ -326,15 +347,15 @@
     weight_ref, _, out_ref, rows_held = refs[pieces:]
     index = lax.axis_index("row")
     for at in range(pieces):
-        rows_held[index ^ at] = refs[at][...].astype(f32)
+        rows_held[row_origin(index, at, pieces)] = refs[at][...].astype(f32)
     left = jnp.concatenate([rows_held[at] for at in range(pieces)], axis=0).astype(bf16)
     width = weight_ref.shape[1]
     for column in range(0, width, TILE):
         out_ref[:, column : column + TILE] = dot(left, weight_ref[:, column : column + TILE])
 
 
-def add_kernel(left_ref, right_ref, _, out_ref):
-    out_ref[...] = left_ref[...] + right_ref[...]
+def add_kernel(count, *refs):
+    refs[-1][...] = tree_sum([ref[...] for ref in refs[:count]])
 
 
 def fixed_exponent(values):
@@ -363,7 +384,7 @@
     def put(value, column, width):
         value = value.astype(jnp.int32).astype(jnp.int16)
         for block in range(blocks):
-            out_ref[block ^ index, :, column : column + width] = value[block * mine : (block + 1) * mine]
+            out_ref[row_place(block, index, blocks), :, column : column + width] = value[block * mine : (block + 1) * mine]
 
     def project(tile, column):
         term = dot(left[...], tile)
@@ -528,7 +549,7 @@
         [ANY] * (len(sources) + 1),
         scratch=[pltpu.SemaphoreType.DMA((sum(dims[0] if kind == "tiles" else 1 for _, kind, _, dims in jobs),))],
         limit=2,
-        cost=size,
+        cost=1000,
         out_specs=[VMEM] * len(outs),
         name=name,
     ))
@@ -564,7 +585,7 @@
     group_devices = head_devices // GROUPS
     columns = group_weight.shape[1]
     entries = columns // GROUPS
-    held_rows = -(-3 * mine // 8) * 8
+    held_rows = 8
 
     heads = jnp.pad(
         jnp.stack([timestep_bias, decay_log, skip_gain]), ((0, 0), (0, LANES - heads_mine))
@@ -598,7 +619,7 @@
         name="group_projection",
     )
     arrived = lax.all_to_all(sent, "head", 0, 0, tiled=True)
-    all_squares = [squares] + [xor_permute(squares, "row", at) for at in range(1, row_devices)]
+    all_squares = [squares] + [row_send(squares, at) for at in range(1, row_devices)]
     pairs = width // TILE
     early = 2 * (pairs * EARLY_INPUT // 8)
     late = width // LANES - early
@@ -643,18 +664,15 @@
         [shape((row_devices, mine, packed_width)), shape((2, held_rows, 2 * state_width))],
         [both, group_part, small, arrived],
         [VMEM] * 4,
+        cost=16 * MIB,
         name="pack_rows",
     )
-    pieces = [packed[0]] + [xor_permute(packed[at], "row", at) for at in range(1, row_devices)]
-
-    output_held, state_held, *fetched, spread = fetch(
-        [
-            (output_weight, "whole", 0, output_weight.shape),
-            (state, "whole", 0, state.shape),
-            lexicon_job(0),
-        ],
+    pieces = [packed[0]] + [row_send(packed[at], at) for at in range(1, row_devices)]
+
+    *fetched, spread = fetch(
+        [lexicon_job(0)],
         packed,
-        "fetch_output",
+        "fetch_lexicon_0",
         [(head_matrix, (LANES, width))],
     )
     finish = group_devices == 1
@@ -667,10 +685,10 @@
             shape((mine, width)),
             shape((mine, state_width)),
         ],
-        pieces + [heads, held, inner_state, conv_inner_weight, state_held, mixer_gain[None], spread],
+        pieces + [heads, held, inner_state, conv_inner_weight, state, mixer_gain[None], spread],
         [VMEM] * (row_devices + 7),
         limit=8,
-        cost=2 * MIB,
+        cost=1000,
         name="state_readout",
     )
     if not finish:
@@ -681,28 +699,35 @@
         group_scale = lax.rsqrt(group_total / (HEADS * HEAD_DIM // GROUPS) + EPSILON)
         mixer_in = (mixer_in * group_scale[:, None] * mixer_gain.astype(f32)[None]).astype(bf16)
 
-    mixer_rows = [mixer_in] + [xor_permute(mixer_in, "row", at) for at in range(1, row_devices)]
+    mixer_rows = [mixer_in] + [row_send(mixer_in, at) for at in range(1, row_devices)]
     ahead = fetch_lexicon(1, mixer_in, "fetch_lexicon_1")
     mixed = call(
         functools.partial(output_kernel, row_devices),
         shape((rows, depth)),
-        mixer_rows + [output_held, ahead],
+        mixer_rows + [output_weight, ahead],
         [VMEM] * (row_devices + 1) + [ANY],
         scratch=[pltpu.VMEM((row_devices, mine, width), f32)],
-        cost=4 * MIB,
+        cost=1000,
         name="output_projection",
     )
-    distance = 1
+    distance, stage = 1, 2
     while distance < head_devices:
-        other = xor_permute(mixed, "head", distance)
+        steps = [distance]
+        if distance > 1 and 4 * distance <= head_devices:
+            steps = [distance, 2 * distance, 3 * distance]
+        others = [xor_permute(mixed, "head", step) for step in steps]
         ahead = mixed
-        for stage, place in ((2, head_devices // 4), (3, head_devices // 2)):
-            if distance == place:
-                ahead = fetch_lexicon(stage, mixed, f"fetch_lexicon_{stage}")
+        if distance > 1 and stage < len(SHARES):
+            ahead = fetch_lexicon(stage, mixed, f"fetch_lexicon_{stage}")
+            stage += 1
         mixed = call(
-            add_kernel, shape((rows, depth)), [mixed, other, ahead], [VMEM, VMEM, ANY], name="add"
+            functools.partial(add_kernel, 1 + len(steps)),
+            shape((rows, depth)),
+            [mixed] + others + [ahead],
+            [VMEM] * (1 + len(steps)) + [ANY],
+            name="add",
         )
-        distance *= 2
+        distance *= 1 + len(steps)
     layer, scores = call(
         functools.partial(lexicon_kernel, len(fetched)),
         [pltpu.VMEM((rows, depth), bf16), shape((row_devices, mine, vocab + LANES), jnp.int16)],
@@ -718,7 +743,7 @@
         cost=16 * MIB,
         name="lexicon_projection",
     )
-    score_rows = [scores[0]] + [xor_permute(scores[at], "row", at) for at in range(1, row_devices)]
+    score_rows = [scores[0]] + [row_send(scores[at], at) for at in range(1, row_devices)]
     next_state, next_inner, next_group, layer_out = call(
         update_kernel,
         [
@@ -727,7 +752,7 @@
             shape((3, mine, columns), bf16),
             shape((rows, depth), bf16),
         ],
-        [driven, decay, state_input, state_held, raw, inner_state, group_state, layer, scores],
+        [driven, decay, state_input, state, raw, inner_state, group_state, layer, scores],
         [VMEM] * 8 + [ANY],
         scratch=[
             pltpu.VMEM((mine, width, state_width), bf16),

time: 78.6 us -> 74.5 us (0.948)
  Pallas kernels: 37.6 us -> 34.2 us
  waiting for transfers between devices: 3.94 us -> 2.06 us
  starting transfers between devices: 26.1 us -> 27.3 us
    ppermute x0 -> x12, starting transfers between devices: none -> 18.5 us  [row_send(): lax.ppermute(values, 'row', [(at, (at + distance) % size) for at in range...]
    ppermute x15 -> x4, starting transfers between devices: 20.9 us -> 3.63 us  [xor_permute(): lax.ppermute(values, axis, [(at, at ^ distance) for at in range(size)])]
    pallas_call x17 -> x15, Pallas kernels: 37.6 us -> 34.2 us  [call(): pl.pallas_call(kernel, out_shape=outs, in_specs=specs, out_specs=out_spec...]
    ppermute x15 -> x4, waiting for transfers between devices: 3.48 us -> 2.03 us  [xor_permute(): lax.ppermute(values, axis, [(at, at ^ distance) for at in range(size)])]
  transfers between devices with their start and end apart: 16 -> 17, of which waited for: 5 -> 2; matrix products, arithmetic and copies ran while one was open for 0% -> 0% of each run, Pallas kernels for 29% -> 26%
where the time goes in v3:
time: 74.5 us; the launch traced here: 74.2 us
  Pallas kernels  34.2 us (46%)
  starting transfers between devices  27.3 us (37%)
  blocking collectives  8.95 us (12%)
  waiting for transfers between devices  2.06 us (3%)
  between operations  1.01 us (1%)
    pallas_call x15, Pallas kernels, call(): pl.pallas_call(kernel, out_shape=outs, in_specs=specs, out_specs=out_spec...  34.2 us
    ppermute x12, starting transfers between devices, row_send(): lax.ppermute(values, 'row', [(at, (at + distance) % size) for at in range...  18.5 us
    all_gather x1, blocking collectives, local(): every = lax.all_gather(shares, 'head', axis=0)  8.95 us
    all_to_all x1, starting transfers between devices, local(): arrived = lax.all_to_all(sent, 'head', 0, 0, tiled=True)  5.18 us
    ppermute x4, starting transfers between devices, xor_permute(): lax.ppermute(values, axis, [(at, at ^ distance) for at in range(size)])  3.63 us
    ppermute x4, waiting for transfers between devices, xor_permute(): lax.ppermute(values, axis, [(at, at ^ distance) for at in range(size)])  2.03 us
  transfers between devices with their start and end apart: 17, of which 2 were waited for; matrix products, arithmetic and copies ran while one was open for 0% of the time, Pallas kernels for 26%

profile of v3, /device:TPU:0, one launch (start us, length us, event | category | flops | bytes accessed | tf_op | source)
XLA Modules:
  0.0 74.2 jit_solution(5281822531612188827)
XLA Ops:
  0.6 3.0 %group_projection.1 = (bf16[8,2048]{1,0:T(8,128)(2,1)S(1)}, bf16[16,128]{1,0:T(8,128)(2,1)S(1)}, bf16[32,2048]{1,0:T(8,128)(2,1)S(1)}, f32[8,512]{1,0:T(8,128)S(...) custom-call(bf16[8,2048]{1,0:T(8,128)(2,1)} %refs_0_.5, bf16[16,128]{1,0:T(8,128)(2,1)} %bitcast.38, ...), custom_call_target="tpu_custom_call" | custom-call | flops 1000 | bytes 2097152 | tf_op jit(solution)/shard_map/group_projection/pallas_call | solution.py:99
  3.7 5.2 %all-to-all-start = ((bf16[8,16,128]{2,1,0:T(8,128)(2,1)}), bf16[8,16,128]{2,1,0:T(8,128)(2,1)S(1)}, u32[]{:S(2)}, u32[]{:S(2)}) async-start(bf16[8,16,128]{2,1,0:T(8,128)(2,1)} %get-tuple-element.41), calls=%async_computation | async-start | bytes 65536 | tf_op jit(solution)/shard_map/all_to_all | solution.py:621
  8.8 1.6 %collective-permute-start = (f32[8,128]{1,0:T(8,128)S(1)}, f32[8,128]{1,0:T(8,128)S(1)}, u32[]{:S(2)}, u32[]{:S(2)}) collective-permute-start(f32[8,128]{1,0:T(8,128)S(1)} %get-tuple-element.37.refs_0_), channel_id=1, source_target_pairs={{0,8},{8,16},{16,24},{24,0},{1,9},{9,17},{17,25},{25,1},{2,10},{10... | collective-permute-start | bytes 12296 | tf_op jit(solution)/shard_map/ppermute | solution.py:39
  10.4 2.6 %collective-permute-start.1 = (f32[8,128]{1,0:T(8,128)S(1)}, f32[8,128]{1,0:T(8,128)S(1)}, u32[]{:S(2)}, u32[]{:S(2)}) collective-permute-start(f32[8,128]{1,0:T(8,128)S(1)} %get-tuple-element.37.refs_0_), channel_id=1, source_target_pairs={{0,16},{8,24},{16,0},{24,8},{1,17},{9,25},{17,1},{25,9},{2,18},{10... | collective-permute-start | bytes 12296 | tf_op jit(solution)/shard_map/ppermute | solution.py:39
  13.0 1.3 %collective-permute-start.2 = (f32[8,128]{1,0:T(8,128)S(1)}, f32[8,128]{1,0:T(8,128)S(1)}, u32[]{:S(2)}, u32[]{:S(2)}) collective-permute-start(f32[8,128]{1,0:T(8,128)S(1)} %get-tuple-element.37.refs_0_), channel_id=1, source_target_pairs={{0,24},{8,0},{16,8},{24,16},{1,25},{9,1},{17,9},{25,17},{2,26},{10... | collective-permute-start | bytes 12296 | tf_op jit(solution)/shard_map/ppermute | solution.py:39
  14.4 0.0 all-to-all-done.refs_1_.arrived_ref
  14.4 4.9 %fetch_input.1 = (bf16[2,4096,128]{2,1,0:T(8,128)(2,1)S(1)}, bf16[2,4096,128]{2,1,0:T(8,128)(2,1)S(1)}, bf16[2,4096,128]{2,1,0:T(8,128)(2,1)S(1)}, bf16[2,4096,1...) custom-call(bf16[2048,2,2048]{2,1,0:T(2,128)(2,1)} %refs_13_.1, ...), custom_call_target="tpu_custom_call" | custom-call | flops 1000 | bytes 1000 | tf_op jit(solution)/shard_map/fetch_input/pallas_call | solution.py:99
  19.3 0.0 copy-start.7
  19.3 0.0 copy-start.8
  19.3 0.0 copy-start.9
  19.3 0.0 copy-start.5
  19.3 3.3 %input_projection.1 = (f32[16,2048]{1,0:T(8,128)S(1)}, f32[8,256]{1,0:T(8,128)S(1)}) custom-call(f32[8,128]{1,0:T(8,128)S(1)} %get-tuple-element.37.refs_0_, f32[8,128]{1,0:T(8,128)S(1)} %collective-permute-done.refs_1_, f32[8,128]{1,0:T(8,128)S(1)} %collective-permute-done.1.refs_2_, f32[8,128]{1,0:T(8,128)S(1)} %collective-permute-done.2.refs_3_, ...), custom_call_target="tpu_custom_call" | custom-call | flops 1000 | bytes 16777216 | tf_op jit(solution)/shard_map/input_projection/pallas_call | solution.py:99
  22.7 0.2 pack_rows.1
  22.8 1.0 %collective-permute-start.3 = (f32[2,5248]{1,0:T(2,128)S(1)}, f32[2,5248]{1,0:T(2,128)S(1)}, u32[]{:S(2)}, u32[]{:S(2)}) collective-permute-start(f32[2,5248]{1,0:T(2,128)S(1)} %get-tuple-element.71), channel_id=1, source_target_pairs={{0,8},{8,16},{16,24},{24,0},{1,9},{9,17},{17,25},{25,1},{2,10},{10... | collective-permute-start | bytes 125960 | tf_op jit(solution)/shard_map/ppermute | solution.py:39
  23.8 2.6 %collective-permute-start.4 = (f32[2,5248]{1,0:T(2,128)S(1)}, f32[2,5248]{1,0:T(2,128)S(1)}, u32[]{:S(2)}, u32[]{:S(2)}) collective-permute-start(f32[2,5248]{1,0:T(2,128)S(1)} %get-tuple-element.70), channel_id=1, source_target_pairs={{0,16},{8,24},{16,0},{24,8},{1,17},{9,25},{17,1},{25,9},{2,18},{10... | collective-permute-start | bytes 125960 | tf_op jit(solution)/shard_map/ppermute | solution.py:39
  26.4 1.3 %collective-permute-start.5 = (f32[2,5248]{1,0:T(2,128)S(1)}, f32[2,5248]{1,0:T(2,128)S(1)}, u32[]{:S(2)}, u32[]{:S(2)}) collective-permute-start(f32[2,5248]{1,0:T(2,128)S(1)} %get-tuple-element.69), channel_id=1, source_target_pairs={{0,24},{8,0},{16,8},{24,16},{1,25},{9,1},{17,9},{25,17},{2,26},{10... | collective-permute-start | bytes 125960 | tf_op jit(solution)/shard_map/ppermute | solution.py:39
  27.8 0.0 copy-start
  27.8 0.0 copy-start.1
  27.8 0.0 copy-start.4
  27.8 3.2 %fetch_lexicon_0.1 = (bf16[2048,1792]{1,0:T(8,128)(2,1)S(1)}, bf16[128,2048]{1,0:T(8,128)(2,1)S(1)}) custom-call(bf16[2048,8192]{1,0:T(8,128)(2,1)} %refs_6_.1, f32[4,2,5248]{2,1,0:T(2,128)S(1)} %get-tuple-element.51.refs_1_), custom_call_target="tpu_custom_call" | custom-call | flops 1000 | bytes 1000 | tf_op jit(solution)/shard_map/fetch_lexicon_0/pallas_call | solution.py:99
  31.1 0.4 copy-done
  31.5 1.0 %state_readout.1 = (bf16[2,2048]{1,0:T(2,128)(2,1)S(1)}, f32[2,2560]{1,0:T(2,128)S(1)}, f32[2,2048]{1,0:T(2,128)S(1)}, f32[2,2048]{1,0:T(2,128)S(1)}, f32[2,256]{1,0:T(2,128)S(1)}) custom-call(f32[2,5248]{1,0:T(2,128)S(1)} %get-tuple-element.72.refs_0_, f32[2,5248]{1,0:T(2,128)S(1)} %collective-permute-done.3.refs_1_, ...), custom_call_target="tpu_custom_call" | custom-call | flops 1000 | bytes 1000 | tf_op jit(solution)/shard_map/state_readout/pallas_call | solution.py:99
  32.5 0.0 slice-start.1
  32.5 0.7 collective-permute-start.6
  33.2 2.0 %collective-permute-start.7 = (bf16[2,2048]{1,0:T(2,128)(2,1)S(1)}, bf16[2,2048]{1,0:T(2,128)(2,1)S(1)}, u32[]{:S(2)}, u32[]{:S(2)}) collective-permute-start(bf16[2,2048]{1,0:T(2,128)(2,1)S(1)} %get-tuple-element.58.refs_1_.refs_0_), channel_id=1, source_target_pairs={{0,16},{8,24},{16,0},{24,8},{1,17},{9,25},{17,1},{25,9},{2,18},{10... | collective-permute-start | bytes 24584 | tf_op jit(solution)/shard_map/ppermute | solution.py:39
  35.2 1.3 %collective-permute-start.8 = (bf16[2,2048]{1,0:T(2,128)(2,1)S(1)}, bf16[2,2048]{1,0:T(2,128)(2,1)S(1)}, u32[]{:S(2)}, u32[]{:S(2)}) collective-permute-start(bf16[2,2048]{1,0:T(2,128)(2,1)S(1)} %get-tuple-element.58.refs_1_.refs_0_), channel_id=1, source_target_pairs={{0,24},{8,0},{16,8},{24,16},{1,25},{9,1},{17,9},{25,17},{2,26},{10... | collective-permute-start | bytes 24584 | tf_op jit(solution)/shard_map/ppermute | solution.py:39
  36.5 3.4 %fetch_lexicon_1.1.refs_5_.refs_4_ = bf16[2048,2048]{1,0:T(8,128)(2,1)S(1)} custom-call(bf16[2048,8192]{1,0:T(8,128)(2,1)} %refs_6_.1, bf16[2,2048]{1,0:T(2,128)(2,1)S(1)} %get-tuple-element.58.refs_1_.refs_0_), custom_call_target="tpu_custom_call" | custom-call | flops 1000 | bytes 1000 | tf_op jit(solution)/shard_map/fetch_lexicon_1/pallas_call | solution.py:99
  39.9 0.0 copy-start.6
  40.0 1.2 %output_projection.1.refs_0_.refs_2_ = f32[8,2048]{1,0:T(8,128)S(1)} custom-call(bf16[2,2048]{1,0:T(2,128)(2,1)S(1)} %get-tuple-element.58.refs_1_.refs_0_, bf16[2,2048]{1,0:T(2,128)(2,1)S(1)} %collective-permute-done.6.refs_1_, bf16[2,2048]{1,0:T(2,128)(2,1)S(1)} %collective-permute-done.7.refs_2_, bf16[2,2048]{1,0:T(2,128)(2,1)S(1)} %collective-permute-done.8.refs_3_, ...), custom_call_target="tpu_custom_call" | custom-call | flops 1000 | bytes 1000 | tf_op jit(solution)/shard_map/output_projection/pallas_call | solution.py:99
  41.2 1.3 %collective-permute-done.9.refs_1_ = f32[8,2048]{1,0:T(8,128)S(1)} collective-permute-done((f32[8,2048]{1,0:T(8,128)S(1)}, f32[8,2048]{1,0:T(8,128)S(1)}, u32[]{:S(2)}, u32[]{:S(2)}) %collective-permute-start.9) | collective-permute-done | bytes 65568 | tf_op jit(solution)/shard_map/ppermute | solution.py:34
  42.4 2.1 %collective-permute-start.10 = (f32[8,2048]{1,0:T(8,128)S(1)}, f32[8,2048]{1,0:T(8,128)S(1)}, u32[]{:S(2)}, u32[]{:S(2)}) collective-permute-start(f32[8,2048]{1,0:T(8,128)S(1)} %add.4.refs_1_.refs_0_), channel_id=1, source_target_pairs={{0,2},{1,3},{2,0},{3,1},{4,6},{5,7},{6,4},{7,5},{8,10},{9,11},{10,... | collective-permute-start | bytes 196616 | tf_op jit(solution)/shard_map/ppermute | solution.py:34
  44.5 1.5 %collective-permute-start.11 = (f32[8,2048]{1,0:T(8,128)S(1)}, f32[8,2048]{1,0:T(8,128)S(1)}, u32[]{:S(2)}, u32[]{:S(2)}) collective-permute-start(f32[8,2048]{1,0:T(8,128)S(1)} %add.4.refs_1_.refs_0_), channel_id=1, source_target_pairs={{0,4},{1,5},{2,6},{3,7},{4,0},{5,1},{6,2},{7,3},{8,12},{9,13},{10,... | collective-permute-start | bytes 196616 | tf_op jit(solution)/shard_map/ppermute | solution.py:34
  46.0 0.1 collective-permute-start.12
  46.1 4.3 %fetch_lexicon_2.1.refs_4_.refs_5_ = bf16[2048,2816]{1,0:T(8,128)(2,1)S(1)} custom-call(bf16[2048,8192]{1,0:T(8,128)(2,1)} %refs_6_.1, f32[8,2048]{1,0:T(8,128)S(1)} %add.4.refs_1_.refs_0_), custom_call_target="tpu_custom_call" | custom-call | flops 1000 | bytes 1000 | tf_op jit(solution)/shard_map/fetch_lexicon_2/pallas_call | solution.py:99
  50.4 0.8 %collective-permute-done.12.refs_3_ = f32[8,2048]{1,0:T(8,128)S(1)} collective-permute-done((f32[8,2048]{1,0:T(8,128)S(1)}, f32[8,2048]{1,0:T(8,128)S(1)}, u32[]{:S(2)}, u32[]{:S(2)}) %collective-permute-start.12) | collective-permute-done | bytes 65568 | tf_op jit(solution)/shard_map/ppermute | solution.py:34
  51.2 0.0 copy-start.3
  51.2 5.0 %lexicon_projection.1 = (bf16[8,2048]{1,0:T(8,128)(2,1)S(1)}, s16[4,2,8320]{2,1,0:T(2,128)(2,1)S(1)}) custom-call(bf16[8,2048]{1,0:T(8,128)(2,1)S(1)} %get-tuple-element.38.refs_4_.refs_0_, bf16[1,2048]{1,0:T(2,128)(2,1)S(1)} %broadcast_in_dim.13.refs_1_, f32[8,2048]{1,0:T(8,128)S(1)} %add.5.refs_2_, bf16[2048,1792]{1,0:T(8,128)(2,1)S(1)} %get-tuple-element.59.refs_3_, ...), custom_call_target="tpu_custom_call" | custom-call | flops 1000 | bytes 16777216 | tf_op jit(solution)/shard_map/lexicon_projection/pallas_call | solution.py:99
  56.2 0.0 copy-start.2
  56.2 0.0 copy-start.10
  56.2 0.1 slice_bitcast_fusion.4
  56.3 0.1 collective-permute-start.13
  56.4 2.5 %collective-permute-start.14 = (s16[2,8320]{1,0:T(2,128)(2,1)S(1)}, s16[2,8320]{1,0:T(2,128)(2,1)S(1)}, u32[]{:S(2)}, u32[]{:S(2)}) collective-permute-start(s16[2,8320]{1,0:T(2,128)(2,1)S(1)} %get-tuple-element.74), channel_id=1, source_target_pairs={{0,16},{8,24},{16,0},{24,8},{1,17},{9,25},{17,1},{25,9},{2,18},{10... | collective-permute-start | bytes 99848 | tf_op jit(solution)/shard_map/ppermute | solution.py:39
  58.9 1.5 %collective-permute-start.15 = (s16[2,8320]{1,0:T(2,128)(2,1)S(1)}, s16[2,8320]{1,0:T(2,128)(2,1)S(1)}, u32[]{:S(2)}, u32[]{:S(2)}) collective-permute-start(s16[2,8320]{1,0:T(2,128)(2,1)S(1)} %get-tuple-element.73), channel_id=1, source_target_pairs={{0,24},{8,0},{16,8},{24,16},{1,25},{9,1},{17,9},{25,17},{2,26},{10... | collective-permute-start | bytes 99848 | tf_op jit(solution)/shard_map/ppermute | solution.py:39
  60.4 3.3 %state_update.1 = (bf16[2,2048,256]{2,1,0:T(8,128)(2,1)}, bf16[3,2,2048]{2,1,0:T(2,128)(2,1)}, bf16[3,2,512]{2,1,0:T(2,128)(2,1)}, bf16[8,2048]{1,0:T(8,128)(2,1)}) custom-call(f32[2,2048]{1,0:T(2,128)S(1)} %get-tuple-element.54.driven_ref, f32[2,2048]{1,0:T(2,128)S(1)} %get-tuple-element.55.decay_ref, f32[2,256]{1,0:T(2,128)S(1)} %get-tuple-element.56.input_ref, ...), custom_call_target="tpu_custom_call" | custom-call | flops 1000 | bytes 4194304 | tf_op jit(solution)/shard_map/state_update/pallas_call | solution.py:99
  63.8 0.3 share_of_peak.1
  64.1 8.9 %all-gather = bf16[128,1152]{1,0:T(8,128)(2,1)S(1)} all-gather(bf16[16,1152]{1,0:T(8,128)(2,1)S(1)} %get-tuple-element.66), channel_id=2, replica_groups=mesh['row'=4,'head'=8] {'head'}, dimensions={0}, use_global_device_ids=true | all-gather | bytes 331776 | tf_op jit(solution)/shard_map/all_gather | solution.py:779
  73.0 0.1 broadcast_in_dim.14.floor_ref
  73.1 1.1 %probabilities.1 = bf16[2,8192]{1,0:T(2,128)(2,1)} custom-call(bf16[8,16,1152]{2,1,0:T(8,128)(2,1)S(1)} %bitcast.32, f32[2,8192]{1,0:T(2,128)S(1)} %get-tuple-element.67.share_ref, f32[2,128]{1,0:T(2,128)S(1)} %get-tuple-element.68.top_ref, s32[2,128]{1,0:T(2,128)S(1)} %broadcast_in_dim.14.floor_ref), custom_call_target="tpu_custom_call" | custom-call | flops 1000 | tf_op jit(solution)/shard_map/probabilities/pallas_call | solution.py:99
  (35 shorter events, 0.1 us)
Async XLA Ops:
  3.7 10.7 %all-to-all-start = ((bf16[8,16,128]{2,1,0:T(8,128)(2,1)}), bf16[8,16,128]{2,1,0:T(8,128)(2,1)S(1)}, u32[]{:S(2)}, u32[]{:S(2)}) async-start(bf16[8,16,128]{2,1,0:T(8,128)(2,1)} %get-tuple-element.41), calls=%async_computation | async-start | bytes 65536 | tf_op jit(solution)/shard_map/all_to_all | solution.py:621
  8.8 10.4 %collective-permute-start = (f32[8,128]{1,0:T(8,128)S(1)}, f32[8,128]{1,0:T(8,128)S(1)}, u32[]{:S(2)}, u32[]{:S(2)}) collective-permute-start(f32[8,128]{1,0:T(8,128)S(1)} %get-tuple-element.37.refs_0_), channel_id=1, source_target_pairs={{0,8},{8,16},{16,24},{24,0},{1,9},{9,17},{17,25},{25,1},{2,10},{10... | collective-permute-start | bytes 12296 | tf_op jit(solution)/shard_map/ppermute | solution.py:39
  10.4 8.8 %collective-permute-start.1 = (f32[8,128]{1,0:T(8,128)S(1)}, f32[8,128]{1,0:T(8,128)S(1)}, u32[]{:S(2)}, u32[]{:S(2)}) collective-permute-start(f32[8,128]{1,0:T(8,128)S(1)} %get-tuple-element.37.refs_0_), channel_id=1, source_target_pairs={{0,16},{8,24},{16,0},{24,8},{1,17},{9,25},{17,1},{25,9},{2,18},{10... | collective-permute-start | bytes 12296 | tf_op jit(solution)/shard_map/ppermute | solution.py:39
  13.0 6.3 %collective-permute-start.2 = (f32[8,128]{1,0:T(8,128)S(1)}, f32[8,128]{1,0:T(8,128)S(1)}, u32[]{:S(2)}, u32[]{:S(2)}) collective-permute-start(f32[8,128]{1,0:T(8,128)S(1)} %get-tuple-element.37.refs_0_), channel_id=1, source_target_pairs={{0,24},{8,0},{16,8},{24,16},{1,25},{9,1},{17,9},{25,17},{2,26},{10... | collective-permute-start | bytes 12296 | tf_op jit(solution)/shard_map/ppermute | solution.py:39
  19.3 8.5 %copy-start.7 = (f32[32]{0:T(128)S(1)}, f32[32]{0:T(128)}, u32[]{:S(2)}) copy-start(f32[32]{0:T(128)} %param.30) | copy-start | bytes 388
  19.3 8.5 %copy-start.8 = (f32[32]{0:T(128)S(1)}, f32[32]{0:T(128)}, u32[]{:S(2)}) copy-start(f32[32]{0:T(128)} %param.29) | copy-start | bytes 388
  19.3 8.4 %copy-start.9 = (f32[32]{0:T(128)S(1)}, f32[32]{0:T(128)}, u32[]{:S(2)}) copy-start(f32[32]{0:T(128)} %param.28) | copy-start | bytes 388
  19.3 8.4 %copy-start.5 = (bf16[2048]{0:T(1024)(128)(2,1)S(1)}, bf16[2048]{0:T(1024)(128)(2,1)}, u32[]{:S(2)}) copy-start(bf16[2048]{0:T(1024)(128)(2,1)} %param.32) | copy-start | bytes 12292
  22.8 8.2 %collective-permute-start.3 = (f32[2,5248]{1,0:T(2,128)S(1)}, f32[2,5248]{1,0:T(2,128)S(1)}, u32[]{:S(2)}, u32[]{:S(2)}) collective-permute-start(f32[2,5248]{1,0:T(2,128)S(1)} %get-tuple-element.71), channel_id=1, source_target_pairs={{0,8},{8,16},{16,24},{24,0},{1,9},{9,17},{17,25},{25,1},{2,10},{10... | collective-permute-start | bytes 125960 | tf_op jit(solution)/shard_map/ppermute | solution.py:39
  23.8 7.3 %collective-permute-start.4 = (f32[2,5248]{1,0:T(2,128)S(1)}, f32[2,5248]{1,0:T(2,128)S(1)}, u32[]{:S(2)}, u32[]{:S(2)}) collective-permute-start(f32[2,5248]{1,0:T(2,128)S(1)} %get-tuple-element.70), channel_id=1, source_target_pairs={{0,16},{8,24},{16,0},{24,8},{1,17},{9,25},{17,1},{25,9},{2,18},{10... | collective-permute-start | bytes 125960 | tf_op jit(solution)/shard_map/ppermute | solution.py:39
  26.4 4.7 %collective-permute-start.5 = (f32[2,5248]{1,0:T(2,128)S(1)}, f32[2,5248]{1,0:T(2,128)S(1)}, u32[]{:S(2)}, u32[]{:S(2)}) collective-permute-start(f32[2,5248]{1,0:T(2,128)S(1)} %get-tuple-element.69), channel_id=1, source_target_pairs={{0,24},{8,0},{16,8},{24,16},{1,25},{9,1},{17,9},{25,17},{2,26},{10... | collective-permute-start | bytes 125960 | tf_op jit(solution)/shard_map/ppermute | solution.py:39
  27.8 3.7 %copy-start = (bf16[2,32,64,256]{3,2,1,0:T(8,128)(2,1)S(1)}, bf16[2,32,64,256]{3,2,1,0:T(8,128)(2,1)}, u32[]{:S(2)}) copy-start(bf16[2,32,64,256]{3,2,1,0:T(8,128)(2,1)} %param.31) | copy-start | bytes 6291460
  27.8 3.7 %copy-start.1 = (bf16[2,3,2048]{2,0,1:T(2,128)(2,1)S(1)}, bf16[2,3,2048]{2,0,1:T(2,128)(2,1)}, u32[]{:S(2)}) copy-start(bf16[2,3,2048]{2,0,1:T(2,128)(2,1)} %param.26) | copy-start | bytes 73732
  27.8 3.7 %copy-start.4 = (bf16[4,2048]{1,0:T(4,128)(2,1)S(1)}, bf16[4,2048]{1,0:T(4,128)(2,1)}, u32[]{:S(2)}) copy-start(bf16[4,2048]{1,0:T(4,128)(2,1)} %refs_7_.1) | copy-start | bytes 49156
  31.5 8.5 %slice-start = ((s8[8388608]{0:T(1024)(128)(4,1)}), s8[4194304]{0:T(1024)(128)(4,1)S(1)}, s32[]{:S(2)}) async-start(s8[8388608]{0:T(1024)(128)(4,1)} %bitcast.28), calls=%async_computation.1 | async-start | bytes 8388608
  32.5 7.5 %slice-start.1 = ((s8[8388608]{0:T(1024)(128)(4,1)}), s8[4194304]{0:T(1024)(128)(4,1)S(1)}, s32[]{:S(2)}) async-start(s8[8388608]{0:T(1024)(128)(4,1)} %bitcast.28), calls=%async_computation.2 | async-start | bytes 8388608
  32.5 7.4 %collective-permute-start.6 = (bf16[2,2048]{1,0:T(2,128)(2,1)S(1)}, bf16[2,2048]{1,0:T(2,128)(2,1)S(1)}, u32[]{:S(2)}, u32[]{:S(2)}) collective-permute-start(bf16[2,2048]{1,0:T(2,128)(2,1)S(1)} %get-tuple-element.58.refs_1_.refs_0_), channel_id=1, source_target_pairs={{0,8},{8,16},{16,24},{24,0},{1,9},{9,17},{17,25},{25,1},{2,10},{10... | collective-permute-start | bytes 24584 | tf_op jit(solution)/shard_map/ppermute | solution.py:39
  33.2 6.7 %collective-permute-start.7 = (bf16[2,2048]{1,0:T(2,128)(2,1)S(1)}, bf16[2,2048]{1,0:T(2,128)(2,1)S(1)}, u32[]{:S(2)}, u32[]{:S(2)}) collective-permute-start(bf16[2,2048]{1,0:T(2,128)(2,1)S(1)} %get-tuple-element.58.refs_1_.refs_0_), channel_id=1, source_target_pairs={{0,16},{8,24},{16,0},{24,8},{1,17},{9,25},{17,1},{25,9},{2,18},{10... | collective-permute-start | bytes 24584 | tf_op jit(solution)/shard_map/ppermute | solution.py:39
  35.2 4.7 %collective-permute-start.8 = (bf16[2,2048]{1,0:T(2,128)(2,1)S(1)}, bf16[2,2048]{1,0:T(2,128)(2,1)S(1)}, u32[]{:S(2)}, u32[]{:S(2)}) collective-permute-start(bf16[2,2048]{1,0:T(2,128)(2,1)S(1)} %get-tuple-element.58.refs_1_.refs_0_), channel_id=1, source_target_pairs={{0,24},{8,0},{16,8},{24,16},{1,25},{9,1},{17,9},{25,17},{2,26},{10... | collective-permute-start | bytes 24584 | tf_op jit(solution)/shard_map/ppermute | solution.py:39
  39.9 6.2 %copy-start.6 = (bf16[2048]{0:T(1024)(128)(2,1)S(1)}, bf16[2048]{0:T(1024)(128)(2,1)}, u32[]{:S(2)}) copy-start(bf16[2048]{0:T(1024)(128)(2,1)} %param.34) | copy-start | bytes 12292
  41.2 1.3 %collective-permute-start.9 = (f32[8,2048]{1,0:T(8,128)S(1)}, f32[8,2048]{1,0:T(8,128)S(1)}, u32[]{:S(2)}, u32[]{:S(2)}) collective-permute-start(f32[8,2048]{1,0:T(8,128)S(1)} %output_projection.1.refs_0_.refs_2_), channel_id=1, source_target_pairs={{0,1},{1,0},{2,3},{3,2},{4,5},{5,4},{6,7},{7,6},{8,9},{9,8},{10,11... | collective-permute-start | bytes 196616 | tf_op jit(solution)/shard_map/ppermute | solution.py:34
  42.4 7.9 %collective-permute-start.10 = (f32[8,2048]{1,0:T(8,128)S(1)}, f32[8,2048]{1,0:T(8,128)S(1)}, u32[]{:S(2)}, u32[]{:S(2)}) collective-permute-start(f32[8,2048]{1,0:T(8,128)S(1)} %add.4.refs_1_.refs_0_), channel_id=1, source_target_pairs={{0,2},{1,3},{2,0},{3,1},{4,6},{5,7},{6,4},{7,5},{8,10},{9,11},{10,... | collective-permute-start | bytes 196616 | tf_op jit(solution)/shard_map/ppermute | solution.py:34
  44.5 5.9 %collective-permute-start.11 = (f32[8,2048]{1,0:T(8,128)S(1)}, f32[8,2048]{1,0:T(8,128)S(1)}, u32[]{:S(2)}, u32[]{:S(2)}) collective-permute-start(f32[8,2048]{1,0:T(8,128)S(1)} %add.4.refs_1_.refs_0_), channel_id=1, source_target_pairs={{0,4},{1,5},{2,6},{3,7},{4,0},{5,1},{6,2},{7,3},{8,12},{9,13},{10,... | collective-permute-start | bytes 196616 | tf_op jit(solution)/shard_map/ppermute | solution.py:34
  46.0 5.2 %collective-permute-start.12 = (f32[8,2048]{1,0:T(8,128)S(1)}, f32[8,2048]{1,0:T(8,128)S(1)}, u32[]{:S(2)}, u32[]{:S(2)}) collective-permute-start(f32[8,2048]{1,0:T(8,128)S(1)} %add.4.refs_1_.refs_0_), channel_id=1, source_target_pairs={{0,6},{1,7},{2,4},{3,5},{4,2},{5,3},{6,0},{7,1},{8,14},{9,15},{10,... | collective-permute-start | bytes 196616 | tf_op jit(solution)/shard_map/ppermute | solution.py:34
  51.2 9.2 %copy-start.3 = (bf16[2,3,512]{2,0,1:T(2,128)(2,1)S(1)}, bf16[2,3,512]{2,0,1:T(2,128)(2,1)}, u32[]{:S(2)}) copy-start(bf16[2,3,512]{2,0,1:T(2,128)(2,1)} %param.27) | copy-start | bytes 18436
  56.2 7.6 %copy-start.2 = (s32[2,8192]{1,0:T(2,128)S(1)}, s32[2,8192]{1,0:T(2,128)}, u32[]{:S(2)}) copy-start(s32[2,8192]{1,0:T(2,128)} %refs_4_.3) | copy-start | bytes 196612
  56.2 16.8 %copy-start.10 = (s32[2]{0:T(128)S(1)}, s32[2]{0:T(128)}, u32[]{:S(2)}) copy-start(s32[2]{0:T(128)} %param.37) | copy-start | bytes 28
  56.3 7.4 %collective-permute-start.13 = (s16[2,8320]{1,0:T(2,128)(2,1)S(1)}, s16[2,8320]{1,0:T(2,128)(2,1)S(1)}, u32[]{:S(2)}, u32[]{:S(2)}) collective-permute-start(s16[2,8320]{1,0:T(2,128)(2,1)S(1)} %get-tuple-element.75), channel_id=1, source_target_pairs={{0,8},{8,16},{16,24},{24,0},{1,9},{9,17},{17,25},{25,1},{2,10},{10... | collective-permute-start | bytes 99848 | tf_op jit(solution)/shard_map/ppermute | solution.py:39
  56.4 7.4 %collective-permute-start.14 = (s16[2,8320]{1,0:T(2,128)(2,1)S(1)}, s16[2,8320]{1,0:T(2,128)(2,1)S(1)}, u32[]{:S(2)}, u32[]{:S(2)}) collective-permute-start(s16[2,8320]{1,0:T(2,128)(2,1)S(1)} %get-tuple-element.74), channel_id=1, source_target_pairs={{0,16},{8,24},{16,0},{24,8},{1,17},{9,25},{17,1},{25,9},{2,18},{10... | collective-permute-start | bytes 99848 | tf_op jit(solution)/shard_map/ppermute | solution.py:39
  58.9 4.8 %collective-permute-start.15 = (s16[2,8320]{1,0:T(2,128)(2,1)S(1)}, s16[2,8320]{1,0:T(2,128)(2,1)S(1)}, u32[]{:S(2)}, u32[]{:S(2)}) collective-permute-start(s16[2,8320]{1,0:T(2,128)(2,1)S(1)} %get-tuple-element.73), channel_id=1, source_target_pairs={{0,24},{8,0},{16,8},{24,16},{1,25},{9,1},{17,9},{25,17},{2,26},{10... | collective-permute-start | bytes 99848 | tf_op jit(solution)/shard_map/ppermute | solution.py:39

commit v4 on v3

--- a/solution.py
+++ b/solution.py
@@ -21,8 +21,8 @@
 MIB = 2**20
 LANES = 128
 TILE = 256
-SHARES = (7, 15, 26)
-EARLY_INPUT = 6
+SHARES = (4, 12, 22)
+EARLY_INPUT = 5
 VMEM = pl.BlockSpec(memory_space=pltpu.VMEM)
 ANY = pl.BlockSpec(memory_space=pl.ANY)
 f32 = jnp.float32
@@ -226,7 +226,11 @@
         project(first, [rest[first - held], rest[first - held + 1]])
 
 
-def pack_kernel(both_ref, part_ref, small_ref, arrived_ref, out_ref, held_ref):
+def fixed_exponent(values):
+    return jnp.floor(jnp.log2(jnp.maximum(values, 1e-30))) + 2.0
+
+
+def pack_kernel(both_ref, part_ref, small_ref, arrived_ref, out_ref, held_ref, joined):
     rows, width = small_ref.shape[0], both_ref.shape[1]
     blocks, mine, _ = out_ref.shape
     devices, _, double = arrived_ref.shape
@@ -246,44 +250,64 @@
                 held_ref[0, at * mine + side : at * mine + side + 1, here] = lines[at : at + 1]
             for at in range(2):
                 held_ref[1, 2 * at + side : 2 * at + side + 1, here] = lines[3 + at : 4 + at]
-    for block in range(blocks):
-        place = row_place(block, index, blocks)
-        here = slice(block * mine, (block + 1) * mine)
-        out_ref[place, :, :width] = both_ref[here]
-        out_ref[place, :, width : 2 * width] = both_ref[rows + block * mine : rows + (block + 1) * mine]
-        out_ref[place, :, 2 * width : 2 * width + columns] = part[here]
-        out_ref[place, :, 2 * width + columns : 2 * width + columns + LANES] = small_ref[here, :LANES]
-        start = 2 * width + columns + LANES
-        for device in range(devices):
-            out_ref[place, :, start + device * entries : start + (device + 1) * entries] = pair[device, here]
+    for device in range(devices):
+        joined[:, device * entries : (device + 1) * entries] = pair[device]
+    sections = [both_ref[:rows], both_ref[rows:], part, small_ref[:, :LANES], joined[...]]
+    lane = lax.broadcasted_iota(jnp.int32, (rows, LANES), 1)
+    tail = jnp.zeros((rows, LANES), f32)
+    start = 0
+
+    def put(value, start):
+        value = value.astype(jnp.int32).astype(jnp.int16)
+        for block in range(blocks):
+            here = value[block * mine : (block + 1) * mine]
+            out_ref[row_place(block, index, blocks), :, start : start + value.shape[1]] = here
+
+    for at, value in enumerate(sections):
+        exponent = fixed_exponent(jnp.max(jnp.abs(value), axis=1, keepdims=True))
+        tail = jnp.where(lane == at, exponent, tail)
+        put(jnp.round(value * jnp.exp2(FIXED_BITS - exponent)), start)
+        start += value.shape[1]
+    put(tail, start)
 
 
 def state_kernel(finish, pieces, *refs):
-    parts = [ref[...] for ref in refs[:pieces]]
     heads_ref, held_ref, inner_state_ref, inner_taps_ref = refs[pieces : pieces + 4]
     state_ref, gain_ref, spread_ref = refs[pieces + 4 : pieces + 7]
     mixer_ref, raw_ref, driven_ref, decay_ref, input_ref = refs[pieces + 7 :]
-    total = tree_sum(parts)
     mine, width, state_width = state_ref.shape
     columns = raw_ref.shape[1] - width
-    start = 2 * width + columns
-    gate = total[:, :width]
-    inner_raw = total[:, width : 2 * width].astype(bf16)
-    raw_ref[...] = total[:, width:start]
+    widths = [width, width, columns, LANES, 2 * state_width]
+    length = sum(widths)
+    tails = [ref[:, length:].astype(jnp.int32).astype(f32) for ref in refs[:pieces]]
+    sections, start = [], 0
+    for at, size in enumerate(widths):
+        sections.append(
+            tree_sum(
+                ref[:, start : start + size].astype(jnp.int32).astype(f32)
+                * jnp.exp2(tail[:, at : at + 1] - FIXED_BITS)
+                for ref, tail in zip(refs[:pieces], tails)
+            )
+        )
+        start += size
+    gate, inner_sum, group_sum, step_sum, pair_sum = sections
+    inner_raw = inner_sum.astype(bf16)
+    raw_ref[:, :width] = inner_sum
+    raw_ref[:, width:] = group_sum
     taps = inner_taps_ref[...].astype(f32)
     mixed = inner_raw.astype(f32) * taps[3:4]
     for at in range(3):
         mixed = mixed + inner_state_ref[at].astype(f32) * taps[at : at + 1]
     conv_inner = silu(mixed)
     taps = held_ref[1]
-    mixed = total[:, start + LANES :].astype(bf16).astype(f32) * taps[3:4]
+    mixed = pair_sum.astype(bf16).astype(f32) * taps[3:4]
     for at in range(3):
         mixed = mixed + held_ref[0, at * mine : (at + 1) * mine] * taps[at : at + 1]
     pair = silu(mixed).astype(bf16)
     state_input = pair[:, :state_width].astype(f32)
     state_output = pair[:, state_width:]
 
-    step_raw = total[:, start : start + LANES] + heads_ref[0:1]
+    step_raw = step_sum + heads_ref[0:1]
     step_size = jnp.maximum(step_raw, 0.0) + jnp.log1p(jnp.exp(-jnp.abs(step_raw)))
     decay_rate = jnp.exp(-step_size * jnp.exp(heads_ref[1:2]))
     stacked = jnp.concatenate([step_size, decay_rate, heads_ref[2:3]], axis=0)
@@ -354,18 +378,29 @@
         out_ref[:, column : column + TILE] = dot(left, weight_ref[:, column : column + TILE])
 
 
-def add_kernel(count, *refs):
-    refs[-1][...] = tree_sum([ref[...] for ref in refs[:count]])
-
-
-def fixed_exponent(values):
-    return jnp.floor(jnp.log2(jnp.maximum(values, 1e-30))) + 2.0
-
-
-def lexicon_kernel(pieces, *refs):
-    hidden_ref, gain_ref, mixed_ref = refs[:3]
-    held_refs = refs[3 : 3 + pieces]
-    weight_ref, layer_ref, out_ref, rest, left, scores, sems = refs[3 + pieces :]
+def plain(ref):
+    if ref.dtype != jnp.int16:
+        return ref[...]
+    width = ref.shape[1] - LANES
+    tail = ref[:, width:].astype(jnp.int32).astype(f32)
+    return ref[:, :width].astype(jnp.int32).astype(f32) * jnp.exp2(tail[:, 0:1] - FIXED_BITS)
+
+
+def encode_kernel(*refs):
+    value = tree_sum([plain(ref) for ref in refs[:-1]])
+    width = value.shape[1]
+    exponent = fixed_exponent(jnp.max(jnp.abs(value), axis=1, keepdims=True))
+    digits = jnp.round(value * jnp.exp2(FIXED_BITS - exponent))
+    refs[-1][:, :width] = digits.astype(jnp.int32).astype(jnp.int16)
+    tail = jnp.broadcast_to(exponent, (value.shape[0], LANES))
+    refs[-1][:, width:] = tail.astype(jnp.int32).astype(jnp.int16)
+
+
+def lexicon_kernel(terms, pieces, *refs):
+    hidden_ref, gain_ref = refs[:2]
+    mixed_refs = refs[2 : 2 + terms]
+    held_refs = refs[2 + terms : 2 + terms + pieces]
+    weight_ref, layer_ref, out_ref, rest, left, scores, sems = refs[2 + terms + pieces :]
     rows = hidden_ref.shape[0]
     blocks, mine, _ = out_ref.shape
     vocab = weight_ref.shape[1]
@@ -392,7 +427,8 @@
 
     @beside_copies
     def _():
-        layer = (hidden_ref[...].astype(f32) + mixed_ref[...]).astype(bf16)
+        mixed = tree_sum([plain(ref) for ref in mixed_refs])
+        layer = (hidden_ref[...].astype(f32) + mixed).astype(bf16)
         layer_ref[...] = layer
         wide = layer.astype(f32)
         squares = jnp.sum(wide * wide, axis=1, keepdims=True)
@@ -661,10 +697,14 @@
     packed_width = 2 * width + columns + LANES + 2 * state_width
     packed, held = call(
         pack_kernel,
-        [shape((row_devices, mine, packed_width)), shape((2, held_rows, 2 * state_width))],
+        [
+            shape((row_devices, mine, packed_width + LANES), jnp.int16),
+            shape((2, held_rows, 2 * state_width)),
+        ],
         [both, group_part, small, arrived],
         [VMEM] * 4,
-        cost=16 * MIB,
+        scratch=[pltpu.VMEM((rows, 2 * state_width), f32)],
+        cost=64 * MIB,
         name="pack_rows",
     )
     pieces = [packed[0]] + [row_send(packed[at], at) for at in range(1, row_devices)]
@@ -710,29 +750,26 @@
         cost=1000,
         name="output_projection",
     )
-    distance, stage = 1, 2
+    distance, stage, terms = 1, 2, [mixed]
     while distance < head_devices:
         steps = [distance]
         if distance > 1 and 4 * distance <= head_devices:
             steps = [distance, 2 * distance, 3 * distance]
-        others = [xor_permute(mixed, "head", step) for step in steps]
-        ahead = mixed
+        mine_now = terms[0]
+        if distance > 1:
+            mine_now = call(
+                encode_kernel, shape((rows, depth + LANES), jnp.int16), terms, [VMEM] * len(terms), name="encode"
+            )
+        terms = [mine_now] + [xor_permute(mine_now, "head", step) for step in steps]
         if distance > 1 and stage < len(SHARES):
-            ahead = fetch_lexicon(stage, mixed, f"fetch_lexicon_{stage}")
+            fetch_lexicon(stage, mine_now, f"fetch_lexicon_{stage}")
             stage += 1
-        mixed = call(
-            functools.partial(add_kernel, 1 + len(steps)),
-            shape((rows, depth)),
-            [mixed] + others + [ahead],
-            [VMEM] * (1 + len(steps)) + [ANY],
-            name="add",
-        )
         distance *= 1 + len(steps)
     layer, scores = call(
-        functools.partial(lexicon_kernel, len(fetched)),
+        functools.partial(lexicon_kernel, len(terms), len(fetched)),
         [pltpu.VMEM((rows, depth), bf16), shape((row_devices, mine, vocab + LANES), jnp.int16)],
-        [hidden_held, final_gain[None], mixed] + fetched + [in_hbm(lexicon_matrix)],
-        [VMEM] * (3 + len(fetched)) + [ANY],
+        [hidden_held, final_gain[None]] + terms + fetched + [in_hbm(lexicon_matrix)],
+        [VMEM] * (2 + len(terms) + len(fetched)) + [ANY],
         scratch=[
             pltpu.VMEM((depth, vocab - cuts[-1]), bf16),
             pltpu.VMEM((2 * rows, depth), bf16),

time: 74.5 us -> 73.6 us (0.988)
  Pallas kernels: 34.2 us -> 33.2 us
    pallas_call x15 -> x14, Pallas kernels: 34.2 us -> 33.2 us  [call(): pl.pallas_call(kernel, out_shape=outs, in_specs=specs, out_specs=out_spec...]
  transfers between devices with their start and end apart: 17 -> 17, of which waited for: 2 -> 2; matrix products, arithmetic and copies ran while one was open for 0% -> 0% of each run, Pallas kernels for 26% -> 24%
where the time goes in v4:
time: 73.6 us; the launch traced here: 73.3 us
  Pallas kernels  33.2 us (45%)
  starting transfers between devices  27.3 us (37%)
  blocking collectives  8.95 us (12%)
  waiting for transfers between devices  2.03 us (3%)
  between operations  1 us (1%)
  local copies, waits for them, and re-layouts  0.77 us (1%)
    pallas_call x14, Pallas kernels, call(): pl.pallas_call(kernel, out_shape=outs, in_specs=specs, out_specs=out_spec...  33.2 us
    ppermute x12, starting transfers between devices, row_send(): lax.ppermute(values, 'row', [(at, (at + distance) % size) for at in range...  18.5 us
    all_gather x1, blocking collectives, local(): every = lax.all_gather(shares, 'head', axis=0)  8.95 us
    all_to_all x1, starting transfers between devices, local(): arrived = lax.all_to_all(sent, 'head', 0, 0, tiled=True)  5.18 us
    ppermute x4, starting transfers between devices, xor_permute(): lax.ppermute(values, axis, [(at, at ^ distance) for at in range(size)])  3.63 us
    ppermute x4, waiting for transfers between devices, xor_permute(): lax.ppermute(values, axis, [(at, at ^ distance) for at in range(size)])  2 us
  transfers between devices with their start and end apart: 17, of which 2 were waited for; matrix products, arithmetic and copies ran while one was open for 0% of the time, Pallas kernels for 24%

profile of v4, /device:TPU:0, one launch (start us, length us, event | category | flops | bytes accessed | tf_op | source)
XLA Modules:
  0.0 73.3 jit_solution(17786784044299127491)
XLA Ops:
  0.6 3.0 %group_projection.1 = (bf16[8,2048]{1,0:T(8,128)(2,1)S(1)}, bf16[16,128]{1,0:T(8,128)(2,1)S(1)}, bf16[32,2048]{1,0:T(8,128)(2,1)S(1)}, f32[8,512]{1,0:T(8,128)S(...) custom-call(bf16[8,2048]{1,0:T(8,128)(2,1)} %refs_0_.5, bf16[16,128]{1,0:T(8,128)(2,1)} %bitcast.38, ...), custom_call_target="tpu_custom_call" | custom-call | flops 1000 | bytes 2097152 | tf_op jit(solution)/shard_map/group_projection/pallas_call | solution.py:99
  3.7 5.2 %all-to-all-start = ((bf16[8,16,128]{2,1,0:T(8,128)(2,1)}), bf16[8,16,128]{2,1,0:T(8,128)(2,1)S(1)}, u32[]{:S(2)}, u32[]{:S(2)}) async-start(bf16[8,16,128]{2,1,0:T(8,128)(2,1)} %get-tuple-element.40), calls=%async_computation | async-start | bytes 65536 | tf_op jit(solution)/shard_map/all_to_all | solution.py:657
  8.8 1.6 %collective-permute-start = (f32[8,128]{1,0:T(8,128)S(1)}, f32[8,128]{1,0:T(8,128)S(1)}, u32[]{:S(2)}, u32[]{:S(2)}) collective-permute-start(f32[8,128]{1,0:T(8,128)S(1)} %get-tuple-element.36.refs_0_), channel_id=1, source_target_pairs={{0,8},{8,16},{16,24},{24,0},{1,9},{9,17},{17,25},{25,1},{2,10},{10... | collective-permute-start | bytes 12296 | tf_op jit(solution)/shard_map/ppermute | solution.py:39
  10.4 2.6 %collective-permute-start.1 = (f32[8,128]{1,0:T(8,128)S(1)}, f32[8,128]{1,0:T(8,128)S(1)}, u32[]{:S(2)}, u32[]{:S(2)}) collective-permute-start(f32[8,128]{1,0:T(8,128)S(1)} %get-tuple-element.36.refs_0_), channel_id=1, source_target_pairs={{0,16},{8,24},{16,0},{24,8},{1,17},{9,25},{17,1},{25,9},{2,18},{10... | collective-permute-start | bytes 12296 | tf_op jit(solution)/shard_map/ppermute | solution.py:39
  13.0 1.3 %collective-permute-start.2 = (f32[8,128]{1,0:T(8,128)S(1)}, f32[8,128]{1,0:T(8,128)S(1)}, u32[]{:S(2)}, u32[]{:S(2)}) collective-permute-start(f32[8,128]{1,0:T(8,128)S(1)} %get-tuple-element.36.refs_0_), channel_id=1, source_target_pairs={{0,24},{8,0},{16,8},{24,16},{1,25},{9,1},{17,9},{25,17},{2,26},{10... | collective-permute-start | bytes 12296 | tf_op jit(solution)/shard_map/ppermute | solution.py:39
  14.4 4.2 %fetch_input.1 = (bf16[2,4096,128]{2,1,0:T(8,128)(2,1)S(1)}, bf16[2,4096,128]{2,1,0:T(8,128)(2,1)S(1)}, bf16[2,4096,128]{2,1,0:T(8,128)(2,1)S(1)}, bf16[2,4096,1...) custom-call(bf16[2048,2,2048]{2,1,0:T(2,128)(2,1)} %refs_12_.1, bf16[8,16,128]{2,1,0:T(8,128)(2,1)S(1)} %all-to-all-done.refs_1_.arrived_ref), custom_call_target="tpu_custom_call" | custom-call | flops 1000 | bytes 1000 | tf_op jit(solution)/shard_map/fetch_input/pallas_call | solution.py:99
  18.6 0.0 copy-start.7
  18.6 0.0 copy-start.8
  18.7 0.0 copy-start.9
  18.7 0.0 copy-start.5
  18.7 3.6 %input_projection.1 = (f32[16,2048]{1,0:T(8,128)S(1)}, f32[8,256]{1,0:T(8,128)S(1)}) custom-call(f32[8,128]{1,0:T(8,128)S(1)} %get-tuple-element.36.refs_0_, f32[8,128]{1,0:T(8,128)S(1)} %collective-permute-done.refs_1_, f32[8,128]{1,0:T(8,128)S(1)} %collective-permute-done.1.refs_2_, f32[8,128]{1,0:T(8,128)S(1)} %collective-permute-done.2.refs_3_, ...), custom_call_target="tpu_custom_call" | custom-call | flops 1000 | bytes 16777216 | tf_op jit(solution)/shard_map/input_projection/pallas_call | solution.py:99
  22.3 0.3 pack_rows.1
  22.6 0.1 slice_bitcast_fusion.4
  22.7 1.0 %collective-permute-start.3 = (s16[2,5376]{1,0:T(2,128)(2,1)S(1)}, s16[2,5376]{1,0:T(2,128)(2,1)S(1)}, u32[]{:S(2)}, u32[]{:S(2)}) collective-permute-start(s16[2,5376]{1,0:T(2,128)(2,1)S(1)} %get-tuple-element.73), channel_id=1, source_target_pairs={{0,8},{8,16},{16,24},{24,0},{1,9},{9,17},{17,25},{25,1},{2,10},{10... | collective-permute-start | bytes 64520 | tf_op jit(solution)/shard_map/ppermute | solution.py:39
  23.6 2.6 %collective-permute-start.4 = (s16[2,5376]{1,0:T(2,128)(2,1)S(1)}, s16[2,5376]{1,0:T(2,128)(2,1)S(1)}, u32[]{:S(2)}, u32[]{:S(2)}) collective-permute-start(s16[2,5376]{1,0:T(2,128)(2,1)S(1)} %get-tuple-element.72), channel_id=1, source_target_pairs={{0,16},{8,24},{16,0},{24,8},{1,17},{9,25},{17,1},{25,9},{2,18},{10... | collective-permute-start | bytes 64520 | tf_op jit(solution)/shard_map/ppermute | solution.py:39
  26.2 1.3 %collective-permute-start.5 = (s16[2,5376]{1,0:T(2,128)(2,1)S(1)}, s16[2,5376]{1,0:T(2,128)(2,1)S(1)}, u32[]{:S(2)}, u32[]{:S(2)}) collective-permute-start(s16[2,5376]{1,0:T(2,128)(2,1)S(1)} %get-tuple-element.71), channel_id=1, source_target_pairs={{0,24},{8,0},{16,8},{24,16},{1,25},{9,1},{17,9},{25,17},{2,26},{10... | collective-permute-start | bytes 64520 | tf_op jit(solution)/shard_map/ppermute | solution.py:39
  27.6 0.0 copy-start
  27.6 0.0 copy-start.1
  27.6 0.0 copy-start.4
  27.6 2.3 %fetch_lexicon_0.1 = (bf16[2048,1024]{1,0:T(8,128)(2,1)S(1)}, bf16[128,2048]{1,0:T(8,128)(2,1)S(1)}) custom-call(bf16[2048,8192]{1,0:T(8,128)(2,1)} %refs_9_.1, s16[4,2,5376]{2,1,0:T(2,128)(2,1)S(1)} %get-tuple-element.49.refs_1_), custom_call_target="tpu_custom_call" | custom-call | flops 1000 | bytes 1000 | tf_op jit(solution)/shard_map/fetch_lexicon_0/pallas_call | solution.py:99
  30.0 0.5 copy-done
  30.5 1.1 %state_readout.1 = (bf16[2,2048]{1,0:T(2,128)(2,1)S(1)}, f32[2,2560]{1,0:T(2,128)S(1)}, f32[2,2048]{1,0:T(2,128)S(1)}, f32[2,2048]{1,0:T(2,128)S(1)}, f32[2,256]{1,0:T(2,128)S(1)}) custom-call(s16[2,5376]{1,0:T(2,128)(2,1)S(1)} %get-tuple-element.74.refs_0_, s16[2,5376]{1,0:T(2,128)(2,1)S(1)} %collective-permute-done.3.refs_1_, ...), custom_call_target="tpu_custom_call" | custom-call | flops 1000 | bytes 1000 | tf_op jit(solution)/shard_map/state_readout/pallas_call | solution.py:99
  31.6 0.0 slice-start.1
  31.6 0.7 collective-permute-start.6
  32.3 2.6 %collective-permute-start.7 = (bf16[2,2048]{1,0:T(2,128)(2,1)S(1)}, bf16[2,2048]{1,0:T(2,128)(2,1)S(1)}, u32[]{:S(2)}, u32[]{:S(2)}) collective-permute-start(bf16[2,2048]{1,0:T(2,128)(2,1)S(1)} %get-tuple-element.56.refs_1_.refs_0_), channel_id=1, source_target_pairs={{0,16},{8,24},{16,0},{24,8},{1,17},{9,25},{17,1},{25,9},{2,18},{10... | collective-permute-start | bytes 24584 | tf_op jit(solution)/shard_map/ppermute | solution.py:39
  34.9 0.7 collective-permute-start.8
  35.6 3.4 %fetch_lexicon_1.1.refs_5_.refs_7_ = bf16[2048,2048]{1,0:T(8,128)(2,1)S(1)} custom-call(bf16[2048,8192]{1,0:T(8,128)(2,1)} %refs_9_.1, bf16[2,2048]{1,0:T(2,128)(2,1)S(1)} %get-tuple-element.56.refs_1_.refs_0_), custom_call_target="tpu_custom_call" | custom-call | flops 1000 | bytes 1000 | tf_op jit(solution)/shard_map/fetch_lexicon_1/pallas_call | solution.py:99
  39.0 0.0 copy-start.6
  39.0 1.2 %output_projection.1.refs_0_ = f32[8,2048]{1,0:T(8,128)S(1)} custom-call(bf16[2,2048]{1,0:T(2,128)(2,1)S(1)} %get-tuple-element.56.refs_1_.refs_0_, bf16[2,2048]{1,0:T(2,128)(2,1)S(1)} %collective-permute-done.6.refs_1_, bf16[2,2048]{1,0:T(2,128)(2,1)S(1)} %collective-permute-done.7.refs_2_, bf16[2,2048]{1,0:T(2,128)(2,1)S(1)} %collective-permute-done.8.refs_3_, ...), custom_call_target="tpu_custom_call" | custom-call | flops 1000 | bytes 1000 | tf_op jit(solution)/shard_map/output_projection/pallas_call | solution.py:99
  40.2 1.3 %collective-permute-done.9.refs_1_ = f32[8,2048]{1,0:T(8,128)S(1)} collective-permute-done((f32[8,2048]{1,0:T(8,128)S(1)}, f32[8,2048]{1,0:T(8,128)S(1)}, u32[]{:S(2)}, u32[]{:S(2)}) %collective-permute-start.9) | collective-permute-done | bytes 65568 | tf_op jit(solution)/shard_map/ppermute | solution.py:34
  41.5 0.1 encode.1.refs_1_.refs_2_
  41.6 2.1 %collective-permute-start.10 = (s16[8,2176]{1,0:T(8,128)(2,1)S(1)}, s16[8,2176]{1,0:T(8,128)(2,1)S(1)}, u32[]{:S(2)}, u32[]{:S(2)}) collective-permute-start(s16[8,2176]{1,0:T(8,128)(2,1)S(1)} %encode.1.refs_1_.refs_2_), channel_id=1, source_target_pairs={{0,2},{1,3},{2,0},{3,1},{4,6},{5,7},{6,4},{7,5},{8,10},{9,11},{10,... | collective-permute-start | bytes 104456 | tf_op jit(solution)/shard_map/ppermute | solution.py:34
  43.7 1.5 %collective-permute-start.11 = (s16[8,2176]{1,0:T(8,128)(2,1)S(1)}, s16[8,2176]{1,0:T(8,128)(2,1)S(1)}, u32[]{:S(2)}, u32[]{:S(2)}) collective-permute-start(s16[8,2176]{1,0:T(8,128)(2,1)S(1)} %encode.1.refs_1_.refs_2_), channel_id=1, source_target_pairs={{0,4},{1,5},{2,6},{3,7},{4,0},{5,1},{6,2},{7,3},{8,12},{9,13},{10,... | collective-permute-start | bytes 104456 | tf_op jit(solution)/shard_map/ppermute | solution.py:34
  45.2 0.1 collective-permute-start.12
  45.2 4.0 %fetch_lexicon_2.1.refs_8_ = bf16[2048,2560]{1,0:T(8,128)(2,1)S(1)} custom-call(bf16[2048,8192]{1,0:T(8,128)(2,1)} %refs_9_.1, s16[8,2176]{1,0:T(8,128)(2,1)S(1)} %encode.1.refs_1_.refs_2_), custom_call_target="tpu_custom_call" | custom-call | flops 1000 | bytes 1000 | tf_op jit(solution)/shard_map/fetch_lexicon_2/pallas_call | solution.py:99
  49.3 0.7 collective-permute-done.12.refs_5_
  50.0 5.3 %lexicon_projection.1 = (bf16[8,2048]{1,0:T(8,128)(2,1)S(1)}, s16[4,2,8320]{2,1,0:T(2,128)(2,1)S(1)}) custom-call(bf16[8,2048]{1,0:T(8,128)(2,1)S(1)} %get-tuple-element.37.refs_4_.refs_0_, bf16[1,2048]{1,0:T(2,128)(2,1)S(1)} %broadcast_in_dim.13.refs_1_, s16[8,2176]{1,0:T(8,128)(2,1)S(1)} %encode.1.refs_1_.refs_2_, ...), custom_call_target="tpu_custom_call" | custom-call | flops 1000 | bytes 16777216 | tf_op jit(solution)/shard_map/lexicon_projection/pallas_call | solution.py:99
  55.3 0.0 copy-start.2
  55.3 0.0 copy-start.10
  55.3 0.1 slice_bitcast_fusion
  55.4 0.6 collective-permute-start.13
  56.1 2.0 %collective-permute-start.14 = (s16[2,8320]{1,0:T(2,128)(2,1)S(1)}, s16[2,8320]{1,0:T(2,128)(2,1)S(1)}, u32[]{:S(2)}, u32[]{:S(2)}) collective-permute-start(s16[2,8320]{1,0:T(2,128)(2,1)S(1)} %get-tuple-element.68), channel_id=1, source_target_pairs={{0,16},{8,24},{16,0},{24,8},{1,17},{9,25},{17,1},{25,9},{2,18},{10... | collective-permute-start | bytes 99848 | tf_op jit(solution)/shard_map/ppermute | solution.py:39
  58.0 1.5 %collective-permute-start.15 = (s16[2,8320]{1,0:T(2,128)(2,1)S(1)}, s16[2,8320]{1,0:T(2,128)(2,1)S(1)}, u32[]{:S(2)}, u32[]{:S(2)}) collective-permute-start(s16[2,8320]{1,0:T(2,128)(2,1)S(1)} %get-tuple-element.67), channel_id=1, source_target_pairs={{0,24},{8,0},{16,8},{24,16},{1,25},{9,1},{17,9},{25,17},{2,26},{10... | collective-permute-start | bytes 99848 | tf_op jit(solution)/shard_map/ppermute | solution.py:39
  59.6 3.3 %state_update.1 = (bf16[2,2048,256]{2,1,0:T(8,128)(2,1)}, bf16[3,2,2048]{2,1,0:T(2,128)(2,1)}, bf16[3,2,512]{2,1,0:T(2,128)(2,1)}, bf16[8,2048]{1,0:T(8,128)(2,1)}) custom-call(f32[2,2048]{1,0:T(2,128)S(1)} %get-tuple-element.52.driven_ref, f32[2,2048]{1,0:T(2,128)S(1)} %get-tuple-element.53.decay_ref, f32[2,256]{1,0:T(2,128)S(1)} %get-tuple-element.54.input_ref, ...), custom_call_target="tpu_custom_call" | custom-call | flops 1000 | bytes 4194304 | tf_op jit(solution)/shard_map/state_update/pallas_call | solution.py:99
  62.9 0.3 share_of_peak.1
  63.2 8.9 %all-gather = bf16[128,1152]{1,0:T(8,128)(2,1)S(1)} all-gather(bf16[16,1152]{1,0:T(8,128)(2,1)S(1)} %get-tuple-element.64), channel_id=2, replica_groups=mesh['row'=4,'head'=8] {'head'}, dimensions={0}, use_global_device_ids=true | all-gather | bytes 331776 | tf_op jit(solution)/shard_map/all_gather | solution.py:816
  72.2 0.1 broadcast_in_dim.14.floor_ref
  72.3 1.1 %probabilities.1 = bf16[2,8192]{1,0:T(2,128)(2,1)} custom-call(bf16[8,16,1152]{2,1,0:T(8,128)(2,1)S(1)} %bitcast.32, f32[2,8192]{1,0:T(2,128)S(1)} %get-tuple-element.65.share_ref, f32[2,128]{1,0:T(2,128)S(1)} %get-tuple-element.66.top_ref, s32[2,128]{1,0:T(2,128)S(1)} %broadcast_in_dim.14.floor_ref), custom_call_target="tpu_custom_call" | custom-call | flops 1000 | tf_op jit(solution)/shard_map/probabilities/pallas_call | solution.py:99
  (34 shorter events, 0.1 us)
Async XLA Ops:
  3.7 10.7 %all-to-all-start = ((bf16[8,16,128]{2,1,0:T(8,128)(2,1)}), bf16[8,16,128]{2,1,0:T(8,128)(2,1)S(1)}, u32[]{:S(2)}, u32[]{:S(2)}) async-start(bf16[8,16,128]{2,1,0:T(8,128)(2,1)} %get-tuple-element.40), calls=%async_computation | async-start | bytes 65536 | tf_op jit(solution)/shard_map/all_to_all | solution.py:657
  8.8 9.8 %collective-permute-start = (f32[8,128]{1,0:T(8,128)S(1)}, f32[8,128]{1,0:T(8,128)S(1)}, u32[]{:S(2)}, u32[]{:S(2)}) collective-permute-start(f32[8,128]{1,0:T(8,128)S(1)} %get-tuple-element.36.refs_0_), channel_id=1, source_target_pairs={{0,8},{8,16},{16,24},{24,0},{1,9},{9,17},{17,25},{25,1},{2,10},{10... | collective-permute-start | bytes 12296 | tf_op jit(solution)/shard_map/ppermute | solution.py:39
  10.4 8.2 %collective-permute-start.1 = (f32[8,128]{1,0:T(8,128)S(1)}, f32[8,128]{1,0:T(8,128)S(1)}, u32[]{:S(2)}, u32[]{:S(2)}) collective-permute-start(f32[8,128]{1,0:T(8,128)S(1)} %get-tuple-element.36.refs_0_), channel_id=1, source_target_pairs={{0,16},{8,24},{16,0},{24,8},{1,17},{9,25},{17,1},{25,9},{2,18},{10... | collective-permute-start | bytes 12296 | tf_op jit(solution)/shard_map/ppermute | solution.py:39
  13.0 5.6 %collective-permute-start.2 = (f32[8,128]{1,0:T(8,128)S(1)}, f32[8,128]{1,0:T(8,128)S(1)}, u32[]{:S(2)}, u32[]{:S(2)}) collective-permute-start(f32[8,128]{1,0:T(8,128)S(1)} %get-tuple-element.36.refs_0_), channel_id=1, source_target_pairs={{0,24},{8,0},{16,8},{24,16},{1,25},{9,1},{17,9},{25,17},{2,26},{10... | collective-permute-start | bytes 12296 | tf_op jit(solution)/shard_map/ppermute | solution.py:39
  18.6 8.9 %copy-start.7 = (f32[32]{0:T(128)S(1)}, f32[32]{0:T(128)}, u32[]{:S(2)}) copy-start(f32[32]{0:T(128)} %param.30) | copy-start | bytes 388
  18.6 8.9 %copy-start.8 = (f32[32]{0:T(128)S(1)}, f32[32]{0:T(128)}, u32[]{:S(2)}) copy-start(f32[32]{0:T(128)} %param.29) | copy-start | bytes 388
  18.7 8.9 %copy-start.9 = (f32[32]{0:T(128)S(1)}, f32[32]{0:T(128)}, u32[]{:S(2)}) copy-start(f32[32]{0:T(128)} %param.28) | copy-start | bytes 388
  18.7 8.9 %copy-start.5 = (bf16[2048]{0:T(1024)(128)(2,1)S(1)}, bf16[2048]{0:T(1024)(128)(2,1)}, u32[]{:S(2)}) copy-start(bf16[2048]{0:T(1024)(128)(2,1)} %param.32) | copy-start | bytes 12292
  22.7 7.3 %collective-permute-start.3 = (s16[2,5376]{1,0:T(2,128)(2,1)S(1)}, s16[2,5376]{1,0:T(2,128)(2,1)S(1)}, u32[]{:S(2)}, u32[]{:S(2)}) collective-permute-start(s16[2,5376]{1,0:T(2,128)(2,1)S(1)} %get-tuple-element.73), channel_id=1, source_target_pairs={{0,8},{8,16},{16,24},{24,0},{1,9},{9,17},{17,25},{25,1},{2,10},{10... | collective-permute-start | bytes 64520 | tf_op jit(solution)/shard_map/ppermute | solution.py:39
  23.6 6.4 %collective-permute-start.4 = (s16[2,5376]{1,0:T(2,128)(2,1)S(1)}, s16[2,5376]{1,0:T(2,128)(2,1)S(1)}, u32[]{:S(2)}, u32[]{:S(2)}) collective-permute-start(s16[2,5376]{1,0:T(2,128)(2,1)S(1)} %get-tuple-element.72), channel_id=1, source_target_pairs={{0,16},{8,24},{16,0},{24,8},{1,17},{9,25},{17,1},{25,9},{2,18},{10... | collective-permute-start | bytes 64520 | tf_op jit(solution)/shard_map/ppermute | solution.py:39
  26.2 3.8 %collective-permute-start.5 = (s16[2,5376]{1,0:T(2,128)(2,1)S(1)}, s16[2,5376]{1,0:T(2,128)(2,1)S(1)}, u32[]{:S(2)}, u32[]{:S(2)}) collective-permute-start(s16[2,5376]{1,0:T(2,128)(2,1)S(1)} %get-tuple-element.71), channel_id=1, source_target_pairs={{0,24},{8,0},{16,8},{24,16},{1,25},{9,1},{17,9},{25,17},{2,26},{10... | collective-permute-start | bytes 64520 | tf_op jit(solution)/shard_map/ppermute | solution.py:39
  27.6 2.9 %copy-start = (bf16[2,32,64,256]{3,2,1,0:T(8,128)(2,1)S(1)}, bf16[2,32,64,256]{3,2,1,0:T(8,128)(2,1)}, u32[]{:S(2)}) copy-start(bf16[2,32,64,256]{3,2,1,0:T(8,128)(2,1)} %param.31) | copy-start | bytes 6291460
  27.6 2.9 %copy-start.1 = (bf16[2,3,2048]{2,0,1:T(2,128)(2,1)S(1)}, bf16[2,3,2048]{2,0,1:T(2,128)(2,1)}, u32[]{:S(2)}) copy-start(bf16[2,3,2048]{2,0,1:T(2,128)(2,1)} %param.26) | copy-start | bytes 73732
  27.6 2.9 %copy-start.4 = (bf16[4,2048]{1,0:T(4,128)(2,1)S(1)}, bf16[4,2048]{1,0:T(4,128)(2,1)}, u32[]{:S(2)}) copy-start(bf16[4,2048]{1,0:T(4,128)(2,1)} %refs_7_.1) | copy-start | bytes 49156
  30.5 8.5 %slice-start = ((s8[8388608]{0:T(1024)(128)(4,1)}), s8[4194304]{0:T(1024)(128)(4,1)S(1)}, s32[]{:S(2)}) async-start(s8[8388608]{0:T(1024)(128)(4,1)} %bitcast.28), calls=%async_computation.1 | async-start | bytes 8388608
  31.6 7.5 %slice-start.1 = ((s8[8388608]{0:T(1024)(128)(4,1)}), s8[4194304]{0:T(1024)(128)(4,1)S(1)}, s32[]{:S(2)}) async-start(s8[8388608]{0:T(1024)(128)(4,1)} %bitcast.28), calls=%async_computation.2 | async-start | bytes 8388608
  31.6 7.4 %collective-permute-start.6 = (bf16[2,2048]{1,0:T(2,128)(2,1)S(1)}, bf16[2,2048]{1,0:T(2,128)(2,1)S(1)}, u32[]{:S(2)}, u32[]{:S(2)}) collective-permute-start(bf16[2,2048]{1,0:T(2,128)(2,1)S(1)} %get-tuple-element.56.refs_1_.refs_0_), channel_id=1, source_target_pairs={{0,8},{8,16},{16,24},{24,0},{1,9},{9,17},{17,25},{25,1},{2,10},{10... | collective-permute-start | bytes 24584 | tf_op jit(solution)/shard_map/ppermute | solution.py:39
  32.3 6.7 %collective-permute-start.7 = (bf16[2,2048]{1,0:T(2,128)(2,1)S(1)}, bf16[2,2048]{1,0:T(2,128)(2,1)S(1)}, u32[]{:S(2)}, u32[]{:S(2)}) collective-permute-start(bf16[2,2048]{1,0:T(2,128)(2,1)S(1)} %get-tuple-element.56.refs_1_.refs_0_), channel_id=1, source_target_pairs={{0,16},{8,24},{16,0},{24,8},{1,17},{9,25},{17,1},{25,9},{2,18},{10... | collective-permute-start | bytes 24584 | tf_op jit(solution)/shard_map/ppermute | solution.py:39
  34.9 4.1 %collective-permute-start.8 = (bf16[2,2048]{1,0:T(2,128)(2,1)S(1)}, bf16[2,2048]{1,0:T(2,128)(2,1)S(1)}, u32[]{:S(2)}, u32[]{:S(2)}) collective-permute-start(bf16[2,2048]{1,0:T(2,128)(2,1)S(1)} %get-tuple-element.56.refs_1_.refs_0_), channel_id=1, source_target_pairs={{0,24},{8,0},{16,8},{24,16},{1,25},{9,1},{17,9},{25,17},{2,26},{10... | collective-permute-start | bytes 24584 | tf_op jit(solution)/shard_map/ppermute | solution.py:39
  39.0 6.3 %copy-start.6 = (bf16[2048]{0:T(1024)(128)(2,1)S(1)}, bf16[2048]{0:T(1024)(128)(2,1)}, u32[]{:S(2)}) copy-start(bf16[2048]{0:T(1024)(128)(2,1)} %param.34) | copy-start | bytes 12292
  40.2 1.3 %collective-permute-start.9 = (f32[8,2048]{1,0:T(8,128)S(1)}, f32[8,2048]{1,0:T(8,128)S(1)}, u32[]{:S(2)}, u32[]{:S(2)}) collective-permute-start(f32[8,2048]{1,0:T(8,128)S(1)} %output_projection.1.refs_0_), channel_id=1, source_target_pairs={{0,1},{1,0},{2,3},{3,2},{4,5},{5,4},{6,7},{7,6},{8,9},{9,8},{10,11... | collective-permute-start | bytes 196616 | tf_op jit(solution)/shard_map/ppermute | solution.py:34
  41.6 7.6 %collective-permute-start.10 = (s16[8,2176]{1,0:T(8,128)(2,1)S(1)}, s16[8,2176]{1,0:T(8,128)(2,1)S(1)}, u32[]{:S(2)}, u32[]{:S(2)}) collective-permute-start(s16[8,2176]{1,0:T(8,128)(2,1)S(1)} %encode.1.refs_1_.refs_2_), channel_id=1, source_target_pairs={{0,2},{1,3},{2,0},{3,1},{4,6},{5,7},{6,4},{7,5},{8,10},{9,11},{10,... | collective-permute-start | bytes 104456 | tf_op jit(solution)/shard_map/ppermute | solution.py:34
  43.7 5.6 %collective-permute-start.11 = (s16[8,2176]{1,0:T(8,128)(2,1)S(1)}, s16[8,2176]{1,0:T(8,128)(2,1)S(1)}, u32[]{:S(2)}, u32[]{:S(2)}) collective-permute-start(s16[8,2176]{1,0:T(8,128)(2,1)S(1)} %encode.1.refs_1_.refs_2_), channel_id=1, source_target_pairs={{0,4},{1,5},{2,6},{3,7},{4,0},{5,1},{6,2},{7,3},{8,12},{9,13},{10,... | collective-permute-start | bytes 104456 | tf_op jit(solution)/shard_map/ppermute | solution.py:34
  45.2 4.8 %collective-permute-start.12 = (s16[8,2176]{1,0:T(8,128)(2,1)S(1)}, s16[8,2176]{1,0:T(8,128)(2,1)S(1)}, u32[]{:S(2)}, u32[]{:S(2)}) collective-permute-start(s16[8,2176]{1,0:T(8,128)(2,1)S(1)} %encode.1.refs_1_.refs_2_), channel_id=1, source_target_pairs={{0,6},{1,7},{2,4},{3,5},{4,2},{5,3},{6,0},{7,1},{8,14},{9,15},{10,... | collective-permute-start | bytes 104456 | tf_op jit(solution)/shard_map/ppermute | solution.py:34
  50.0 9.6 %copy-start.3 = (bf16[2,3,512]{2,0,1:T(2,128)(2,1)S(1)}, bf16[2,3,512]{2,0,1:T(2,128)(2,1)}, u32[]{:S(2)}) copy-start(bf16[2,3,512]{2,0,1:T(2,128)(2,1)} %param.27) | copy-start | bytes 18436
  55.3 7.6 %copy-start.2 = (s32[2,8192]{1,0:T(2,128)S(1)}, s32[2,8192]{1,0:T(2,128)}, u32[]{:S(2)}) copy-start(s32[2,8192]{1,0:T(2,128)} %refs_4_.3) | copy-start | bytes 196612
  55.3 16.9 %copy-start.10 = (s32[2]{0:T(128)S(1)}, s32[2]{0:T(128)}, u32[]{:S(2)}) copy-start(s32[2]{0:T(128)} %param.37) | copy-start | bytes 28
  55.4 7.5 %collective-permute-start.13 = (s16[2,8320]{1,0:T(2,128)(2,1)S(1)}, s16[2,8320]{1,0:T(2,128)(2,1)S(1)}, u32[]{:S(2)}, u32[]{:S(2)}) collective-permute-start(s16[2,8320]{1,0:T(2,128)(2,1)S(1)} %get-tuple-element.69), channel_id=1, source_target_pairs={{0,8},{8,16},{16,24},{24,0},{1,9},{9,17},{17,25},{25,1},{2,10},{10... | collective-permute-start | bytes 99848 | tf_op jit(solution)/shard_map/ppermute | solution.py:39
  56.1 6.8 %collective-permute-start.14 = (s16[2,8320]{1,0:T(2,128)(2,1)S(1)}, s16[2,8320]{1,0:T(2,128)(2,1)S(1)}, u32[]{:S(2)}, u32[]{:S(2)}) collective-permute-start(s16[2,8320]{1,0:T(2,128)(2,1)S(1)} %get-tuple-element.68), channel_id=1, source_target_pairs={{0,16},{8,24},{16,0},{24,8},{1,17},{9,25},{17,1},{25,9},{2,18},{10... | collective-permute-start | bytes 99848 | tf_op jit(solution)/shard_map/ppermute | solution.py:39
  58.0 4.9 %collective-permute-start.15 = (s16[2,8320]{1,0:T(2,128)(2,1)S(1)}, s16[2,8320]{1,0:T(2,128)(2,1)S(1)}, u32[]{:S(2)}, u32[]{:S(2)}) collective-permute-start(s16[2,8320]{1,0:T(2,128)(2,1)S(1)} %get-tuple-element.67), channel_id=1, source_target_pairs={{0,24},{8,0},{16,8},{24,16},{1,25},{9,1},{17,9},{25,17},{2,26},{10... | collective-permute-start | bytes 99848 | tf_op jit(solution)/shard_map/ppermute | solution.py:39
